TPU v7x, 32 devices: a whole 2x2x4 slice. The times are simulated.
32 devices in a mesh: row: 8 (over z, x), col: 2 (over y), rep: 2 (over core).
Axes of the slice: x: 2, y: 2, z: 4, core: 2. Of those that a mesh axis runs over, the one named last changes fastest.
Arguments:
- adj_tiles: float32 [8, 2, 4, 512, 512], P('row', 'col'), may hold values from -0.25 to 0.25
- tile_rows: int32 [8, 2, 4], P('row', 'col'), may hold values from 0 to 1
- tile_cols: int32 [8, 2, 4], P('row', 'col'), may hold values from 0 to 7
- tile_counts: int32 [8, 2], P('row', 'col'), may hold values from 1 to 4, as said below
- features_t: float32 [128, 8192], P('rep', ('row', 'col')), may hold values from -6 to 6
- weight: float32 [128, 128], P('rep'), may hold values from -0.5 to 0.5
- bias_vec: float32 [128], replicated, may hold values from -3 to 3
- cotangent: float32 [8192, 128], P(('row', 'col', 'rep')), may hold values from -0.02 to 0.02
Outputs:
- output: float32 [8192, 128], P(('row', 'col', 'rep'))
- grad_weight: float32 [128, 128], P('rep')
- grad_bias: float32 [128], replicated
Inputs may be any that keep to these rules, and one draw needn't show every extreme that they name: `tile_counts`: the number of live slots of each cell; some cell has all 4 slots live. `tile_rows`: block row of a slot inside its row group; dead slots hold arbitrary values. `tile_cols`: block column of a slot inside its column group; dead slots hold arbitrary values.
All inputs are finite; a program needn't handle non-finite values.
Results may differ from a plain program's by a relative error of at most 0.0001.
Values sent between devices are 32-bit elements; how exact they have to be, the bound alone decides.
No kernel may reach another device: no remote copies, remote signals or barrier semaphores. Data moves between devices by JAX's collectives and lax.ppermute only.
A program may use at most 64 MiB of HBM per device.

v0:
```python
import jax
import jax.numpy as jnp
from jax import lax
from jax.sharding import PartitionSpec as P


def local(adj_tiles, tile_rows, tile_cols, tile_counts, features_t, weight, bias_vec, cotangent):
    slabs = adj_tiles[0, 0]
    rows_here = tile_rows[0, 0]
    cols_here = tile_cols[0, 0]
    live_count = tile_counts[0, 0]
    slot_count = slabs.shape[0]
    block_len = slabs.shape[1]
    half_width = features_t.shape[0]
    groups = lax.axis_size("col")
    is_live = jnp.arange(slot_count, dtype=jnp.int32) < live_count
    start_slots = jnp.zeros((slot_count, half_width, block_len), jnp.float32)
    running = start_slots
    shard_piece = lax.all_gather(features_t, "row", axis=1, tiled=True)
    span = shard_piece.shape[1]
    for slot_idx in range(slot_count):
        offset_col = cols_here[slot_idx] * block_len
        usable = is_live[slot_idx] & (offset_col >= 0) & (offset_col < span)
        begin_col = jnp.clip(offset_col, 0, span - block_len)

        def add_block(current, slot_idx=slot_idx, begin_col=begin_col):
            columns = lax.dynamic_slice_in_dim(shard_piece, begin_col, block_len, 1)
            product = lax.dot_general(
                columns,
                slabs[slot_idx],
                (((1,), (1,)), ((), ())),
                precision=lax.Precision.HIGHEST,
                preferred_element_type=jnp.float32,
            )
            return current.at[slot_idx].add(product)

        def keep_block(current):
            return current

        running = lax.cond(usable, add_block, keep_block, running)
    placing = (
        (rows_here[:, None] == jnp.arange(groups, dtype=jnp.int32)[None, :]) & is_live[:, None]
    ).astype(jnp.float32)
    mixed_t = jnp.einsum("tg,tfb->fgb", placing, running, precision=lax.Precision.HIGHEST).reshape(
        half_width, groups * block_len
    )
    part_cols = mixed_t
    preact = lax.psum_scatter(
        lax.dot_general(
            part_cols,
            weight,
            (((0,), (0,)), ((), ())),
            precision=lax.Precision.HIGHEST,
            preferred_element_type=jnp.float32,
        ),
        ("col", "rep"),
        scatter_dimension=0,
        tiled=True,
    )
    preact = preact + bias_vec
    squash = jax.nn.sigmoid(preact)
    output = preact * squash
    slope = cotangent * squash * (1.0 + preact * (1.0 - squash))
    contract_shard_piece = lax.all_gather(slope, ("col", "rep"), axis=0, tiled=True)
    part_cols = mixed_t
    grad_part = jnp.dot(
        part_cols,
        contract_shard_piece,
        precision=lax.Precision.HIGHEST,
        preferred_element_type=jnp.float32,
    )
    local_bias = jnp.sum(contract_shard_piece, axis=0)
    grad_weight, summed_bias = lax.psum((grad_part, local_bias), ("row", "col"))
    grad_bias = summed_bias / groups
    return (output, grad_weight, grad_bias)


def solution(mesh):
    in_specs = (
        P("row", "col", None, None, None),
        P("row", "col", None),
        P("row", "col", None),
        P("row", "col"),
        P("rep", ("row", "col")),
        P("rep", None),
        P(),
        P(("row", "col", "rep"), None),
    )
    out_specs = (P(("row", "col", "rep"), None), P("rep", None), P())
    return jax.shard_map(local, mesh=mesh, in_specs=in_specs, out_specs=out_specs, check_vma=False)
```

profile of v0, /device:TPU:0, one launch (start us, length us, event | category | flops | bytes accessed | tf_op | source)
XLA Modules:
  0.0 179.8 jit_solution(14497203921965962007)
XLA Ops:
  7.2 0.0 copy-start
  7.2 0.0 all-gather.2.cloned.1.call-start
  7.2 0.7 all-gather.2.cloned.1.call-update
  7.9 0.0 reduce-scatter.2.cloned.1.call-start
  8.0 1.5 fusion.30
  12.8 0.6 fusion.31
  15.9 37.2 %all-gather.2.cloned.1.call-done = f32[64,4096]{1,0:T(8,128)} async-done(((f32[64,512]{1,0:T(8,128)}), f32[64,4096]{1,0:T(8,128)}) %all-gather.2.cloned.1.call-update) | async-done | bytes 1048592 | tf_op jit(solution)/shard_map/all_gather | solution.py:19
  53.1 2.5 %conditional.4 = (f32[4,64,512]{2,1,0:T(8,128)S(1)}) conditional(s32[]{:T(128)} %convert_element_type.16, () %tuple.48, (s32[1,1,1]{2,1,0:T(1,128)}, f32[64,4096]{1,0:T(8,128)}, f32[4,512,512]{2,1,0:T(8,128)}, s32[1,1,1]{2,1,0:T(1,128)}, s32[1,1,1]{2,1,0:T(1,128)}) %tuple.75), branch_computations={%region_0.1_spmd, %region_1.2_spmd} | conditional | flops 201326592 | bytes 1966154 | solution.py:40
  53.1 2.4 %convolution_bitcast_fusion = f32[1,64,512]{2,1,0:T(8,128)S(1)} fusion(f32[4,512,512]{2,1,0:T(8,128)} %get-tuple-element.99, f32[64,4096]{1,0:T(8,128)} %get-tuple-element.97, s32[]{:T(128)S(6)} %select_n.8), kind=kOutput, calls=%fused_computation | convolution fusion | flops 201326592 | bytes 1310724 | tf_op jit(solution)/shard_map/cond/branch_1_fun/dot_general | solution.py:28
  55.6 0.1 scatter-add.6
  55.7 0.0 copy-start.1
  55.7 0.0 copy-start.3
  55.7 0.4 conditional.7
  55.7 0.3 copy.12
  56.1 0.6 fusion.23
  56.8 1.8 fusion.32
  58.6 0.0 reduce-scatter.2.cloned.1.call-update
  58.6 28.0 %reduce-scatter.2.cloned.1.call-done = f32[256,128]{1,0:T(8,128)} async-done(((f32[1024,128]{1,0:T(8,128)}), f32[256,128]{1,0:T(8,128)}) %reduce-scatter.2.cloned.1.call-update) | async-done | bytes 131088 | tf_op jit(solution)/shard_map/reduce_scatter | solution.py:48
  86.7 1.6 add_multiply_fusion
  88.3 6.8 %all_gather.7 = f32[1024,128]{1,0:T(8,128)S(1)} all-gather(f32[256,128]{1,0:T(8,128)S(1)} %get-tuple-element.133), channel_id=1, replica_groups=mesh['row'=8,'col'=2,'rep'=2] {'col','rep'}, dimensions={0}, use_global_device_ids=true | all-gather | bytes 655360 | tf_op jit(solution)/shard_map/all_gather | solution.py:64
  95.1 0.4 fusion.33
  95.5 0.1 reduce_sum.9
  95.7 76.8 %all-reduce.1 = (f32[64,128]{1,0:T(8,128)}, f32[128]{0:T(128)S(1)}) all-reduce(f32[64,128]{1,0:T(8,128)S(1)} %fusion.33, f32[128]{0:T(128)S(1)} %reduce_sum.9), channel_id=1, replica_groups=mesh['row'=8,'col'=2,'rep'=2] {'row','col'}, use_global_device_ids=true, to_apply=%region_9.10 | all-reduce | flops 8320 | bytes 66560 | tf_op jit(solution)/shard_map/psum | solution.py:73
  172.4 0.5 broadcast_multiply_fusion
  (9 shorter events, 0.1 us)
Async XLA Ops:
  7.2 49.6 %copy-start = (f32[64,128]{1,0:T(8,128)S(1)}, f32[64,128]{1,0:T(8,128)}, u32[]{:S(2)}) copy-start(f32[64,128]{1,0:T(8,128)} %param.29) | copy-start | bytes 98308
  7.2 46.0 %all-gather.2.cloned.1.call-start = ((), (), s32[]{:S(2)}) async-start(), calls=%async_computation.1 | async-start | bytes 1179648 | tf_op jit(solution)/shard_map/all_gather | solution.py:19
  7.9 78.7 %reduce-scatter.2.cloned.1.call-start = ((), (), s32[]{:S(2)}) async-start(), calls=%async_computation.2 | async-start | bytes 655360 | tf_op jit(solution)/shard_map/reduce_scatter | solution.py:48
  53.1 2.9 %copy-start.2 = (s32[1,1,4]{2,1,0:T(1,128)S(1)}, s32[1,1,4]{2,1,0:T(1,128)}, u32[]{:S(2)}) copy-start(s32[1,1,4]{2,1,0:T(1,128)} %param.25) | copy-start | bytes 52
  55.7 31.0 %copy-start.1 = (f32[256,128]{1,0:T(8,128)S(1)}, f32[256,128]{1,0:T(8,128)}, u32[]{:S(2)}) copy-start(f32[256,128]{1,0:T(8,128)} %param.31) | copy-start | bytes 393220
  55.7 31.0 %copy-start.3 = (f32[128]{0:T(128)S(1)}, f32[128]{0:T(128)}, u32[]{:S(2)}) copy-start(f32[128]{0:T(128)} %param.30) | copy-start | bytes 1540
Sparse Core Ops, SparseCore 0:
  10.2 42.8 all-gather.1
  58.7 27.8 reduce-scatter.1
where the time goes:
time: 180 us
  blocking collectives  83.6 us (46%)
  waiting for transfers between devices  66 us (37%)
  between operations  20 us (11%)
  matrix products  5.29 us (3%)
  local copies, waits for them, and re-layouts  2.54 us (1%)
  other arithmetic  2.29 us (1%)
    psum x1, blocking collectives, local(): grad_weight, summed_bias = lax.psum((grad_part, local_bias), ('row', 'col'))  76.8 us
    all_gather x1, waiting for transfers between devices, local(): shard_piece = lax.all_gather(features_t, 'row', axis=1, tiled=True)  37.2 us
    reduce_scatter x1, waiting for transfers between devices, local(): lax.psum_scatter(lax.dot_general(part_cols, weight, (((0,), (0,)), ((), (...  28 us
    all_gather x1, blocking collectives, local(): lax.all_gather(slope, ('col', 'rep'), axis=0, tiled=True)  6.78 us
  transfers between devices with their start and end apart: 2, of which 2 were waited for; matrix products, arithmetic and copies ran while one was open for 1% of the time, Pallas kernels for 0%

commit v1 on v0

v1 whole, which is shorter than its diff:
```python
import functools

import jax
import jax.numpy as jnp
from jax import lax
from jax.experimental import pallas as pl
from jax.experimental.pallas import tpu as pltpu
from jax.sharding import PartitionSpec as P

F32 = jnp.float32
BF16 = jnp.bfloat16
SUBLANES = 8


def dot(a, b, dims, precision=None):
    return lax.dot_general(a, b, (dims, ((), ())), precision=precision, preferred_element_type=F32)


def split(x):
    high = x.astype(BF16)
    return high, (x - high.astype(F32)).astype(BF16)


def split_kernel(slabs, high, low, held, sems):
    count = slabs.shape[0]
    copies = [pltpu.make_async_copy(slabs.at[t], held.at[t], sems.at[t]) for t in range(count)]
    for copy in copies:
        copy.start()
    for t, copy in enumerate(copies):
        copy.wait()
        high[t], low[t] = split(held[t])


def split_slabs(slabs):
    count = slabs.shape[0]
    return pl.pallas_call(
        split_kernel,
        out_shape=(pltpu.VMEM(slabs.shape, BF16), pltpu.VMEM(slabs.shape, BF16)),
        in_specs=[pl.BlockSpec(memory_space=pl.ANY)],
        out_specs=[pl.BlockSpec(memory_space=pltpu.VMEM)] * 2,
        scratch_shapes=[pltpu.VMEM(slabs.shape, F32), pltpu.SemaphoreType.DMA((count,))],
        compiler_params=pltpu.CompilerParams(vmem_limit_bytes=32 * 2**20),
        cost_estimate=pl.CostEstimate(flops=4 * slabs.size, bytes_accessed=8 * slabs.size, transcendentals=0),
        name="split_slabs",
    )(slabs)


def mix_kernel(sizes, sources, rows, cols, counts, slab_high, slab_low, *refs):
    groups, halves = sizes
    pieces, outs, (picked, total) = refs[: len(sources)], refs[len(sources) : -2], refs[-2:]
    slots = slab_high.shape[0]
    half_width, block = pieces[0].shape
    live = counts[0, 0]
    row, col, rep = lax.axis_index("row"), lax.axis_index("col"), lax.axis_index("rep")

    total[...] = jnp.zeros_like(total)
    for piece, source in zip(pieces, sources):
        block_id = source(row)

        @pl.loop(0, slots)
        def _(t):
            @pl.when((t < live) & (cols[0, 0, t] == block_id))
            def _():
                high, low = split(piece[...])
                picked[t, :half_width] = high
                picked[t, half_width:] = low

    for t in range(slots):

        @pl.when(t < live)
        def _():
            by_high = dot(picked[t], slab_high[t], ((1,), (1,)))
            by_low = dot(picked[t, :half_width], slab_low[t], ((1,), (1,)))
            total[rows[0, 0, t]] += by_high[:half_width] + by_high[half_width:] + by_low

    part = block // halves
    for k, out in enumerate(outs):
        for h in range(halves):
            begin = pl.multiple_of(lax.rem(rep + h, halves) * part, part)
            out[h] = total[lax.rem(col + k, groups), :, pl.ds(begin, part)]


def mix(sizes, sources, rows, cols, counts, slab_high, slab_low, pieces):
    groups, halves = sizes
    slots = slab_high.shape[0]
    half_width, block = pieces[0].shape
    out = jax.ShapeDtypeStruct((halves, half_width, block // halves), F32)
    return pl.pallas_call(
        functools.partial(mix_kernel, sizes, sources),
        out_shape=[out] * groups,
        in_specs=[pl.BlockSpec(memory_space=pltpu.SMEM)] * 3
        + [pl.BlockSpec(memory_space=pltpu.VMEM)] * (2 + len(pieces)),
        out_specs=[pl.BlockSpec(memory_space=pltpu.VMEM)] * groups,
        scratch_shapes=[
            pltpu.VMEM((slots, 2 * half_width, block), BF16),
            pltpu.VMEM((groups, half_width, block), F32),
        ],
        compiler_params=pltpu.CompilerParams(vmem_limit_bytes=32 * 2**20),
        name="mix",
    )(rows, cols, counts, slab_high, slab_low, *pieces)


def node_kernel(parts, *refs):
    highest = lax.Precision.HIGHEST
    (own, got), refs = refs[:2], refs[2:]
    others, refs = refs[: parts - 1], refs[parts - 1 :]
    weights, refs = refs[:parts], refs[parts:]
    bias, cotangent, output, *grads = refs
    mixed = [own[...] + got[...]] + [other[...] for other in others]
    preact = bias[...] + sum(dot(m, w[...], ((0,), (0,)), highest) for m, w in zip(mixed, weights))
    squash = 1.0 / (1.0 + jnp.exp(-preact))
    output[...] = preact * squash
    slope = cotangent[...] * squash * (1.0 + preact * (1.0 - squash))
    half_width = own.shape[0]
    bias_term = jnp.sum(slope, axis=0, keepdims=True)
    for k, (m, grad) in enumerate(zip(mixed, grads)):
        grad[:half_width] = dot(m, slope, ((1,), (0,)), highest)
        grad[half_width:] = jnp.broadcast_to(bias_term, (SUBLANES, bias_term.shape[1]))


def node_step(own, got, others, weights, bias, cotangent):
    parts = len(weights)
    half_width = own.shape[0]
    width = cotangent.shape[1]
    grad = jax.ShapeDtypeStruct((half_width + SUBLANES, width), F32)
    return pl.pallas_call(
        functools.partial(node_kernel, parts),
        out_shape=[jax.ShapeDtypeStruct(cotangent.shape, F32)] + [grad] * parts,
        in_specs=[pl.BlockSpec(memory_space=pltpu.VMEM)] * (4 + 2 * parts - 1),
        out_specs=[pl.BlockSpec(memory_space=pltpu.VMEM)] * (1 + parts),
        compiler_params=pltpu.CompilerParams(vmem_limit_bytes=32 * 2**20),
        name="node_step",
    )(own, got, *others, *weights, bias.reshape(1, width), cotangent)


def shift(x, axis, size, k, inner=1):
    outer = size // inner
    return lax.ppermute(x, axis, [(i, (i // inner + k) % outer * inner + i % inner) for i in range(size)])


def swap(x, axis, size, bit):
    return lax.ppermute(x, axis, [(i, i ^ bit) for i in range(size)])


def sum_over(x, axis, size):
    if size & (size - 1):
        return lax.psum(x, axis)
    bit = 1
    while bit < size:
        x = x + swap(x, axis, size, bit)
        bit *= 2
    return x


def local(row_size, groups, halves, adj_tiles, tile_rows, tile_cols, tile_counts, features_t, weight, bias_vec, cotangent):
    inner = 2 if row_size % 2 == 0 else 1
    outer = row_size // inner

    weights = [weight] + [shift(weight, "rep", halves, -k) for k in range(1, halves)]

    pieces, sources = [], []
    for k in range(outer):
        piece = shift(features_t, "row", row_size, k, inner) if k else features_t
        for j in range(inner):
            pieces.append(swap(piece, "row", row_size, j) if j else piece)
            sources.append(
                lambda row, k=k, j=j: lax.rem(row // inner + outer - k, outer) * inner + lax.bitwise_xor(row % inner, j)
            )
    slab_high, slab_low = split_slabs(adj_tiles[0, 0])
    parts = mix((groups, halves), sources, tile_rows, tile_cols, tile_counts, slab_high, slab_low, pieces)

    own = parts[0]
    got = shift(parts[1], "col", groups, 1) if groups > 1 else jnp.zeros_like(own)
    for k in range(2, groups):
        got = got + shift(parts[k], "col", groups, k)
    others = [shift(own[k] + got[k], "rep", halves, k) for k in range(1, halves)]
    output, *grads = node_step(own[0], got[0], others, _by_source(weights, halves), bias_vec, cotangent)
    grad = grads[0]
    for k in range(1, halves):
        grad = grad + shift(grads[k], "rep", halves, -k)
    grad = sum_over(grad, "col", groups)
    grad = sum_over(grad, "row", row_size)
    half_width = features_t.shape[0]
    return output, grad[:half_width], grad[half_width]


def _by_source(weights, halves):
    return [weights[0]] + [weights[halves - k] for k in range(1, halves)]


def solution(mesh):
    row_size, groups, halves = (mesh.shape[axis] for axis in ("row", "col", "rep"))
    in_specs = (
        P("row", "col", None, None, None),
        P("row", "col", None),
        P("row", "col", None),
        P("row", "col"),
        P("rep", ("row", "col")),
        P("rep", None),
        P(),
        P(("row", "col", "rep"), None),
    )
    out_specs = (P(("row", "col", "rep"), None), P("rep", None), P())
    return jax.shard_map(
        functools.partial(local, row_size, groups, halves),
        mesh=mesh,
        in_specs=in_specs,
        out_specs=out_specs,
        check_vma=False,
    )
```

time: 180 us -> 53.5 us (0.30)
  blocking collectives: 83.6 us -> 0 us
  waiting for transfers between devices: 66 us -> 22.8 us
  starting transfers between devices: 0.08 us -> 20.5 us
  between operations: 20 us -> 1.39 us
  matrix products: 5.29 us -> 0 us
  Pallas kernels: 0 us -> 5.23 us
  other arithmetic: 2.29 us -> 0.05 us
    psum x1 -> x0, blocking collectives: 76.8 us -> none  [local(): grad_weight, summed_bias = lax.psum((grad_part, local_bias), ('row', 'col'))]
    all_gather x1 -> x0, waiting for transfers between devices: 37.2 us -> none  [local(): shard_piece = lax.all_gather(features_t, 'row', axis=1, tiled=True)]
    reduce_scatter x1 -> x0, waiting for transfers between devices: 28 us -> none  [local(): lax.psum_scatter(lax.dot_general(part_cols, weight, (((0,), (0,)), ((), (...]
    ppermute x0 -> x15, waiting for transfers between devices: none -> 22.8 us  [the longest x8 13.4 us: swap(): return lax.ppermute(x, axis, [(i, i ^ bit) for i in range(size)])]
    ppermute x0 -> x15, starting transfers between devices: none -> 20.5 us  [the longest x8 11 us: swap(): return lax.ppermute(x, axis, [(i, i ^ bit) for i in range(size)])]
    all_gather x1 -> x0, blocking collectives: 6.78 us -> none  [local(): lax.all_gather(slope, ('col', 'rep'), axis=0, tiled=True)]
    dot_general x4 -> x0, matrix products: 5.29 us -> none  [the longest x1 2.43 us: add_block(): lax.dot_general(columns, slabs[slot_idx], (((1,), (1,)), ((), ())), preci...]
    pallas_call x0 -> x3, Pallas kernels: none -> 5.23 us  [the longest x1 2.91 us: mix(): pl.pallas_call(functools.partial(mix_kernel, sizes, sources), out_shape=[...]
  transfers between devices with their start and end apart: 2 -> 15, of which waited for: 2 -> 11; matrix products, arithmetic and copies ran while one was open for 1% -> 0% of each run, Pallas kernels for 0% -> 2%
where the time goes in v1:
time: 53.5 us; the launch traced here: 53.3 us
  waiting for transfers between devices  22.8 us (43%)
  starting transfers between devices  20.5 us (38%)
  Pallas kernels  5.23 us (10%)
  local copies, waits for them, and re-layouts  3.34 us (6%)
  between operations  1.39 us (3%)
    ppermute x8, waiting for transfers between devices, swap(): return lax.ppermute(x, axis, [(i, i ^ bit) for i in range(size)])  13.4 us
    ppermute x8, starting transfers between devices, swap(): return lax.ppermute(x, axis, [(i, i ^ bit) for i in range(size)])  11 us
    ppermute x7, starting transfers between devices, shift(): lax.ppermute(x, axis, [(i, (i // inner + k) % outer * inner + i % inner)...  9.51 us
    ppermute x7, waiting for transfers between devices, shift(): lax.ppermute(x, axis, [(i, (i // inner + k) % outer * inner + i % inner)...  9.45 us
    pallas_call x1, Pallas kernels, mix(): pl.pallas_call(functools.partial(mix_kernel, sizes, sources), out_shape=[...  2.91 us
    unnamed x14, local copies, waits for them, and re-layouts  2.21 us
    pallas_call x1, Pallas kernels, node_step(): pl.pallas_call(functools.partial(node_kernel, parts), out_shape=[jax.Shap...  1.44 us
  transfers between devices with their start and end apart: 15, of which 11 were waited for; matrix products, arithmetic and copies ran while one was open for 0% of the time, Pallas kernels for 2%

profile of v1, /device:TPU:0, one launch (start us, length us, event | category | flops | bytes accessed | tf_op | source)
XLA Modules:
  0.0 53.3 jit_solution(7634237735174528606)
XLA Ops:
  0.6 3.1 %collective-permute-start.1 = (f32[64,512]{1,0:T(8,128)}, f32[64,512]{1,0:T(8,128)S(1)}, u32[]{:S(2)}, u32[]{:S(2)}) collective-permute-start(f32[64,512]{1,0:T(8,128)} %refs_0_.1), channel_id=1, source_target_pairs={{0,8},{4,12},{8,16},{12,20},{16,24},{20,28},{24,0},{28,4},{1,9},{5... | collective-permute-start | bytes 393224 | tf_op jit(solution)/shard_map/ppermute | solution.py:138
  3.7 2.6 %collective-permute-start.3 = (f32[64,512]{1,0:T(8,128)}, f32[64,512]{1,0:T(8,128)S(1)}, u32[]{:S(2)}, u32[]{:S(2)}) collective-permute-start(f32[64,512]{1,0:T(8,128)} %refs_0_.1), channel_id=1, source_target_pairs={{0,16},{4,20},{8,24},{12,28},{16,0},{20,4},{24,8},{28,12},{1,17},{... | collective-permute-start | bytes 393224 | tf_op jit(solution)/shard_map/ppermute | solution.py:138
  6.3 1.3 %collective-permute-start.5 = (f32[64,512]{1,0:T(8,128)}, f32[64,512]{1,0:T(8,128)S(1)}, u32[]{:S(2)}, u32[]{:S(2)}) collective-permute-start(f32[64,512]{1,0:T(8,128)} %refs_0_.1), channel_id=1, source_target_pairs={{0,24},{4,28},{8,0},{12,4},{16,8},{20,12},{24,16},{28,20},{1,25},{... | collective-permute-start | bytes 393224 | tf_op jit(solution)/shard_map/ppermute | solution.py:138
  7.6 1.5 %collective-permute-start = (f32[64,512]{1,0:T(8,128)}, f32[64,512]{1,0:T(8,128)S(1)}, u32[]{:S(2)}, u32[]{:S(2)}) collective-permute-start(f32[64,512]{1,0:T(8,128)} %refs_0_.1), channel_id=1, source_target_pairs={{0,4},{4,0},{8,12},{12,8},{16,20},{20,16},{24,28},{28,24},{1,5},{5... | collective-permute-start | bytes 393224 | tf_op jit(solution)/shard_map/ppermute | solution.py:142
  9.1 1.2 %collective-permute-done.1.refs_2_ = f32[64,512]{1,0:T(8,128)S(1)} collective-permute-done((f32[64,512]{1,0:T(8,128)}, f32[64,512]{1,0:T(8,128)S(1)}, u32[]{:S(2)}, u32[]{:S(2)}) %collective-permute-start.1) | collective-permute-done | bytes 131104 | tf_op jit(solution)/shard_map/ppermute | solution.py:138
  10.4 1.7 %collective-permute-start.2 = (f32[64,512]{1,0:T(8,128)S(1)}, f32[64,512]{1,0:T(8,128)S(1)}, u32[]{:S(2)}, u32[]{:S(2)}) collective-permute-start(f32[64,512]{1,0:T(8,128)S(1)} %collective-permute-done.1.refs_2_), channel_id=1, source_target_pairs={{0,4},{4,0},{8,12},{12,8},{16,20},{20,16},{24,28},{28,24},{1,5},{5... | collective-permute-start | bytes 393224 | tf_op jit(solution)/shard_map/ppermute | solution.py:142
  12.1 3.0 %collective-permute-done.3.refs_4_ = f32[64,512]{1,0:T(8,128)S(1)} collective-permute-done((f32[64,512]{1,0:T(8,128)}, f32[64,512]{1,0:T(8,128)S(1)}, u32[]{:S(2)}, u32[]{:S(2)}) %collective-permute-start.3) | collective-permute-done | bytes 131104 | tf_op jit(solution)/shard_map/ppermute | solution.py:138
  15.2 1.5 %collective-permute-start.4 = (f32[64,512]{1,0:T(8,128)S(1)}, f32[64,512]{1,0:T(8,128)S(1)}, u32[]{:S(2)}, u32[]{:S(2)}) collective-permute-start(f32[64,512]{1,0:T(8,128)S(1)} %collective-permute-done.3.refs_4_), channel_id=1, source_target_pairs={{0,4},{4,0},{8,12},{12,8},{16,20},{20,16},{24,28},{28,24},{1,5},{5... | collective-permute-start | bytes 393224 | tf_op jit(solution)/shard_map/ppermute | solution.py:142
  17.8 2.2 %copy-done = f32[1,1,4,512,512]{4,3,2,1,0:T(8,128)S(1)} copy-done((f32[1,1,4,512,512]{4,3,2,1,0:T(8,128)S(1)}, f32[1,1,4,512,512]{4,3,2,1,0:T(8,128)}, u32[]{:S(2)}) %copy-start) | copy-done | bytes 4194328
  20.0 0.9 %split_slabs.1 = (bf16[4,512,512]{2,1,0:T(8,128)(2,1)S(1)}, bf16[4,512,512]{2,1,0:T(8,128)(2,1)S(1)}) custom-call(f32[4,512,512]{2,1,0:T(8,128)S(1)} %bitcast.10), custom_call_target="tpu_custom_call" | custom-call | flops 4194304 | bytes 8388608 | tf_op jit(solution)/shard_map/split_slabs/pallas_call | solution.py:36
  21.5 1.8 %collective-permute-done.6.refs_7_ = f32[64,512]{1,0:T(8,128)S(1)} collective-permute-done((f32[64,512]{1,0:T(8,128)S(1)}, f32[64,512]{1,0:T(8,128)S(1)}, u32[]{:S(2)}, u32[]{:S(2)}) %collective-permute-start.6) | collective-permute-done | bytes 131104 | tf_op jit(solution)/shard_map/ppermute | solution.py:142
  23.3 2.9 %mix.1 = (f32[2,64,256]{2,1,0:T(8,128)S(1)}, f32[2,64,256]{2,1,0:T(8,128)S(1)}) custom-call(s32[1,1,4]{2,1,0:T(1,128)S(1)} %copy-done.4, s32[1,1,4]{2,1,0:T(1,128)S(1)} %copy-done.5, s32[1,1]{1,0:T(1,128)S(6)} %copy.11.counts, bf16[4,512,512]{2,1,0:T(8,128)(2,1)S(1)} %get-tuple-element.10.slab_high, bf16[4,512,512]{2,1,0:T(8,128)(2,1)S(1)} %get-tuple-element.11.slab_low, ...), custom_call_target="tpu_custom_call" | custom-call | tf_op jit(solution)/shard_map/mix/pallas_call | solution.py:88
  26.3 1.6 %collective-permute-start.7 = (f32[2,64,256]{2,1,0:T(8,128)S(1)}, f32[2,64,256]{2,1,0:T(8,128)S(1)}, u32[]{:S(2)}, u32[]{:S(2)}) collective-permute-start(f32[2,64,256]{2,1,0:T(8,128)S(1)} %get-tuple-element.13), channel_id=1, source_target_pairs={{0,2},{2,0},{1,3},{3,1},{4,6},{6,4},{5,7},{7,5},{8,10},{10,8},{9,1... | collective-permute-start | bytes 393224 | tf_op jit(solution)/shard_map/ppermute | solution.py:138
  27.8 3.5 %collective-permute-done.7 = f32[2,64,256]{2,1,0:T(8,128)S(1)} collective-permute-done((f32[2,64,256]{2,1,0:T(8,128)S(1)}, f32[2,64,256]{2,1,0:T(8,128)S(1)}, u32[]{:S(2)}, u32[]{:S(2)}) %collective-permute-start.7) | collective-permute-done | bytes 131104 | tf_op jit(solution)/shard_map/ppermute | solution.py:138
  31.9 0.9 %collective-permute-done.9.refs_4_ = f32[64,128]{1,0:T(8,128)S(1)} collective-permute-done((f32[64,128]{1,0:T(8,128)S(1)}, f32[64,128]{1,0:T(8,128)S(1)}, u32[]{:S(2)}, u32[]{:S(2)}) %collective-permute-start.9) | collective-permute-done | bytes 32800 | tf_op jit(solution)/shard_map/ppermute | solution.py:138
  32.8 1.4 %node_step.1 = (f32[256,128]{1,0:T(8,128)}, f32[72,128]{1,0:T(8,128)S(1)}, f32[72,128]{1,0:T(8,128)S(1)}) custom-call(f32[64,256]{1,0:T(8,128)S(1)} %get-tuple-element.18.refs_0_, f32[64,256]{1,0:T(8,128)S(1)} %get-tuple-element.19.refs_1_, f32[64,256]{1,0:T(8,128)S(1)} %collective-permute-done.8.refs_2_, f32[64,128]{1,0:T(8,128)S(1)} %copy-done.3, ...), custom_call_target="tpu_custom_call" | custom-call | tf_op jit(solution)/shard_map/node_step/pallas_call | solution.py:126
  34.6 0.9 %collective-permute-done.10 = f32[72,128]{1,0:T(8,128)S(1)} collective-permute-done((f32[72,128]{1,0:T(8,128)S(1)}, f32[72,128]{1,0:T(8,128)S(1)}, u32[]{:S(2)}, u32[]{:S(2)}) %collective-permute-start.10) | collective-permute-done | bytes 36896 | tf_op jit(solution)/shard_map/ppermute | solution.py:138
  35.4 1.5 %collective-permute-start.11 = (f32[72,128]{1,0:T(8,128)S(1)}, f32[72,128]{1,0:T(8,128)S(1)}, u32[]{:S(2)}, u32[]{:S(2)}) collective-permute-start(f32[72,128]{1,0:T(8,128)S(1)} %add.23), channel_id=1, source_target_pairs={{0,2},{2,0},{1,3},{3,1},{4,6},{6,4},{5,7},{7,5},{8,10},{10,8},{9,1... | collective-permute-start | bytes 110600 | tf_op jit(solution)/shard_map/ppermute | solution.py:142
  36.9 2.4 %collective-permute-done.11 = f32[72,128]{1,0:T(8,128)S(1)} collective-permute-done((f32[72,128]{1,0:T(8,128)S(1)}, f32[72,128]{1,0:T(8,128)S(1)}, u32[]{:S(2)}, u32[]{:S(2)}) %collective-permute-start.11) | collective-permute-done | bytes 36896 | tf_op jit(solution)/shard_map/ppermute | solution.py:142
  39.5 3.9 %collective-permute-done.12 = f32[72,128]{1,0:T(8,128)S(1)} collective-permute-done((f32[72,128]{1,0:T(8,128)S(1)}, f32[72,128]{1,0:T(8,128)S(1)}, u32[]{:S(2)}, u32[]{:S(2)}) %collective-permute-start.12) | collective-permute-done | bytes 36896 | tf_op jit(solution)/shard_map/ppermute | solution.py:142
  43.4 1.6 %collective-permute-start.13 = (f32[72,128]{1,0:T(8,128)S(1)}, f32[72,128]{1,0:T(8,128)S(1)}, u32[]{:S(2)}, u32[]{:S(2)}) collective-permute-start(f32[72,128]{1,0:T(8,128)S(1)} %add.25), channel_id=1, source_target_pairs={{0,8},{4,12},{8,0},{12,4},{16,24},{20,28},{24,16},{28,20},{1,9},{5... | collective-permute-start | bytes 110600 | tf_op jit(solution)/shard_map/ppermute | solution.py:142
  45.0 2.3 %collective-permute-done.13 = f32[72,128]{1,0:T(8,128)S(1)} collective-permute-done((f32[72,128]{1,0:T(8,128)S(1)}, f32[72,128]{1,0:T(8,128)S(1)}, u32[]{:S(2)}, u32[]{:S(2)}) %collective-permute-start.13) | collective-permute-done | bytes 36896 | tf_op jit(solution)/shard_map/ppermute | solution.py:142
  47.3 2.5 %collective-permute-start.14 = (f32[72,128]{1,0:T(8,128)S(1)}, f32[72,128]{1,0:T(8,128)S(1)}, u32[]{:S(2)}, u32[]{:S(2)}) collective-permute-start(f32[72,128]{1,0:T(8,128)S(1)} %add.26), channel_id=1, source_target_pairs={{0,16},{4,20},{8,24},{12,28},{16,0},{20,4},{24,8},{28,12},{1,17},{... | collective-permute-start | bytes 110600 | tf_op jit(solution)/shard_map/ppermute | solution.py:142
  49.8 2.4 %collective-permute-done.14 = f32[72,128]{1,0:T(8,128)S(1)} collective-permute-done((f32[72,128]{1,0:T(8,128)S(1)}, f32[72,128]{1,0:T(8,128)S(1)}, u32[]{:S(2)}, u32[]{:S(2)}) %collective-permute-start.14) | collective-permute-done | bytes 36896 | tf_op jit(solution)/shard_map/ppermute | solution.py:142
  (31 shorter events, 3.4 us)
Async XLA Ops:
  0.6 9.7 %collective-permute-start.1 = (f32[64,512]{1,0:T(8,128)}, f32[64,512]{1,0:T(8,128)S(1)}, u32[]{:S(2)}, u32[]{:S(2)}) collective-permute-start(f32[64,512]{1,0:T(8,128)} %refs_0_.1), channel_id=1, source_target_pairs={{0,8},{4,12},{8,16},{12,20},{16,24},{20,28},{24,0},{28,4},{1,9},{5... | collective-permute-start | bytes 393224 | tf_op jit(solution)/shard_map/ppermute | solution.py:138
  3.7 11.4 %collective-permute-start.3 = (f32[64,512]{1,0:T(8,128)}, f32[64,512]{1,0:T(8,128)S(1)}, u32[]{:S(2)}, u32[]{:S(2)}) collective-permute-start(f32[64,512]{1,0:T(8,128)} %refs_0_.1), channel_id=1, source_target_pairs={{0,16},{4,20},{8,24},{12,28},{16,0},{20,4},{24,8},{28,12},{1,17},{... | collective-permute-start | bytes 393224 | tf_op jit(solution)/shard_map/ppermute | solution.py:138
  6.3 10.3 %collective-permute-start.5 = (f32[64,512]{1,0:T(8,128)}, f32[64,512]{1,0:T(8,128)S(1)}, u32[]{:S(2)}, u32[]{:S(2)}) collective-permute-start(f32[64,512]{1,0:T(8,128)} %refs_0_.1), channel_id=1, source_target_pairs={{0,24},{4,28},{8,0},{12,4},{16,8},{20,12},{24,16},{28,20},{1,25},{... | collective-permute-start | bytes 393224 | tf_op jit(solution)/shard_map/ppermute | solution.py:138
  7.6 13.3 %collective-permute-start = (f32[64,512]{1,0:T(8,128)}, f32[64,512]{1,0:T(8,128)S(1)}, u32[]{:S(2)}, u32[]{:S(2)}) collective-permute-start(f32[64,512]{1,0:T(8,128)} %refs_0_.1), channel_id=1, source_target_pairs={{0,4},{4,0},{8,12},{12,8},{16,20},{20,16},{24,28},{28,24},{1,5},{5... | collective-permute-start | bytes 393224 | tf_op jit(solution)/shard_map/ppermute | solution.py:142
  10.4 10.6 %collective-permute-start.2 = (f32[64,512]{1,0:T(8,128)S(1)}, f32[64,512]{1,0:T(8,128)S(1)}, u32[]{:S(2)}, u32[]{:S(2)}) collective-permute-start(f32[64,512]{1,0:T(8,128)S(1)} %collective-permute-done.1.refs_2_), channel_id=1, source_target_pairs={{0,4},{4,0},{8,12},{12,8},{16,20},{20,16},{24,28},{28,24},{1,5},{5... | collective-permute-start | bytes 393224 | tf_op jit(solution)/shard_map/ppermute | solution.py:142
  15.2 6.4 %collective-permute-start.4 = (f32[64,512]{1,0:T(8,128)S(1)}, f32[64,512]{1,0:T(8,128)S(1)}, u32[]{:S(2)}, u32[]{:S(2)}) collective-permute-start(f32[64,512]{1,0:T(8,128)S(1)} %collective-permute-done.3.refs_4_), channel_id=1, source_target_pairs={{0,4},{4,0},{8,12},{12,8},{16,20},{20,16},{24,28},{28,24},{1,5},{5... | collective-permute-start | bytes 393224 | tf_op jit(solution)/shard_map/ppermute | solution.py:142
  16.6 6.6 %collective-permute-start.6 = (f32[64,512]{1,0:T(8,128)S(1)}, f32[64,512]{1,0:T(8,128)S(1)}, u32[]{:S(2)}, u32[]{:S(2)}) collective-permute-start(f32[64,512]{1,0:T(8,128)S(1)} %collective-permute-done.5.refs_6_), channel_id=1, source_target_pairs={{0,4},{4,0},{8,12},{12,8},{16,20},{20,16},{24,28},{28,24},{1,5},{5... | collective-permute-start | bytes 393224 | tf_op jit(solution)/shard_map/ppermute | solution.py:142
  17.8 2.2 %copy-start = (f32[1,1,4,512,512]{4,3,2,1,0:T(8,128)S(1)}, f32[1,1,4,512,512]{4,3,2,1,0:T(8,128)}, u32[]{:S(2)}) copy-start(f32[1,1,4,512,512]{4,3,2,1,0:T(8,128)} %param.8) | copy-start | bytes 12582916
  20.0 3.3 %copy-start.1 = (f32[64,512]{1,0:T(8,128)S(1)}, f32[64,512]{1,0:T(8,128)}, u32[]{:S(2)}) copy-start(f32[64,512]{1,0:T(8,128)} %refs_0_.1) | copy-start | bytes 393220
  20.0 3.3 %copy-start.4 = (s32[1,1,4]{2,1,0:T(1,128)S(1)}, s32[1,1,4]{2,1,0:T(1,128)}, u32[]{:S(2)}) copy-start(s32[1,1,4]{2,1,0:T(1,128)} %rows.1) | copy-start | bytes 52
  20.0 3.3 %copy-start.5 = (s32[1,1,4]{2,1,0:T(1,128)S(1)}, s32[1,1,4]{2,1,0:T(1,128)}, u32[]{:S(2)}) copy-start(s32[1,1,4]{2,1,0:T(1,128)} %cols.1) | copy-start | bytes 52
  23.3 8.1 %copy-start.3 = (f32[64,128]{1,0:T(8,128)S(1)}, f32[64,128]{1,0:T(8,128)}, u32[]{:S(2)}) copy-start(f32[64,128]{1,0:T(8,128)} %refs_3_.1) | copy-start | bytes 98308
  23.3 9.4 %copy-start.2 = (f32[256,128]{1,0:T(8,128)S(1)}, f32[256,128]{1,0:T(8,128)}, u32[]{:S(2)}) copy-start(f32[256,128]{1,0:T(8,128)} %refs_6_.1) | copy-start | bytes 393220
  23.3 9.4 %copy-start.6 = (f32[128]{0:T(128)S(1)}, f32[128]{0:T(128)}, u32[]{:S(2)}) copy-start(f32[128]{0:T(128)} %param.14) | copy-start | bytes 1540
  26.3 5.0 %collective-permute-start.7 = (f32[2,64,256]{2,1,0:T(8,128)S(1)}, f32[2,64,256]{2,1,0:T(8,128)S(1)}, u32[]{:S(2)}, u32[]{:S(2)}) collective-permute-start(f32[2,64,256]{2,1,0:T(8,128)S(1)} %get-tuple-element.13), channel_id=1, source_target_pairs={{0,2},{2,0},{1,3},{3,1},{4,6},{6,4},{5,7},{7,5},{8,10},{10,8},{9,1... | collective-permute-start | bytes 393224 | tf_op jit(solution)/shard_map/ppermute | solution.py:138
  31.3 1.4 %collective-permute-start.8 = (f32[64,256]{1,0:T(8,128)S(1)}, f32[64,256]{1,0:T(8,128)S(1)}, u32[]{:S(2)}, u32[]{:S(2)}) collective-permute-start(f32[64,256]{1,0:T(8,128)S(1)} %get-tuple-element.17), channel_id=1, source_target_pairs={{0,1},{1,0},{2,3},{3,2},{4,5},{5,4},{6,7},{7,6},{8,9},{9,8},{10,11... | collective-permute-start | bytes 196616 | tf_op jit(solution)/shard_map/ppermute | solution.py:138
  31.4 1.4 %collective-permute-start.9 = (f32[64,128]{1,0:T(8,128)S(1)}, f32[64,128]{1,0:T(8,128)S(1)}, u32[]{:S(2)}, u32[]{:S(2)}) collective-permute-start(f32[64,128]{1,0:T(8,128)S(1)} %copy-done.3), channel_id=1, source_target_pairs={{0,1},{1,0},{2,3},{3,2},{4,5},{5,4},{6,7},{7,6},{8,9},{9,8},{10,11... | collective-permute-start | bytes 98312 | tf_op jit(solution)/shard_map/ppermute | solution.py:138
  34.2 1.2 %collective-permute-start.10 = (f32[72,128]{1,0:T(8,128)S(1)}, f32[72,128]{1,0:T(8,128)S(1)}, u32[]{:S(2)}, u32[]{:S(2)}) collective-permute-start(f32[72,128]{1,0:T(8,128)S(1)} %get-tuple-element.16), channel_id=1, source_target_pairs={{0,1},{1,0},{2,3},{3,2},{4,5},{5,4},{6,7},{7,6},{8,9},{9,8},{10,11... | collective-permute-start | bytes 110600 | tf_op jit(solution)/shard_map/ppermute | solution.py:138
  35.4 4.0 %collective-permute-start.11 = (f32[72,128]{1,0:T(8,128)S(1)}, f32[72,128]{1,0:T(8,128)S(1)}, u32[]{:S(2)}, u32[]{:S(2)}) collective-permute-start(f32[72,128]{1,0:T(8,128)S(1)} %add.23), channel_id=1, source_target_pairs={{0,2},{2,0},{1,3},{3,1},{4,6},{6,4},{5,7},{7,5},{8,10},{10,8},{9,1... | collective-permute-start | bytes 110600 | tf_op jit(solution)/shard_map/ppermute | solution.py:142
  39.4 4.0 %collective-permute-start.12 = (f32[72,128]{1,0:T(8,128)S(1)}, f32[72,128]{1,0:T(8,128)S(1)}, u32[]{:S(2)}, u32[]{:S(2)}) collective-permute-start(f32[72,128]{1,0:T(8,128)S(1)} %add.24), channel_id=1, source_target_pairs={{0,4},{4,0},{8,12},{12,8},{16,20},{20,16},{24,28},{28,24},{1,5},{5... | collective-permute-start | bytes 110600 | tf_op jit(solution)/shard_map/ppermute | solution.py:142
  43.4 4.0 %collective-permute-start.13 = (f32[72,128]{1,0:T(8,128)S(1)}, f32[72,128]{1,0:T(8,128)S(1)}, u32[]{:S(2)}, u32[]{:S(2)}) collective-permute-start(f32[72,128]{1,0:T(8,128)S(1)} %add.25), channel_id=1, source_target_pairs={{0,8},{4,12},{8,0},{12,4},{16,24},{20,28},{24,16},{28,20},{1,9},{5... | collective-permute-start | bytes 110600 | tf_op jit(solution)/shard_map/ppermute | solution.py:142
  47.3 4.9 %collective-permute-start.14 = (f32[72,128]{1,0:T(8,128)S(1)}, f32[72,128]{1,0:T(8,128)S(1)}, u32[]{:S(2)}, u32[]{:S(2)}) collective-permute-start(f32[72,128]{1,0:T(8,128)S(1)} %add.26), channel_id=1, source_target_pairs={{0,16},{4,20},{8,24},{12,28},{16,0},{20,4},{24,8},{28,12},{1,17},{... | collective-permute-start | bytes 110600 | tf_op jit(solution)/shard_map/ppermute | solution.py:142

commit v2 on v1

v2 whole, which is shorter than its diff:
```python
import functools

import jax
import jax.numpy as jnp
from jax import lax
from jax.experimental import pallas as pl
from jax.experimental.pallas import tpu as pltpu
from jax.sharding import PartitionSpec as P

F32 = jnp.float32
BF16 = jnp.bfloat16
SUBLANES = 8
VMEM_BYTES = 40 * 2**20


def dot(a, b, dims=((1,), (0,))):
    return lax.dot_general(a, b, (dims, ((), ())), preferred_element_type=F32)


def split(x):
    high = x.astype(BF16)
    return high, (x - high.astype(F32)).astype(BF16)


def dot_split(a, b, dims):
    (ah, al), (bh, bl) = a, b
    return dot(ah, bh, dims) + (dot(ah, bl, dims) + dot(al, bh, dims))


def call(kernel, out_shape, spaces, name, scratch=(), cost=None):
    return pl.pallas_call(
        kernel,
        out_shape=out_shape,
        in_specs=[pl.BlockSpec(memory_space=space) for space in spaces],
        out_specs=jax.tree.map(lambda _: pl.BlockSpec(memory_space=pltpu.VMEM), out_shape),
        scratch_shapes=list(scratch),
        compiler_params=pltpu.CompilerParams(vmem_limit_bytes=VMEM_BYTES),
        cost_estimate=cost,
        name=name,
    )


def split_kernel(slabs, high, low, held, sems):
    count = slabs.shape[0]
    copies = [pltpu.make_async_copy(slabs.at[t], held.at[t], sems.at[t]) for t in range(count)]
    for copy in copies:
        copy.start()
    for t, copy in enumerate(copies):
        copy.wait()
        high[t], low[t] = split(held[t].T)


def split_slabs(slabs):
    count = slabs.shape[0]
    out = pltpu.VMEM(slabs.shape, BF16)
    scratch = [pltpu.VMEM(slabs.shape, F32), pltpu.SemaphoreType.DMA((count,))]
    cost = pl.CostEstimate(flops=4 * slabs.size, bytes_accessed=8 * slabs.size, transcendentals=0)
    return call(split_kernel, (out, out), [pl.ANY], "split_slabs", scratch, cost)(
        pltpu.with_memory_space_constraint(slabs, pltpu.HBM)
    )


def product(piece, high, low):
    half_width = piece.shape[0] // 2
    by_high = dot(piece, high)
    return by_high[:half_width] + by_high[half_width:] + dot(piece[:half_width], low)


def pick(picked, t, piece):
    half_width = piece.shape[0]
    picked[t, :half_width], picked[t, half_width:] = split(piece[...])


def early_kernel(sources, rows, cols, counts, high, low, *refs):
    pieces, (total, picked, found) = refs[: len(sources)], refs[-3:]
    slots = high.shape[0]
    live = counts[0, 0]
    row = lax.axis_index("row")
    for t in range(slots):
        found[t] = 0
    for piece, source in zip(pieces, sources):
        block = source(row)

        @pl.loop(0, slots)
        def _(t):
            @pl.when((t < live) & (cols[0, 0, t] == block))
            def _():
                found[t] = 1
                pick(picked, t, piece)

    total[...] = jnp.zeros_like(total)
    for t in range(slots):

        @pl.when(found[t] == 1)
        def _():
            total[rows[0, 0, t]] += product(picked[t], high[t], low[t])


def late_kernel(sizes, sources, rows, cols, counts, high, low, early, *refs):
    groups, halves = sizes
    pieces, outs, (total, picked) = refs[: len(sources)], refs[len(sources) : -2], refs[-2:]
    slots = high.shape[0]
    block_len = early.shape[2]
    live = counts[0, 0]
    row, col, rep = lax.axis_index("row"), lax.axis_index("col"), lax.axis_index("rep")
    total[...] = early[...]
    for piece, source in zip(pieces, sources):
        block = source(row)
        pick(picked, 0, piece)
        for t in range(slots):

            @pl.when((t < live) & (cols[0, 0, t] == block))
            def _():
                total[rows[0, 0, t]] += product(picked[0], high[t], low[t])

    part = block_len // halves
    for k, out in enumerate(outs):
        for h in range(halves):
            begin = pl.multiple_of(lax.rem(rep + h, halves) * part, part)
            out[h] = total[lax.rem(col + k, groups), :, pl.ds(begin, part)]


def mix(sizes, slot_info, slabs, early, late):
    groups, halves = sizes
    slots = slabs[0].shape[0]
    half_width, block_len = early[0][0].shape
    spaces = [pltpu.SMEM] * 3 + [pltpu.VMEM] * 2
    picked = pltpu.VMEM((slots, 2 * half_width, block_len), BF16)
    pieces, sources = zip(*early)
    total = call(
        functools.partial(early_kernel, sources),
        pltpu.VMEM((groups, half_width, block_len), F32),
        spaces + [pltpu.VMEM] * len(pieces),
        "mix_early",
        [picked, pltpu.SMEM((slots,), jnp.int32)],
        pl.CostEstimate(flops=6 * slabs[0].size * half_width, bytes_accessed=4 * slabs[0].size, transcendentals=0),
    )(*slot_info, *slabs, *pieces)
    pieces, sources = zip(*late)
    return call(
        functools.partial(late_kernel, sizes, sources),
        [pltpu.VMEM((halves, half_width, block_len // halves), F32)] * groups,
        spaces + [pltpu.VMEM] * (1 + len(pieces)),
        "mix_late",
        [pltpu.VMEM(total.shape, F32), picked],
    )(*slot_info, *slabs, total, *pieces)


def node_kernel(parts, *refs):
    (own, got), refs = refs[:2], refs[2:]
    others, refs = refs[: parts - 1], refs[parts - 1 :]
    weights, refs = refs[:parts], refs[parts:]
    bias, cotangent, output, *grads = refs
    half_width = own.shape[0]
    mixed = split(jnp.concatenate([own[...] + got[...]] + [other[...] for other in others]))
    weight = split(jnp.concatenate([w[...] for w in weights]))
    preact = bias[...] + dot_split(mixed, weight, ((0,), (0,)))
    squash = 1.0 / (1.0 + jnp.exp(-preact))
    output[...] = preact * squash
    slope = cotangent[...] * squash * (1.0 + preact * (1.0 - squash))
    bias_term = jnp.sum(slope, axis=0, keepdims=True)
    product = dot_split(mixed, split(slope), ((1,), (0,)))
    for k, grad in enumerate(grads):
        grad[:half_width] = product[k * half_width : (k + 1) * half_width]
        grad[half_width:] = jnp.broadcast_to(bias_term, (SUBLANES, bias_term.shape[1]))


def node_step(own, got, others, weights, bias, cotangent):
    parts = len(weights)
    width = cotangent.shape[1]
    grad = pltpu.VMEM((own.shape[0] + SUBLANES, width), F32)
    return call(
        functools.partial(node_kernel, parts),
        [pltpu.VMEM(cotangent.shape, F32)] + [grad] * parts,
        [pltpu.VMEM] * (4 + 2 * parts - 1),
        "node_step",
    )(own, got, *others, *weights, bias.reshape(1, width), cotangent)


def last_kernel(a, b, grad_weight, grad_bias):
    half_width = grad_weight.shape[0]
    grad_weight[...] = a[:half_width] + b[:half_width]
    grad_bias[...] = a[half_width] + b[half_width]


def last_step(a, b):
    half_width, width = a.shape[0] - SUBLANES, a.shape[1]
    out = [jax.ShapeDtypeStruct((half_width, width), F32), jax.ShapeDtypeStruct((width,), F32)]
    return call(last_kernel, out, [pltpu.VMEM] * 2, "last_step")(a, b)


def shift(x, axis, size, k):
    return lax.ppermute(x, axis, [(i, (i + k) % size) for i in range(size)])


def swap(x, axis, size, bit):
    return lax.ppermute(x, axis, [(i, i ^ bit) for i in range(size)])


def swap_two(x, axes, sizes, bits):
    (_, minor), perm = sizes, []
    for i in range(sizes[0]):
        for j in range(minor):
            perm.append((i * minor + j, (i ^ bits[0]) * minor + (j ^ bits[1])))
    return lax.ppermute(x, axes, perm)


def is_power(n):
    return n & (n - 1) == 0


def gather_row(x, size, held):
    if not is_power(size) or size < 2:
        pieces = [x] + [shift(x, "row", size, k) for k in range(1, size)]
        return [(p, lambda row, k=k: lax.rem(row + size - k, size)) for k, p in enumerate(pieces)], held
    found = {0: x}
    bit = size // 2
    while bit > 1:
        for mask in list(found):
            found[mask ^ bit] = swap(found[mask], "row", size, bit)
        if bit == size // 2:
            found[bit], held = lax.optimization_barrier((found[bit], held))
        bit //= 2
    order = sorted(found, key=lambda mask: (bin(mask).count("1"), mask))
    crossed = {0: swap(x, "row", size, 1)}
    first, _ = lax.optimization_barrier((found[order[1]], crossed[0])) if len(order) > 1 else (x, x)
    for mask in order[1:]:
        crossed[mask] = swap(first if mask == order[1] else found[mask], "row", size, 1)
    far = [(mask ^ 1, crossed[mask]) for mask in order]
    near = [(mask, found[mask]) for mask in order]
    return [(p, lambda row, mask=mask: lax.bitwise_xor(row, mask)) for mask, p in near + far], held


def sum_all(grad, groups, row_size):
    if not (is_power(groups) and is_power(row_size)) or groups * row_size == 1:
        grad = lax.psum(grad, ("row", "col"))
        return grad, jnp.zeros_like(grad)
    col_bits = [1 << i for i in range(groups.bit_length() - 1)]
    row_bits = [1 << i for i in range(row_size.bit_length() - 1)]
    steps = []
    if col_bits and row_bits:
        axes, sizes, a, b = ("row", "col"), (row_size, groups), row_bits.pop(0), col_bits.pop(0)

        def square(x):
            one = swap_two(x, axes, sizes, (a, 0))
            two = swap_two(x, axes, sizes, (0, b))
            both = swap_two(x, axes, sizes, (a, b))
            return x + one, two + both

        steps.append(square)
    steps += [lambda x, bit=bit: (x, swap(x, "col", groups, bit)) for bit in col_bits]
    steps += [lambda x, bit=bit: (x, swap(x, "row", row_size, bit)) for bit in row_bits]
    for step in steps[:-1]:
        a, b = step(grad)
        grad = a + b
    return steps[-1](grad)


def local(row_size, groups, halves, adj_tiles, tile_rows, tile_cols, tile_counts, features_t, weight, bias_vec, cotangent):
    weights = [weight] + [shift(weight, "rep", halves, k) for k in range(1, halves)]
    pieces, (slabs, weights) = gather_row(features_t, row_size, (split_slabs(adj_tiles[0, 0]), weights))
    slot_info = (tile_rows, tile_cols, tile_counts)
    parts = mix((groups, halves), slot_info, slabs, pieces[:-1], pieces[-1:])

    own = parts[0]
    got = shift(parts[1], "col", groups, 1) if groups > 1 else jnp.zeros_like(own)
    for k in range(2, groups):
        got = got + shift(parts[k], "col", groups, k)
    others = [shift(own[k] + got[k], "rep", halves, k) for k in range(1, halves)]
    output, *grads = node_step(own[0], got[0], others, weights, bias_vec, cotangent)
    grad = grads[0]
    for k in range(1, halves):
        grad = grad + shift(grads[k], "rep", halves, -k)
    grad_weight, grad_bias = last_step(*sum_all(grad, groups, row_size))
    return output, grad_weight, grad_bias


def solution(mesh):
    row_size, groups, halves = (mesh.shape[axis] for axis in ("row", "col", "rep"))
    in_specs = (
        P("row", "col", None, None, None),
        P("row", "col", None),
        P("row", "col", None),
        P("row", "col"),
        P("rep", ("row", "col")),
        P("rep", None),
        P(),
        P(("row", "col", "rep"), None),
    )
    out_specs = (P(("row", "col", "rep"), None), P("rep", None), P())
    return jax.shard_map(
        functools.partial(local, row_size, groups, halves),
        mesh=mesh,
        in_specs=in_specs,
        out_specs=out_specs,
        check_vma=False,
    )
```

time: 53.5 us -> 49 us (0.916)
  waiting for transfers between devices: 22.8 us -> 20 us
  local copies, waits for them, and re-layouts: 3.34 us -> 0.68 us
    ppermute x8 -> x9, starting transfers between devices: 11 us -> 15.4 us  [swap(): return lax.ppermute(x, axis, [(i, i ^ bit) for i in range(size)])]
    ppermute x7, starting transfers between devices: 9.51 us -> 5.64 us  [the longest x3 3.49 us: swap_two(): return lax.ppermute(x, axes, perm)]
    ppermute x8 -> x9, waiting for transfers between devices: 13.4 us -> 11 us  [swap(): return lax.ppermute(x, axis, [(i, i ^ bit) for i in range(size)])]
    unnamed x14 -> x13, local copies, waits for them, and re-layouts: 2.21 us -> 0.68 us
    slice x1 -> x0, local copies, waits for them, and re-layouts: 0.62 us -> none  [local(): return (output, grad[:half_width], grad[half_width])]
    pallas_call x3 -> x5, Pallas kernels: 5.23 us -> 5.72 us  [the longest x1 2.66 us: split_slabs(): call(split_kernel, (out, out), [pl.ANY], 'split_slabs', scratch, cost)]
  transfers between devices with their start and end apart: 15 -> 16, of which waited for: 11 -> 12; matrix products, arithmetic and copies ran while one was open for 0% -> 1% of each run, Pallas kernels for 2% -> 8%
where the time goes in v2:
time: 49 us; the launch traced here: 48.9 us
  starting transfers between devices  21 us (43%)
  waiting for transfers between devices  20 us (41%)
  Pallas kernels  5.72 us (12%)
  between operations  1.4 us (3%)
  local copies, waits for them, and re-layouts  0.68 us (1%)
    ppermute x9, starting transfers between devices, swap(): return lax.ppermute(x, axis, [(i, i ^ bit) for i in range(size)])  15.4 us
    ppermute x9, waiting for transfers between devices, swap(): return lax.ppermute(x, axis, [(i, i ^ bit) for i in range(size)])  11 us
    ppermute x4, waiting for transfers between devices, shift(): return lax.ppermute(x, axis, [(i, (i + k) % size) for i in range(size)])  5.47 us
    ppermute x3, waiting for transfers between devices, swap_two(): return lax.ppermute(x, axes, perm)  3.51 us
    ppermute x3, starting transfers between devices, swap_two(): return lax.ppermute(x, axes, perm)  3.49 us
    pallas_call x1, Pallas kernels, split_slabs(): call(split_kernel, (out, out), [pl.ANY], 'split_slabs', scratch, cost)  2.66 us
    ppermute x4, starting transfers between devices, shift(): return lax.ppermute(x, axis, [(i, (i + k) % size) for i in range(size)])  2.16 us
    pallas_call x1, Pallas kernels, mix(): call(functools.partial(early_kernel, sources), pltpu.VMEM((groups, half_w...  1.28 us
  transfers between devices with their start and end apart: 16, of which 12 were waited for; matrix products, arithmetic and copies ran while one was open for 1% of the time, Pallas kernels for 8%

profile of v2, /device:TPU:0, one launch (start us, length us, event | category | flops | bytes accessed | tf_op | source)
XLA Modules:
  0.0 48.9 jit_solution(15098875800853357001)
XLA Ops:
  0.6 4.1 %collective-permute-start = (f32[64,512]{1,0:T(8,128)}, f32[64,512]{1,0:T(8,128)S(1)}, u32[]{:S(2)}, u32[]{:S(2)}) collective-permute-start(f32[64,512]{1,0:T(8,128)} %refs_0_.1), channel_id=1, source_target_pairs={{0,16},{4,20},{8,24},{12,28},{16,0},{20,4},{24,8},{28,12},{1,17},{... | collective-permute-start | bytes 393224 | tf_op jit(solution)/shard_map/ppermute | solution.py:196
  4.7 1.6 %collective-permute-start.2 = (f32[64,512]{1,0:T(8,128)}, f32[64,512]{1,0:T(8,128)S(1)}, u32[]{:S(2)}, u32[]{:S(2)}) collective-permute-start(f32[64,512]{1,0:T(8,128)} %refs_0_.1), channel_id=1, source_target_pairs={{0,8},{4,12},{8,0},{12,4},{16,24},{20,28},{24,16},{28,20},{1,9},{5... | collective-permute-start | bytes 393224 | tf_op jit(solution)/shard_map/ppermute | solution.py:196
  6.3 1.5 %collective-permute-start.4 = (f32[64,512]{1,0:T(8,128)}, f32[64,512]{1,0:T(8,128)S(1)}, u32[]{:S(2)}, u32[]{:S(2)}) collective-permute-start(f32[64,512]{1,0:T(8,128)} %refs_0_.1), channel_id=1, source_target_pairs={{0,4},{4,0},{8,12},{12,8},{16,20},{20,16},{24,28},{28,24},{1,5},{5... | collective-permute-start | bytes 393224 | tf_op jit(solution)/shard_map/ppermute | solution.py:196
  7.8 2.7 %split_slabs.1 = (bf16[4,512,512]{2,1,0:T(8,128)(2,1)S(1)}, bf16[4,512,512]{2,1,0:T(8,128)(2,1)S(1)}) custom-call(f32[4,512,512]{2,1,0:T(8,128)} %bitcast.9), custom_call_target="tpu_custom_call" | custom-call | flops 4194304 | bytes 8388608 | tf_op jit(solution)/shard_map/split_slabs/pallas_call | solution.py:58
  10.5 0.9 %collective-permute-done.refs_2_ = f32[64,512]{1,0:T(8,128)S(1)} collective-permute-done((f32[64,512]{1,0:T(8,128)}, f32[64,512]{1,0:T(8,128)S(1)}, u32[]{:S(2)}, u32[]{:S(2)}) %collective-permute-start) | collective-permute-done | bytes 131104 | tf_op jit(solution)/shard_map/ppermute | solution.py:196
  11.4 0.7 %collective-permute-start.3 = (f32[64,512]{1,0:T(8,128)S(1)}, f32[64,512]{1,0:T(8,128)S(1)}, u32[]{:S(2)}, u32[]{:S(2)}) collective-permute-start(f32[64,512]{1,0:T(8,128)S(1)} %collective-permute-done.refs_2_), channel_id=1, source_target_pairs={{0,8},{4,12},{8,0},{12,4},{16,24},{20,28},{24,16},{28,20},{1,9},{5... | collective-permute-start | bytes 393224 | tf_op jit(solution)/shard_map/ppermute | solution.py:196
  12.1 1.5 %collective-permute-start.5 = (f32[64,512]{1,0:T(8,128)S(1)}, f32[64,512]{1,0:T(8,128)S(1)}, u32[]{:S(2)}, u32[]{:S(2)}) collective-permute-start(f32[64,512]{1,0:T(8,128)S(1)} %collective-permute-done.2.refs_1_), channel_id=1, source_target_pairs={{0,4},{4,0},{8,12},{12,8},{16,20},{20,16},{24,28},{28,24},{1,5},{5... | collective-permute-start | bytes 393224 | tf_op jit(solution)/shard_map/ppermute | solution.py:196
  14.1 2.4 %collective-permute-done.3.refs_3_ = f32[64,512]{1,0:T(8,128)S(1)} collective-permute-done((f32[64,512]{1,0:T(8,128)S(1)}, f32[64,512]{1,0:T(8,128)S(1)}, u32[]{:S(2)}, u32[]{:S(2)}) %collective-permute-start.3) | collective-permute-done | bytes 131104 | tf_op jit(solution)/shard_map/ppermute | solution.py:196
  16.5 1.4 %collective-permute-start.7 = (f32[64,512]{1,0:T(8,128)S(1)}, f32[64,512]{1,0:T(8,128)S(1)}, u32[]{:S(2)}, u32[]{:S(2)}) collective-permute-start(f32[64,512]{1,0:T(8,128)S(1)} %collective-permute-done.3.refs_3_), channel_id=1, source_target_pairs={{0,4},{4,0},{8,12},{12,8},{16,20},{20,16},{24,28},{28,24},{1,5},{5... | collective-permute-start | bytes 393224 | tf_op jit(solution)/shard_map/ppermute | solution.py:196
  18.5 2.8 %collective-permute-done.6.refs_6_ = f32[64,512]{1,0:T(8,128)S(1)} collective-permute-done((f32[64,512]{1,0:T(8,128)S(1)}, f32[64,512]{1,0:T(8,128)S(1)}, u32[]{:S(2)}, u32[]{:S(2)}) %collective-permute-start.6) | collective-permute-done | bytes 131104 | tf_op jit(solution)/shard_map/ppermute | solution.py:196
  21.3 1.3 %mix_early.1.early = f32[2,64,512]{2,1,0:T(8,128)S(1)} custom-call(s32[1,1,4]{2,1,0:T(1,128)S(1)} %copy-done.3, s32[1,1,4]{2,1,0:T(1,128)S(1)} %copy-done.4, s32[1,1]{1,0:T(1,128)S(6)} %copy.12.counts, bf16[4,512,512]{2,1,0:T(8,128)(2,1)S(1)} %get-tuple-element.20.high, bf16[4,512,512]{2,1,0:T(8,128)(2,1)S(1)} %get-tuple-element.21.low, ...), custom_call_target="tpu_custom_call" | custom-call | flops 402653184 | bytes 4194304 | tf_op jit(solution)/shard_map/mix_early/pallas_call | solution.py:130
  22.8 0.6 %mix_late.1 = (f32[2,64,256]{2,1,0:T(8,128)S(1)}, f32[2,64,256]{2,1,0:T(8,128)S(1)}) custom-call(s32[1,1,4]{2,1,0:T(1,128)S(1)} %copy-done.3, s32[1,1,4]{2,1,0:T(1,128)S(1)} %copy-done.4, s32[1,1]{1,0:T(1,128)S(6)} %copy.12.counts, bf16[4,512,512]{2,1,0:T(8,128)(2,1)S(1)} %get-tuple-element.20.high, bf16[4,512,512]{2,1,0:T(8,128)(2,1)S(1)} %get-tuple-element.21.low, ...), custom_call_target="tpu_custom_call" | custom-call | tf_op jit(solution)/shard_map/mix_late/pallas_call | solution.py:139
  23.5 1.9 %collective-permute-start.8 = (f32[2,64,256]{2,1,0:T(8,128)S(1)}, f32[2,64,256]{2,1,0:T(8,128)S(1)}, u32[]{:S(2)}, u32[]{:S(2)}) collective-permute-start(f32[2,64,256]{2,1,0:T(8,128)S(1)} %get-tuple-element.25), channel_id=1, source_target_pairs={{0,2},{2,0},{1,3},{3,1},{4,6},{6,4},{5,7},{7,5},{8,10},{10,8},{9,1... | collective-permute-start | bytes 393224 | tf_op jit(solution)/shard_map/ppermute | solution.py:192
  25.3 3.2 %collective-permute-done.8 = f32[2,64,256]{2,1,0:T(8,128)S(1)} collective-permute-done((f32[2,64,256]{2,1,0:T(8,128)S(1)}, f32[2,64,256]{2,1,0:T(8,128)S(1)}, u32[]{:S(2)}, u32[]{:S(2)}) %collective-permute-start.8) | collective-permute-done | bytes 131104 | tf_op jit(solution)/shard_map/ppermute | solution.py:192
  28.6 1.2 %collective-permute-done.9.refs_2_ = f32[64,256]{1,0:T(8,128)S(1)} collective-permute-done((f32[64,256]{1,0:T(8,128)S(1)}, f32[64,256]{1,0:T(8,128)S(1)}, u32[]{:S(2)}, u32[]{:S(2)}) %collective-permute-start.9) | collective-permute-done | bytes 65568 | tf_op jit(solution)/shard_map/ppermute | solution.py:192
  30.6 1.1 %collective-permute-done.10 = f32[72,128]{1,0:T(8,128)S(1)} collective-permute-done((f32[72,128]{1,0:T(8,128)S(1)}, f32[72,128]{1,0:T(8,128)S(1)}, u32[]{:S(2)}, u32[]{:S(2)}) %collective-permute-start.10) | collective-permute-done | bytes 36896 | tf_op jit(solution)/shard_map/ppermute | solution.py:192
  31.7 2.4 %collective-permute-start.13 = (f32[72,128]{1,0:T(8,128)S(1)}, f32[72,128]{1,0:T(8,128)S(1)}, u32[]{:S(2)}, u32[]{:S(2)}) collective-permute-start(f32[72,128]{1,0:T(8,128)S(1)} %add.23), channel_id=1, source_target_pairs={{0,6},{2,4},{4,2},{6,0},{8,14},{10,12},{12,10},{14,8},{16,22},{18,... | collective-permute-start | bytes 110600 | tf_op jit(solution)/shard_map/ppermute | solution.py:204
  35.2 1.4 %collective-permute-done.13 = f32[72,128]{1,0:T(8,128)S(1)} collective-permute-done((f32[72,128]{1,0:T(8,128)S(1)}, f32[72,128]{1,0:T(8,128)S(1)}, u32[]{:S(2)}, u32[]{:S(2)}) %collective-permute-start.13) | collective-permute-done | bytes 36896 | tf_op jit(solution)/shard_map/ppermute | solution.py:204
  36.6 1.5 %collective-permute-done.12 = f32[72,128]{1,0:T(8,128)S(1)} collective-permute-done((f32[72,128]{1,0:T(8,128)S(1)}, f32[72,128]{1,0:T(8,128)S(1)}, u32[]{:S(2)}, u32[]{:S(2)}) %collective-permute-start.12) | collective-permute-done | bytes 36896 | tf_op jit(solution)/shard_map/ppermute | solution.py:204
  39.2 3.5 %collective-permute-done.14 = f32[72,128]{1,0:T(8,128)S(1)} collective-permute-done((f32[72,128]{1,0:T(8,128)S(1)}, f32[72,128]{1,0:T(8,128)S(1)}, u32[]{:S(2)}, u32[]{:S(2)}) %collective-permute-start.14) | collective-permute-done | bytes 36896 | tf_op jit(solution)/shard_map/ppermute | solution.py:196
  42.7 3.6 %collective-permute-start.15 = (f32[72,128]{1,0:T(8,128)S(1)}, f32[72,128]{1,0:T(8,128)S(1)}, u32[]{:S(2)}, u32[]{:S(2)}) collective-permute-start(f32[72,128]{1,0:T(8,128)S(1)} %add.27.a), channel_id=1, source_target_pairs={{0,16},{4,20},{8,24},{12,28},{16,0},{20,4},{24,8},{28,12},{1,17},{... | collective-permute-start | bytes 110600 | tf_op jit(solution)/shard_map/ppermute | solution.py:196
  46.3 0.7 %copy.11 = f32[256,128]{1,0:T(8,128)} copy(f32[256,128]{1,0:T(8,128)S(1)} %get-tuple-element.36) | data formatting | bytes 262144
  47.0 1.3 %collective-permute-done.15.b = f32[72,128]{1,0:T(8,128)S(1)} collective-permute-done((f32[72,128]{1,0:T(8,128)S(1)}, f32[72,128]{1,0:T(8,128)S(1)}, u32[]{:S(2)}, u32[]{:S(2)}) %collective-permute-start.15) | collective-permute-done | bytes 36896 | tf_op jit(solution)/shard_map/ppermute | solution.py:196
  48.2 0.6 %last_step.1 = (f32[64,128]{1,0:T(8,128)}, f32[128]{0:T(128)}) custom-call(f32[72,128]{1,0:T(8,128)S(1)} %add.27.a, f32[72,128]{1,0:T(8,128)S(1)} %collective-permute-done.15.b), custom_call_target="tpu_custom_call" | custom-call | tf_op jit(solution)/shard_map/last_step/pallas_call | solution.py:188
  (30 shorter events, 3.8 us)
Async XLA Ops:
  0.6 10.7 %collective-permute-start = (f32[64,512]{1,0:T(8,128)}, f32[64,512]{1,0:T(8,128)S(1)}, u32[]{:S(2)}, u32[]{:S(2)}) collective-permute-start(f32[64,512]{1,0:T(8,128)} %refs_0_.1), channel_id=1, source_target_pairs={{0,16},{4,20},{8,24},{12,28},{16,0},{20,4},{24,8},{28,12},{1,17},{... | collective-permute-start | bytes 393224 | tf_op jit(solution)/shard_map/ppermute | solution.py:196
  4.7 7.3 %collective-permute-start.2 = (f32[64,512]{1,0:T(8,128)}, f32[64,512]{1,0:T(8,128)S(1)}, u32[]{:S(2)}, u32[]{:S(2)}) collective-permute-start(f32[64,512]{1,0:T(8,128)} %refs_0_.1), channel_id=1, source_target_pairs={{0,8},{4,12},{8,0},{12,4},{16,24},{20,28},{24,16},{28,20},{1,9},{5... | collective-permute-start | bytes 393224 | tf_op jit(solution)/shard_map/ppermute | solution.py:196
  6.3 5.8 %collective-permute-start.4 = (f32[64,512]{1,0:T(8,128)}, f32[64,512]{1,0:T(8,128)S(1)}, u32[]{:S(2)}, u32[]{:S(2)}) collective-permute-start(f32[64,512]{1,0:T(8,128)} %refs_0_.1), channel_id=1, source_target_pairs={{0,4},{4,0},{8,12},{12,8},{16,20},{20,16},{24,28},{28,24},{1,5},{5... | collective-permute-start | bytes 393224 | tf_op jit(solution)/shard_map/ppermute | solution.py:196
  7.8 2.7 %collective-permute-start.1 = (f32[64,128]{1,0:T(8,128)}, f32[64,128]{1,0:T(8,128)S(1)}, u32[]{:S(2)}, u32[]{:S(2)}) collective-permute-start(f32[64,128]{1,0:T(8,128)} %refs_3_), channel_id=1, source_target_pairs={{0,1},{1,0},{2,3},{3,2},{4,5},{5,4},{6,7},{7,6},{8,9},{9,8},{10,11... | collective-permute-start | bytes 98312 | tf_op jit(solution)/shard_map/ppermute | solution.py:192
  7.8 13.5 %copy-start = (f32[64,512]{1,0:T(8,128)S(1)}, f32[64,512]{1,0:T(8,128)}, u32[]{:S(2)}) copy-start(f32[64,512]{1,0:T(8,128)} %refs_0_.1) | copy-start | bytes 393220
  7.8 13.5 %copy-start.3 = (s32[1,1,4]{2,1,0:T(1,128)S(1)}, s32[1,1,4]{2,1,0:T(1,128)}, u32[]{:S(2)}) copy-start(s32[1,1,4]{2,1,0:T(1,128)} %rows.3) | copy-start | bytes 52
  7.8 13.5 %copy-start.4 = (s32[1,1,4]{2,1,0:T(1,128)S(1)}, s32[1,1,4]{2,1,0:T(1,128)}, u32[]{:S(2)}) copy-start(s32[1,1,4]{2,1,0:T(1,128)} %cols.3) | copy-start | bytes 52
  11.4 5.1 %collective-permute-start.3 = (f32[64,512]{1,0:T(8,128)S(1)}, f32[64,512]{1,0:T(8,128)S(1)}, u32[]{:S(2)}, u32[]{:S(2)}) collective-permute-start(f32[64,512]{1,0:T(8,128)S(1)} %collective-permute-done.refs_2_), channel_id=1, source_target_pairs={{0,8},{4,12},{8,0},{12,4},{16,24},{20,28},{24,16},{28,20},{1,9},{5... | collective-permute-start | bytes 393224 | tf_op jit(solution)/shard_map/ppermute | solution.py:196
  12.1 6.4 %collective-permute-start.5 = (f32[64,512]{1,0:T(8,128)S(1)}, f32[64,512]{1,0:T(8,128)S(1)}, u32[]{:S(2)}, u32[]{:S(2)}) collective-permute-start(f32[64,512]{1,0:T(8,128)S(1)} %collective-permute-done.2.refs_1_), channel_id=1, source_target_pairs={{0,4},{4,0},{8,12},{12,8},{16,20},{20,16},{24,28},{28,24},{1,5},{5... | collective-permute-start | bytes 393224 | tf_op jit(solution)/shard_map/ppermute | solution.py:196
  13.6 7.7 %collective-permute-start.6 = (f32[64,512]{1,0:T(8,128)S(1)}, f32[64,512]{1,0:T(8,128)S(1)}, u32[]{:S(2)}, u32[]{:S(2)}) collective-permute-start(f32[64,512]{1,0:T(8,128)S(1)} %collective-permute-done.refs_2_), channel_id=1, source_target_pairs={{0,4},{4,0},{8,12},{12,8},{16,20},{20,16},{24,28},{28,24},{1,5},{5... | collective-permute-start | bytes 393224 | tf_op jit(solution)/shard_map/ppermute | solution.py:196
  16.5 6.4 %collective-permute-start.7 = (f32[64,512]{1,0:T(8,128)S(1)}, f32[64,512]{1,0:T(8,128)S(1)}, u32[]{:S(2)}, u32[]{:S(2)}) collective-permute-start(f32[64,512]{1,0:T(8,128)S(1)} %collective-permute-done.3.refs_3_), channel_id=1, source_target_pairs={{0,4},{4,0},{8,12},{12,8},{16,20},{20,16},{24,28},{28,24},{1,5},{5... | collective-permute-start | bytes 393224 | tf_op jit(solution)/shard_map/ppermute | solution.py:196
  22.6 7.3 %copy-start.1 = (f32[256,128]{1,0:T(8,128)S(1)}, f32[256,128]{1,0:T(8,128)}, u32[]{:S(2)}) copy-start(f32[256,128]{1,0:T(8,128)} %refs_6_.1) | copy-start | bytes 393220
  22.6 7.3 %copy-start.2 = (f32[64,128]{1,0:T(8,128)S(1)}, f32[64,128]{1,0:T(8,128)}, u32[]{:S(2)}) copy-start(f32[64,128]{1,0:T(8,128)} %refs_3_) | copy-start | bytes 98308
  22.6 7.2 %copy-start.5 = (f32[128]{0:T(128)S(1)}, f32[128]{0:T(128)}, u32[]{:S(2)}) copy-start(f32[128]{0:T(128)} %param.14) | copy-start | bytes 1540
  23.5 5.0 %collective-permute-start.8 = (f32[2,64,256]{2,1,0:T(8,128)S(1)}, f32[2,64,256]{2,1,0:T(8,128)S(1)}, u32[]{:S(2)}, u32[]{:S(2)}) collective-permute-start(f32[2,64,256]{2,1,0:T(8,128)S(1)} %get-tuple-element.25), channel_id=1, source_target_pairs={{0,2},{2,0},{1,3},{3,1},{4,6},{6,4},{5,7},{7,5},{8,10},{10,8},{9,1... | collective-permute-start | bytes 393224 | tf_op jit(solution)/shard_map/ppermute | solution.py:192
  28.5 1.3 %collective-permute-start.9 = (f32[64,256]{1,0:T(8,128)S(1)}, f32[64,256]{1,0:T(8,128)S(1)}, u32[]{:S(2)}, u32[]{:S(2)}) collective-permute-start(f32[64,256]{1,0:T(8,128)S(1)} %get-tuple-element.33), channel_id=1, source_target_pairs={{0,1},{1,0},{2,3},{3,2},{4,5},{5,4},{6,7},{7,6},{8,9},{9,8},{10,11... | collective-permute-start | bytes 196616 | tf_op jit(solution)/shard_map/ppermute | solution.py:192
  30.4 1.3 %collective-permute-start.10 = (f32[72,128]{1,0:T(8,128)S(1)}, f32[72,128]{1,0:T(8,128)S(1)}, u32[]{:S(2)}, u32[]{:S(2)}) collective-permute-start(f32[72,128]{1,0:T(8,128)S(1)} %get-tuple-element.30), channel_id=1, source_target_pairs={{0,1},{1,0},{2,3},{3,2},{4,5},{5,4},{6,7},{7,6},{8,9},{9,8},{10,11... | collective-permute-start | bytes 110600 | tf_op jit(solution)/shard_map/ppermute | solution.py:192
  31.7 4.9 %collective-permute-start.13 = (f32[72,128]{1,0:T(8,128)S(1)}, f32[72,128]{1,0:T(8,128)S(1)}, u32[]{:S(2)}, u32[]{:S(2)}) collective-permute-start(f32[72,128]{1,0:T(8,128)S(1)} %add.23), channel_id=1, source_target_pairs={{0,6},{2,4},{4,2},{6,0},{8,14},{10,12},{12,10},{14,8},{16,22},{18,... | collective-permute-start | bytes 110600 | tf_op jit(solution)/shard_map/ppermute | solution.py:204
  34.1 4.0 %collective-permute-start.12 = (f32[72,128]{1,0:T(8,128)S(1)}, f32[72,128]{1,0:T(8,128)S(1)}, u32[]{:S(2)}, u32[]{:S(2)}) collective-permute-start(f32[72,128]{1,0:T(8,128)S(1)} %add.23), channel_id=1, source_target_pairs={{0,2},{2,0},{4,6},{6,4},{8,10},{10,8},{12,14},{14,12},{16,18},{18,... | collective-permute-start | bytes 110600 | tf_op jit(solution)/shard_map/ppermute | solution.py:204
  34.7 4.0 %collective-permute-start.11 = (f32[72,128]{1,0:T(8,128)S(1)}, f32[72,128]{1,0:T(8,128)S(1)}, u32[]{:S(2)}, u32[]{:S(2)}) collective-permute-start(f32[72,128]{1,0:T(8,128)S(1)} %add.23), channel_id=1, source_target_pairs={{0,4},{2,6},{4,0},{6,2},{8,12},{10,14},{12,8},{14,10},{16,20},{18,... | collective-permute-start | bytes 110600 | tf_op jit(solution)/shard_map/ppermute | solution.py:204
  38.7 4.0 %collective-permute-start.14 = (f32[72,128]{1,0:T(8,128)S(1)}, f32[72,128]{1,0:T(8,128)S(1)}, u32[]{:S(2)}, u32[]{:S(2)}) collective-permute-start(f32[72,128]{1,0:T(8,128)S(1)} %add_add_fusion), channel_id=1, source_target_pairs={{0,8},{4,12},{8,0},{12,4},{16,24},{20,28},{24,16},{28,20},{1,9},{5... | collective-permute-start | bytes 110600 | tf_op jit(solution)/shard_map/ppermute | solution.py:196
  42.7 5.5 %collective-permute-start.15 = (f32[72,128]{1,0:T(8,128)S(1)}, f32[72,128]{1,0:T(8,128)S(1)}, u32[]{:S(2)}, u32[]{:S(2)}) collective-permute-start(f32[72,128]{1,0:T(8,128)S(1)} %add.27.a), channel_id=1, source_target_pairs={{0,16},{4,20},{8,24},{12,28},{16,0},{20,4},{24,8},{28,12},{1,17},{... | collective-permute-start | bytes 110600 | tf_op jit(solution)/shard_map/ppermute | solution.py:196

commit v3 on v2

--- a/solution.py
+++ b/solution.py
@@ -114,10 +114,10 @@
                 total[rows[0, 0, t]] += product(picked[0], high[t], low[t])
 
     part = block_len // halves
-    for k, out in enumerate(outs):
-        for h in range(halves):
-            begin = pl.multiple_of(lax.rem(rep + h, halves) * part, part)
-            out[h] = total[lax.rem(col + k, groups), :, pl.ds(begin, part)]
+    for i, out in enumerate(outs):
+        k, h = divmod(i, halves)
+        begin = pl.multiple_of(lax.rem(rep + h, halves) * part, part)
+        out[...] = total[lax.rem(col + k, groups), :, pl.ds(begin, part)]
 
 
 def mix(sizes, slot_info, slabs, early, late):
@@ -138,20 +138,19 @@
     pieces, sources = zip(*late)
     return call(
         functools.partial(late_kernel, sizes, sources),
-        [pltpu.VMEM((halves, half_width, block_len // halves), F32)] * groups,
+        [pltpu.VMEM((half_width, block_len // halves), F32)] * (groups * halves),
         spaces + [pltpu.VMEM] * (1 + len(pieces)),
         "mix_late",
         [pltpu.VMEM(total.shape, F32), picked],
     )(*slot_info, *slabs, total, *pieces)
 
 
-def node_kernel(parts, *refs):
-    (own, got), refs = refs[:2], refs[2:]
-    others, refs = refs[: parts - 1], refs[parts - 1 :]
-    weights, refs = refs[:parts], refs[parts:]
-    bias, cotangent, output, *grads = refs
-    half_width = own.shape[0]
-    mixed = split(jnp.concatenate([own[...] + got[...]] + [other[...] for other in others]))
+def node_kernel(groups, halves, *refs):
+    terms, refs = refs[: groups * halves], refs[groups * halves :]
+    weights, (bias, cotangent, output, *grads) = refs[:halves], refs[halves:]
+    half_width = terms[0].shape[0]
+    mixed = [sum(terms[k * halves + h][...] for k in range(groups)) for h in range(halves)]
+    mixed = split(jnp.concatenate(mixed))
     weight = split(jnp.concatenate([w[...] for w in weights]))
     preact = bias[...] + dot_split(mixed, weight, ((0,), (0,)))
     squash = 1.0 / (1.0 + jnp.exp(-preact))
@@ -159,21 +158,21 @@
     slope = cotangent[...] * squash * (1.0 + preact * (1.0 - squash))
     bias_term = jnp.sum(slope, axis=0, keepdims=True)
     product = dot_split(mixed, split(slope), ((1,), (0,)))
-    for k, grad in enumerate(grads):
-        grad[:half_width] = product[k * half_width : (k + 1) * half_width]
+    for h, grad in enumerate(grads):
+        grad[:half_width] = product[h * half_width : (h + 1) * half_width]
         grad[half_width:] = jnp.broadcast_to(bias_term, (SUBLANES, bias_term.shape[1]))
 
 
-def node_step(own, got, others, weights, bias, cotangent):
-    parts = len(weights)
+def node_step(sizes, terms, weights, bias, cotangent):
+    groups, halves = sizes
     width = cotangent.shape[1]
-    grad = pltpu.VMEM((own.shape[0] + SUBLANES, width), F32)
+    grad = pltpu.VMEM((terms[0].shape[0] + SUBLANES, width), F32)
     return call(
-        functools.partial(node_kernel, parts),
-        [pltpu.VMEM(cotangent.shape, F32)] + [grad] * parts,
-        [pltpu.VMEM] * (4 + 2 * parts - 1),
+        functools.partial(node_kernel, groups, halves),
+        [pltpu.VMEM(cotangent.shape, F32)] + [grad] * halves,
+        [pltpu.VMEM] * (len(terms) + halves + 2),
         "node_step",
-    )(own, got, *others, *weights, bias.reshape(1, width), cotangent)
+    )(*terms, *weights, bias.reshape(1, width), cotangent)
 
 
 def last_kernel(a, b, grad_weight, grad_bias):
@@ -190,6 +189,14 @@
 
 def shift(x, axis, size, k):
     return lax.ppermute(x, axis, [(i, (i + k) % size) for i in range(size)])
+
+
+def shift_two(x, sizes, steps):
+    (groups, halves), (k, h) = sizes, steps
+    perm = [
+        (c * halves + r, (c + k) % groups * halves + (r + h) % halves) for c in range(groups) for r in range(halves)
+    ]
+    return lax.ppermute(x, ("col", "rep"), perm)
 
 
 def swap(x, axis, size, bit):
@@ -213,18 +220,25 @@
         pieces = [x] + [shift(x, "row", size, k) for k in range(1, size)]
         return [(p, lambda row, k=k: lax.rem(row + size - k, size)) for k, p in enumerate(pieces)], held
     found = {0: x}
+    own_cross = swap(x, "row", size, 1)
     bit = size // 2
     while bit > 1:
         for mask in list(found):
             found[mask ^ bit] = swap(found[mask], "row", size, bit)
         if bit == size // 2:
-            found[bit], held = lax.optimization_barrier((found[bit], held))
+            found[bit], own_cross, held = lax.optimization_barrier((found[bit], own_cross, held))
         bit //= 2
     order = sorted(found, key=lambda mask: (bin(mask).count("1"), mask))
-    crossed = {0: swap(x, "row", size, 1)}
-    first, _ = lax.optimization_barrier((found[order[1]], crossed[0])) if len(order) > 1 else (x, x)
+    crossed = {0: own_cross}
     for mask in order[1:]:
-        crossed[mask] = swap(first if mask == order[1] else found[mask], "row", size, 1)
+        direct = is_power(mask) and mask < size // 2
+        crossed[mask] = swap(x, "row", size, mask ^ 1) if direct else None
+    for mask in order[1:]:
+        if crossed[mask] is None:
+            passed = found[mask]
+            if mask == order[-1] and size > 4:
+                passed, _ = lax.optimization_barrier((passed, crossed[order[1]]))
+            crossed[mask] = swap(passed, "row", size, 1)
     far = [(mask ^ 1, crossed[mask]) for mask in order]
     near = [(mask, found[mask]) for mask in order]
     return [(p, lambda row, mask=mask: lax.bitwise_xor(row, mask)) for mask, p in near + far], held
@@ -248,7 +262,17 @@
 
         steps.append(square)
     steps += [lambda x, bit=bit: (x, swap(x, "col", groups, bit)) for bit in col_bits]
-    steps += [lambda x, bit=bit: (x, swap(x, "row", row_size, bit)) for bit in row_bits]
+    while row_bits:
+        (one, two), row_bits = (row_bits + [0])[:2], row_bits[2:]
+        if two:
+            steps.append(
+                lambda x, one=one, two=two: (
+                    x + swap(x, "row", row_size, one),
+                    swap(x, "row", row_size, two) + swap(x, "row", row_size, one ^ two),
+                )
+            )
+        else:
+            steps.append(lambda x, one=one: (x, swap(x, "row", row_size, one)))
     for step in steps[:-1]:
         a, b = step(grad)
         grad = a + b
@@ -261,12 +285,8 @@
     slot_info = (tile_rows, tile_cols, tile_counts)
     parts = mix((groups, halves), slot_info, slabs, pieces[:-1], pieces[-1:])
 
-    own = parts[0]
-    got = shift(parts[1], "col", groups, 1) if groups > 1 else jnp.zeros_like(own)
-    for k in range(2, groups):
-        got = got + shift(parts[k], "col", groups, k)
-    others = [shift(own[k] + got[k], "rep", halves, k) for k in range(1, halves)]
-    output, *grads = node_step(own[0], got[0], others, weights, bias_vec, cotangent)
+    terms = [shift_two(part, (groups, halves), divmod(i, halves)) if i else part for i, part in enumerate(parts)]
+    output, *grads = node_step((groups, halves), terms, weights, bias_vec, cotangent)
     grad = grads[0]
     for k in range(1, halves):
         grad = grad + shift(grads[k], "rep", halves, -k)

time: 49 us -> 47.6 us (0.971)
  starting transfers between devices: 21 us -> 20.4 us
  waiting for transfers between devices: 20 us -> 19.4 us
    ppermute x4 -> x2, waiting for transfers between devices: 5.47 us -> 1.05 us  [shift(): return lax.ppermute(x, axis, [(i, (i + k) % size) for i in range(size)])]
    ppermute x0 -> x3, waiting for transfers between devices: none -> 3.77 us  [shift_two(): return lax.ppermute(x, ('col', 'rep'), perm)]
    ppermute x0 -> x3, starting transfers between devices: none -> 1.93 us  [shift_two(): return lax.ppermute(x, ('col', 'rep'), perm)]
    ppermute x4 -> x2, starting transfers between devices: 2.16 us -> 0.24 us  [shift(): return lax.ppermute(x, axis, [(i, (i + k) % size) for i in range(size)])]
    ppermute x9 -> x10, starting transfers between devices: 15.4 us -> 14.8 us  [swap(): return lax.ppermute(x, axis, [(i, i ^ bit) for i in range(size)])]
    ppermute x9 -> x10, waiting for transfers between devices: 11 us -> 11.3 us  [swap(): return lax.ppermute(x, axis, [(i, i ^ bit) for i in range(size)])]
  transfers between devices with their start and end apart: 16 -> 18, of which waited for: 12 -> 12; matrix products, arithmetic and copies ran while one was open for 1% -> 1% of each run, Pallas kernels for 8% -> 8%
where the time goes in v3:
time: 47.6 us; the launch traced here: 47.7 us
  starting transfers between devices  20.4 us (43%)
  waiting for transfers between devices  19.4 us (41%)
  Pallas kernels  5.72 us (12%)
  between operations  1.4 us (3%)
  local copies, waits for them, and re-layouts  0.68 us (1%)
    ppermute x10, starting transfers between devices, swap(): return lax.ppermute(x, axis, [(i, i ^ bit) for i in range(size)])  14.8 us
    ppermute x10, waiting for transfers between devices, swap(): return lax.ppermute(x, axis, [(i, i ^ bit) for i in range(size)])  11.3 us
    ppermute x3, waiting for transfers between devices, shift_two(): return lax.ppermute(x, ('col', 'rep'), perm)  3.77 us
    ppermute x3, starting transfers between devices, swap_two(): return lax.ppermute(x, axes, perm)  3.49 us
    ppermute x3, waiting for transfers between devices, swap_two(): return lax.ppermute(x, axes, perm)  3.34 us
    pallas_call x1, Pallas kernels, split_slabs(): call(split_kernel, (out, out), [pl.ANY], 'split_slabs', scratch, cost)  2.66 us
    ppermute x3, starting transfers between devices, shift_two(): return lax.ppermute(x, ('col', 'rep'), perm)  1.93 us
    pallas_call x1, Pallas kernels, mix(): call(functools.partial(early_kernel, sources), pltpu.VMEM((groups, half_w...  1.28 us
  transfers between devices with their start and end apart: 18, of which 12 were waited for; matrix products, arithmetic and copies ran while one was open for 1% of the time, Pallas kernels for 8%

profile of v3, /device:TPU:0, one launch (start us, length us, event | category | flops | bytes accessed | tf_op | source)
XLA Modules:
  0.0 47.7 jit_solution(14993326077656585045)
XLA Ops:
  0.6 3.0 %collective-permute-start.1 = (f32[64,512]{1,0:T(8,128)}, f32[64,512]{1,0:T(8,128)S(1)}, u32[]{:S(2)}, u32[]{:S(2)}) collective-permute-start(f32[64,512]{1,0:T(8,128)} %refs_0_.1), channel_id=1, source_target_pairs={{0,4},{4,0},{8,12},{12,8},{16,20},{20,16},{24,28},{28,24},{1,5},{5... | collective-permute-start | bytes 393224 | tf_op jit(solution)/shard_map/ppermute | solution.py:203
  3.6 2.6 %collective-permute-start = (f32[64,512]{1,0:T(8,128)}, f32[64,512]{1,0:T(8,128)S(1)}, u32[]{:S(2)}, u32[]{:S(2)}) collective-permute-start(f32[64,512]{1,0:T(8,128)} %refs_0_.1), channel_id=1, source_target_pairs={{0,16},{4,20},{8,24},{12,28},{16,0},{20,4},{24,8},{28,12},{1,17},{... | collective-permute-start | bytes 393224 | tf_op jit(solution)/shard_map/ppermute | solution.py:203
  6.2 1.5 %collective-permute-start.5 = (f32[64,512]{1,0:T(8,128)}, f32[64,512]{1,0:T(8,128)S(1)}, u32[]{:S(2)}, u32[]{:S(2)}) collective-permute-start(f32[64,512]{1,0:T(8,128)} %refs_0_.1), channel_id=1, source_target_pairs={{0,12},{4,8},{8,4},{12,0},{16,28},{20,24},{24,20},{28,16},{1,13},{... | collective-permute-start | bytes 393224 | tf_op jit(solution)/shard_map/ppermute | solution.py:203
  7.8 2.7 %split_slabs.1 = (bf16[4,512,512]{2,1,0:T(8,128)(2,1)S(1)}, bf16[4,512,512]{2,1,0:T(8,128)(2,1)S(1)}) custom-call(f32[4,512,512]{2,1,0:T(8,128)} %bitcast.3), custom_call_target="tpu_custom_call" | custom-call | flops 4194304 | bytes 8388608 | tf_op jit(solution)/shard_map/split_slabs/pallas_call | solution.py:58
  10.5 2.2 %collective-permute-done.refs_2_ = f32[64,512]{1,0:T(8,128)S(1)} collective-permute-done((f32[64,512]{1,0:T(8,128)}, f32[64,512]{1,0:T(8,128)S(1)}, u32[]{:S(2)}, u32[]{:S(2)}) %collective-permute-start) | collective-permute-done | bytes 131104 | tf_op jit(solution)/shard_map/ppermute | solution.py:203
  12.6 0.7 %collective-permute-start.4 = (f32[64,512]{1,0:T(8,128)S(1)}, f32[64,512]{1,0:T(8,128)S(1)}, u32[]{:S(2)}, u32[]{:S(2)}) collective-permute-start(f32[64,512]{1,0:T(8,128)S(1)} %collective-permute-done.refs_2_), channel_id=1, source_target_pairs={{0,8},{4,12},{8,0},{12,4},{16,24},{20,28},{24,16},{28,20},{1,9},{5... | collective-permute-start | bytes 393224 | tf_op jit(solution)/shard_map/ppermute | solution.py:203
  13.3 1.3 %collective-permute-start.3 = (f32[64,512]{1,0:T(8,128)S(1)}, f32[64,512]{1,0:T(8,128)S(1)}, u32[]{:S(2)}, u32[]{:S(2)}) collective-permute-start(f32[64,512]{1,0:T(8,128)S(1)} %copy-done), channel_id=1, source_target_pairs={{0,8},{4,12},{8,0},{12,4},{16,24},{20,28},{24,16},{28,20},{1,9},{5... | collective-permute-start | bytes 393224 | tf_op jit(solution)/shard_map/ppermute | solution.py:203
  15.2 3.3 %collective-permute-done.4.refs_3_ = f32[64,512]{1,0:T(8,128)S(1)} collective-permute-done((f32[64,512]{1,0:T(8,128)S(1)}, f32[64,512]{1,0:T(8,128)S(1)}, u32[]{:S(2)}, u32[]{:S(2)}) %collective-permute-start.4) | collective-permute-done | bytes 131104 | tf_op jit(solution)/shard_map/ppermute | solution.py:203
  18.5 1.1 %collective-permute-start.7 = (f32[64,512]{1,0:T(8,128)S(1)}, f32[64,512]{1,0:T(8,128)S(1)}, u32[]{:S(2)}, u32[]{:S(2)}) collective-permute-start(f32[64,512]{1,0:T(8,128)S(1)} %collective-permute-done.4.refs_3_), channel_id=1, source_target_pairs={{0,4},{4,0},{8,12},{12,8},{16,20},{20,16},{24,28},{28,24},{1,5},{5... | collective-permute-start | bytes 393224 | tf_op jit(solution)/shard_map/ppermute | solution.py:203
  20.9 1.3 %mix_early.1.early = f32[2,64,512]{2,1,0:T(8,128)S(1)} custom-call(s32[1,1,4]{2,1,0:T(1,128)S(1)} %copy-done.3, s32[1,1,4]{2,1,0:T(1,128)S(1)} %copy-done.4, s32[1,1]{1,0:T(1,128)S(6)} %copy.12.counts, bf16[4,512,512]{2,1,0:T(8,128)(2,1)S(1)} %get-tuple-element.23.high, bf16[4,512,512]{2,1,0:T(8,128)(2,1)S(1)} %get-tuple-element.24.low, ...), custom_call_target="tpu_custom_call" | custom-call | flops 402653184 | bytes 4194304 | tf_op jit(solution)/shard_map/mix_early/pallas_call | solution.py:130
  22.2 1.3 %collective-permute-done.7.refs_0_ = f32[64,512]{1,0:T(8,128)S(1)} collective-permute-done((f32[64,512]{1,0:T(8,128)S(1)}, f32[64,512]{1,0:T(8,128)S(1)}, u32[]{:S(2)}, u32[]{:S(2)}) %collective-permute-start.7) | collective-permute-done | bytes 131104 | tf_op jit(solution)/shard_map/ppermute | solution.py:203
  24.2 1.6 %collective-permute-start.9 = (f32[64,256]{1,0:T(8,128)S(1)}, f32[64,256]{1,0:T(8,128)S(1)}, u32[]{:S(2)}, u32[]{:S(2)}) collective-permute-start(f32[64,256]{1,0:T(8,128)S(1)} %get-tuple-element.30), channel_id=1, source_target_pairs={{0,2},{1,3},{2,0},{3,1},{4,6},{5,7},{6,4},{7,5},{8,10},{9,11},{10,... | collective-permute-start | bytes 196616 | tf_op jit(solution)/shard_map/ppermute | solution.py:199
  26.0 2.6 %collective-permute-done.9.refs_2_ = f32[64,256]{1,0:T(8,128)S(1)} collective-permute-done((f32[64,256]{1,0:T(8,128)S(1)}, f32[64,256]{1,0:T(8,128)S(1)}, u32[]{:S(2)}, u32[]{:S(2)}) %collective-permute-start.9) | collective-permute-done | bytes 65568 | tf_op jit(solution)/shard_map/ppermute | solution.py:199
  28.7 1.1 %collective-permute-done.10.refs_3_ = f32[64,256]{1,0:T(8,128)S(1)} collective-permute-done((f32[64,256]{1,0:T(8,128)S(1)}, f32[64,256]{1,0:T(8,128)S(1)}, u32[]{:S(2)}, u32[]{:S(2)}) %collective-permute-start.10) | collective-permute-done | bytes 65568 | tf_op jit(solution)/shard_map/ppermute | solution.py:199
  30.6 1.0 %collective-permute-done.11 = f32[72,128]{1,0:T(8,128)S(1)} collective-permute-done((f32[72,128]{1,0:T(8,128)S(1)}, f32[72,128]{1,0:T(8,128)S(1)}, u32[]{:S(2)}, u32[]{:S(2)}) %collective-permute-start.11) | collective-permute-done | bytes 36896 | tf_op jit(solution)/shard_map/ppermute | solution.py:191
  31.6 2.2 %collective-permute-start.14 = (f32[72,128]{1,0:T(8,128)S(1)}, f32[72,128]{1,0:T(8,128)S(1)}, u32[]{:S(2)}, u32[]{:S(2)}) collective-permute-start(f32[72,128]{1,0:T(8,128)S(1)} %add.18), channel_id=1, source_target_pairs={{0,6},{2,4},{4,2},{6,0},{8,14},{10,12},{12,10},{14,8},{16,22},{18,... | collective-permute-start | bytes 110600 | tf_op jit(solution)/shard_map/ppermute | solution.py:211
  33.8 0.7 %collective-permute-start.13 = (f32[72,128]{1,0:T(8,128)S(1)}, f32[72,128]{1,0:T(8,128)S(1)}, u32[]{:S(2)}, u32[]{:S(2)}) collective-permute-start(f32[72,128]{1,0:T(8,128)S(1)} %add.18), channel_id=1, source_target_pairs={{0,2},{2,0},{4,6},{6,4},{8,10},{10,8},{12,14},{14,12},{16,18},{18,... | collective-permute-start | bytes 110600 | tf_op jit(solution)/shard_map/ppermute | solution.py:211
  35.1 1.4 %collective-permute-done.14 = f32[72,128]{1,0:T(8,128)S(1)} collective-permute-done((f32[72,128]{1,0:T(8,128)S(1)}, f32[72,128]{1,0:T(8,128)S(1)}, u32[]{:S(2)}, u32[]{:S(2)}) %collective-permute-start.14) | collective-permute-done | bytes 36896 | tf_op jit(solution)/shard_map/ppermute | solution.py:211
  36.5 1.3 %collective-permute-done.13 = f32[72,128]{1,0:T(8,128)S(1)} collective-permute-done((f32[72,128]{1,0:T(8,128)S(1)}, f32[72,128]{1,0:T(8,128)S(1)}, u32[]{:S(2)}, u32[]{:S(2)}) %collective-permute-start.13) | collective-permute-done | bytes 36896 | tf_op jit(solution)/shard_map/ppermute | solution.py:211
  37.8 0.7 %collective-permute-done.12 = f32[72,128]{1,0:T(8,128)S(1)} collective-permute-done((f32[72,128]{1,0:T(8,128)S(1)}, f32[72,128]{1,0:T(8,128)S(1)}, u32[]{:S(2)}, u32[]{:S(2)}) %collective-permute-start.12) | collective-permute-done | bytes 36896 | tf_op jit(solution)/shard_map/ppermute | solution.py:211
  38.5 1.0 %collective-permute-start.15 = (f32[72,128]{1,0:T(8,128)S(1)}, f32[72,128]{1,0:T(8,128)S(1)}, u32[]{:S(2)}, u32[]{:S(2)}) collective-permute-start(f32[72,128]{1,0:T(8,128)S(1)} %add_add_fusion), channel_id=1, source_target_pairs={{0,8},{4,12},{8,0},{12,4},{16,24},{20,28},{24,16},{28,20},{1,9},{5... | collective-permute-start | bytes 110600 | tf_op jit(solution)/shard_map/ppermute | solution.py:203
  39.5 2.7 %collective-permute-start.17 = (f32[72,128]{1,0:T(8,128)S(1)}, f32[72,128]{1,0:T(8,128)S(1)}, u32[]{:S(2)}, u32[]{:S(2)}) collective-permute-start(f32[72,128]{1,0:T(8,128)S(1)} %add_add_fusion), channel_id=1, source_target_pairs={{0,24},{4,28},{8,16},{12,20},{16,8},{20,12},{24,0},{28,4},{1,25},{... | collective-permute-start | bytes 110600 | tf_op jit(solution)/shard_map/ppermute | solution.py:203
  43.2 2.2 %collective-permute-done.17 = f32[72,128]{1,0:T(8,128)S(1)} collective-permute-done((f32[72,128]{1,0:T(8,128)S(1)}, f32[72,128]{1,0:T(8,128)S(1)}, u32[]{:S(2)}, u32[]{:S(2)}) %collective-permute-start.17) | collective-permute-done | bytes 36896 | tf_op jit(solution)/shard_map/ppermute | solution.py:203
  45.3 1.7 %collective-permute-done.16 = f32[72,128]{1,0:T(8,128)S(1)} collective-permute-done((f32[72,128]{1,0:T(8,128)S(1)}, f32[72,128]{1,0:T(8,128)S(1)}, u32[]{:S(2)}, u32[]{:S(2)}) %collective-permute-start.16) | collective-permute-done | bytes 36896 | tf_op jit(solution)/shard_map/ppermute | solution.py:203
  (34 shorter events, 5.2 us)
Async XLA Ops:
  0.6 9.8 %collective-permute-start.1 = (f32[64,512]{1,0:T(8,128)}, f32[64,512]{1,0:T(8,128)S(1)}, u32[]{:S(2)}, u32[]{:S(2)}) collective-permute-start(f32[64,512]{1,0:T(8,128)} %refs_0_.1), channel_id=1, source_target_pairs={{0,4},{4,0},{8,12},{12,8},{16,20},{20,16},{24,28},{28,24},{1,5},{5... | collective-permute-start | bytes 393224 | tf_op jit(solution)/shard_map/ppermute | solution.py:203
  3.6 9.0 %collective-permute-start = (f32[64,512]{1,0:T(8,128)}, f32[64,512]{1,0:T(8,128)S(1)}, u32[]{:S(2)}, u32[]{:S(2)}) collective-permute-start(f32[64,512]{1,0:T(8,128)} %refs_0_.1), channel_id=1, source_target_pairs={{0,16},{4,20},{8,24},{12,28},{16,0},{20,4},{24,8},{28,12},{1,17},{... | collective-permute-start | bytes 393224 | tf_op jit(solution)/shard_map/ppermute | solution.py:203
  6.2 4.2 %collective-permute-start.2 = (f32[64,128]{1,0:T(8,128)}, f32[64,128]{1,0:T(8,128)S(1)}, u32[]{:S(2)}, u32[]{:S(2)}) collective-permute-start(f32[64,128]{1,0:T(8,128)} %refs_4_), channel_id=1, source_target_pairs={{0,1},{1,0},{2,3},{3,2},{4,5},{5,4},{6,7},{7,6},{8,9},{9,8},{10,11... | collective-permute-start | bytes 98312 | tf_op jit(solution)/shard_map/ppermute | solution.py:191
  6.2 8.9 %collective-permute-start.5 = (f32[64,512]{1,0:T(8,128)}, f32[64,512]{1,0:T(8,128)S(1)}, u32[]{:S(2)}, u32[]{:S(2)}) collective-permute-start(f32[64,512]{1,0:T(8,128)} %refs_0_.1), channel_id=1, source_target_pairs={{0,12},{4,8},{8,4},{12,0},{16,28},{20,24},{24,20},{28,16},{1,13},{... | collective-permute-start | bytes 393224 | tf_op jit(solution)/shard_map/ppermute | solution.py:203
  7.8 5.6 %copy-start = (f32[64,512]{1,0:T(8,128)S(1)}, f32[64,512]{1,0:T(8,128)}, u32[]{:S(2)}) copy-start(f32[64,512]{1,0:T(8,128)} %refs_0_.1) | copy-start | bytes 393220
  7.8 13.1 %copy-start.3 = (s32[1,1,4]{2,1,0:T(1,128)S(1)}, s32[1,1,4]{2,1,0:T(1,128)}, u32[]{:S(2)}) copy-start(s32[1,1,4]{2,1,0:T(1,128)} %rows.3) | copy-start | bytes 52
  7.8 13.1 %copy-start.4 = (s32[1,1,4]{2,1,0:T(1,128)S(1)}, s32[1,1,4]{2,1,0:T(1,128)}, u32[]{:S(2)}) copy-start(s32[1,1,4]{2,1,0:T(1,128)} %cols.3) | copy-start | bytes 52
  12.6 5.8 %collective-permute-start.4 = (f32[64,512]{1,0:T(8,128)S(1)}, f32[64,512]{1,0:T(8,128)S(1)}, u32[]{:S(2)}, u32[]{:S(2)}) collective-permute-start(f32[64,512]{1,0:T(8,128)S(1)} %collective-permute-done.refs_2_), channel_id=1, source_target_pairs={{0,8},{4,12},{8,0},{12,4},{16,24},{20,28},{24,16},{28,20},{1,9},{5... | collective-permute-start | bytes 393224 | tf_op jit(solution)/shard_map/ppermute | solution.py:203
  13.3 6.9 %collective-permute-start.3 = (f32[64,512]{1,0:T(8,128)S(1)}, f32[64,512]{1,0:T(8,128)S(1)}, u32[]{:S(2)}, u32[]{:S(2)}) collective-permute-start(f32[64,512]{1,0:T(8,128)S(1)} %copy-done), channel_id=1, source_target_pairs={{0,8},{4,12},{8,0},{12,4},{16,24},{20,28},{24,16},{28,20},{1,9},{5... | collective-permute-start | bytes 393224 | tf_op jit(solution)/shard_map/ppermute | solution.py:203
  14.7 6.2 %collective-permute-start.6 = (f32[64,512]{1,0:T(8,128)S(1)}, f32[64,512]{1,0:T(8,128)S(1)}, u32[]{:S(2)}, u32[]{:S(2)}) collective-permute-start(f32[64,512]{1,0:T(8,128)S(1)} %collective-permute-done.refs_2_), channel_id=1, source_target_pairs={{0,4},{4,0},{8,12},{12,8},{16,20},{20,16},{24,28},{28,24},{1,5},{5... | collective-permute-start | bytes 393224 | tf_op jit(solution)/shard_map/ppermute | solution.py:203
  18.5 5.0 %collective-permute-start.7 = (f32[64,512]{1,0:T(8,128)S(1)}, f32[64,512]{1,0:T(8,128)S(1)}, u32[]{:S(2)}, u32[]{:S(2)}) collective-permute-start(f32[64,512]{1,0:T(8,128)S(1)} %collective-permute-done.4.refs_3_), channel_id=1, source_target_pairs={{0,4},{4,0},{8,12},{12,8},{16,20},{20,16},{24,28},{28,24},{1,5},{5... | collective-permute-start | bytes 393224 | tf_op jit(solution)/shard_map/ppermute | solution.py:203
  22.1 7.7 %copy-start.1 = (f32[256,128]{1,0:T(8,128)S(1)}, f32[256,128]{1,0:T(8,128)}, u32[]{:S(2)}) copy-start(f32[256,128]{1,0:T(8,128)} %refs_7_.1) | copy-start | bytes 393220
  22.1 7.6 %copy-start.2 = (f32[64,128]{1,0:T(8,128)S(1)}, f32[64,128]{1,0:T(8,128)}, u32[]{:S(2)}) copy-start(f32[64,128]{1,0:T(8,128)} %refs_4_) | copy-start | bytes 98308
  22.2 7.6 %copy-start.5 = (f32[128]{0:T(128)S(1)}, f32[128]{0:T(128)}, u32[]{:S(2)}) copy-start(f32[128]{0:T(128)} %param.14) | copy-start | bytes 1540
  24.1 1.9 %collective-permute-start.8 = (f32[64,256]{1,0:T(8,128)S(1)}, f32[64,256]{1,0:T(8,128)S(1)}, u32[]{:S(2)}, u32[]{:S(2)}) collective-permute-start(f32[64,256]{1,0:T(8,128)S(1)} %get-tuple-element.29), channel_id=1, source_target_pairs={{0,1},{1,0},{2,3},{3,2},{4,5},{5,4},{6,7},{7,6},{8,9},{9,8},{10,11... | collective-permute-start | bytes 196616 | tf_op jit(solution)/shard_map/ppermute | solution.py:199
  24.2 4.5 %collective-permute-start.9 = (f32[64,256]{1,0:T(8,128)S(1)}, f32[64,256]{1,0:T(8,128)S(1)}, u32[]{:S(2)}, u32[]{:S(2)}) collective-permute-start(f32[64,256]{1,0:T(8,128)S(1)} %get-tuple-element.30), channel_id=1, source_target_pairs={{0,2},{1,3},{2,0},{3,1},{4,6},{5,7},{6,4},{7,5},{8,10},{9,11},{10,... | collective-permute-start | bytes 196616 | tf_op jit(solution)/shard_map/ppermute | solution.py:199
  25.7 4.0 %collective-permute-start.10 = (f32[64,256]{1,0:T(8,128)S(1)}, f32[64,256]{1,0:T(8,128)S(1)}, u32[]{:S(2)}, u32[]{:S(2)}) collective-permute-start(f32[64,256]{1,0:T(8,128)S(1)} %get-tuple-element.31), channel_id=1, source_target_pairs={{0,3},{1,2},{2,1},{3,0},{4,7},{5,6},{6,5},{7,4},{8,11},{9,10},{10,... | collective-permute-start | bytes 196616 | tf_op jit(solution)/shard_map/ppermute | solution.py:199
  30.3 1.3 %collective-permute-start.11 = (f32[72,128]{1,0:T(8,128)S(1)}, f32[72,128]{1,0:T(8,128)S(1)}, u32[]{:S(2)}, u32[]{:S(2)}) collective-permute-start(f32[72,128]{1,0:T(8,128)S(1)} %get-tuple-element.36), channel_id=1, source_target_pairs={{0,1},{1,0},{2,3},{3,2},{4,5},{5,4},{6,7},{7,6},{8,9},{9,8},{10,11... | collective-permute-start | bytes 110600 | tf_op jit(solution)/shard_map/ppermute | solution.py:191
  31.6 4.9 %collective-permute-start.14 = (f32[72,128]{1,0:T(8,128)S(1)}, f32[72,128]{1,0:T(8,128)S(1)}, u32[]{:S(2)}, u32[]{:S(2)}) collective-permute-start(f32[72,128]{1,0:T(8,128)S(1)} %add.18), channel_id=1, source_target_pairs={{0,6},{2,4},{4,2},{6,0},{8,14},{10,12},{12,10},{14,8},{16,22},{18,... | collective-permute-start | bytes 110600 | tf_op jit(solution)/shard_map/ppermute | solution.py:211
  33.8 4.0 %collective-permute-start.13 = (f32[72,128]{1,0:T(8,128)S(1)}, f32[72,128]{1,0:T(8,128)S(1)}, u32[]{:S(2)}, u32[]{:S(2)}) collective-permute-start(f32[72,128]{1,0:T(8,128)S(1)} %add.18), channel_id=1, source_target_pairs={{0,2},{2,0},{4,6},{6,4},{8,10},{10,8},{12,14},{14,12},{16,18},{18,... | collective-permute-start | bytes 110600 | tf_op jit(solution)/shard_map/ppermute | solution.py:211
  34.5 4.0 %collective-permute-start.12 = (f32[72,128]{1,0:T(8,128)S(1)}, f32[72,128]{1,0:T(8,128)S(1)}, u32[]{:S(2)}, u32[]{:S(2)}) collective-permute-start(f32[72,128]{1,0:T(8,128)S(1)} %add.18), channel_id=1, source_target_pairs={{0,4},{2,6},{4,0},{6,2},{8,12},{10,14},{12,8},{14,10},{16,20},{18,... | collective-permute-start | bytes 110600 | tf_op jit(solution)/shard_map/ppermute | solution.py:211
  38.5 4.7 %collective-permute-start.15 = (f32[72,128]{1,0:T(8,128)S(1)}, f32[72,128]{1,0:T(8,128)S(1)}, u32[]{:S(2)}, u32[]{:S(2)}) collective-permute-start(f32[72,128]{1,0:T(8,128)S(1)} %add_add_fusion), channel_id=1, source_target_pairs={{0,8},{4,12},{8,0},{12,4},{16,24},{20,28},{24,16},{28,20},{1,9},{5... | collective-permute-start | bytes 110600 | tf_op jit(solution)/shard_map/ppermute | solution.py:203
  39.5 5.9 %collective-permute-start.17 = (f32[72,128]{1,0:T(8,128)S(1)}, f32[72,128]{1,0:T(8,128)S(1)}, u32[]{:S(2)}, u32[]{:S(2)}) collective-permute-start(f32[72,128]{1,0:T(8,128)S(1)} %add_add_fusion), channel_id=1, source_target_pairs={{0,24},{4,28},{8,16},{12,20},{16,8},{20,12},{24,0},{28,4},{1,25},{... | collective-permute-start | bytes 110600 | tf_op jit(solution)/shard_map/ppermute | solution.py:203
  42.2 4.9 %collective-permute-start.16 = (f32[72,128]{1,0:T(8,128)S(1)}, f32[72,128]{1,0:T(8,128)S(1)}, u32[]{:S(2)}, u32[]{:S(2)}) collective-permute-start(f32[72,128]{1,0:T(8,128)S(1)} %add_add_fusion), channel_id=1, source_target_pairs={{0,16},{4,20},{8,24},{12,28},{16,0},{20,4},{24,8},{28,12},{1,17},{... | collective-permute-start | bytes 110600 | tf_op jit(solution)/shard_map/ppermute | solution.py:203

commit v4 on v3

--- a/solution.py
+++ b/solution.py
@@ -219,26 +219,31 @@
     if not is_power(size) or size < 2:
         pieces = [x] + [shift(x, "row", size, k) for k in range(1, size)]
         return [(p, lambda row, k=k: lax.rem(row + size - k, size)) for k, p in enumerate(pieces)], held
+    bits = [1 << i for i in range(1, size.bit_length() - 1)]
+    basis = [size - 2] + bits[-2::-1] if bits else []
+    own_cross = swap(x, "row", size, 1)
     found = {0: x}
-    own_cross = swap(x, "row", size, 1)
-    bit = size // 2
-    while bit > 1:
-        for mask in list(found):
-            found[mask ^ bit] = swap(found[mask], "row", size, bit)
-        if bit == size // 2:
-            found[bit], own_cross, held = lax.optimization_barrier((found[bit], own_cross, held))
-        bit //= 2
-    order = sorted(found, key=lambda mask: (bin(mask).count("1"), mask))
+    for step, mask in enumerate(basis):
+        new = {}
+        for other, block in found.items():
+            new[other ^ mask] = swap(block, "row", size, mask)
+        if step == 0:
+            near = swap(x, "row", size, basis[-1]) if len(basis) > 1 else x
+            new[mask], own_cross, held = lax.optimization_barrier((new[mask], own_cross, held))
+        elif step == len(basis) - 1:
+            new[mask] = near
+        found.update(new)
     crossed = {0: own_cross}
-    for mask in order[1:]:
-        direct = is_power(mask) and mask < size // 2
-        crossed[mask] = swap(x, "row", size, mask ^ 1) if direct else None
-    for mask in order[1:]:
-        if crossed[mask] is None:
-            passed = found[mask]
-            if mask == order[-1] and size > 4:
-                passed, _ = lax.optimization_barrier((passed, crossed[order[1]]))
-            crossed[mask] = swap(passed, "row", size, 1)
+    if len(basis) > 1:
+        crossed[basis[-1]] = swap(x, "row", size, basis[-1] ^ 1)
+    last = None
+    for mask, block in found.items():
+        if mask not in crossed:
+            if mask not in basis and last is None:
+                last = mask
+                block, _ = lax.optimization_barrier((block, crossed[basis[-1]]))
+            crossed[mask] = swap(block, "row", size, 1)
+    order = sorted(found, key=lambda mask: (mask == last, mask not in basis and mask != 0, mask))
     far = [(mask ^ 1, crossed[mask]) for mask in order]
     near = [(mask, found[mask]) for mask in order]
     return [(p, lambda row, mask=mask: lax.bitwise_xor(row, mask)) for mask, p in near + far], held
@@ -285,7 +290,9 @@
     slot_info = (tile_rows, tile_cols, tile_counts)
     parts = mix((groups, halves), slot_info, slabs, pieces[:-1], pieces[-1:])
 
-    terms = [shift_two(part, (groups, halves), divmod(i, halves)) if i else part for i, part in enumerate(parts)]
+    terms = [None] * len(parts)
+    for i in sorted(range(len(parts)), key=lambda i: -i):
+        terms[i] = shift_two(parts[i], (groups, halves), divmod(i, halves)) if i else parts[i]
     output, *grads = node_step((groups, halves), terms, weights, bias_vec, cotangent)
     grad = grads[0]
     for k in range(1, halves):

time: 47.6 us -> 46.2 us (0.971)
  starting transfers between devices: 20.4 us -> 18.1 us
  Pallas kernels: 5.72 us -> 6.61 us
    ppermute x10, starting transfers between devices: 14.8 us -> 12.5 us  [swap(): return lax.ppermute(x, axis, [(i, i ^ bit) for i in range(size)])]
    ppermute x3, waiting for transfers between devices: 3.34 us -> 1.99 us  [swap_two(): return lax.ppermute(x, axes, perm)]
    ppermute x10, waiting for transfers between devices: 11.3 us -> 12.4 us  [swap(): return lax.ppermute(x, axis, [(i, i ^ bit) for i in range(size)])]
    pallas_call x1, Pallas kernels: 1.28 us -> 1.87 us  [mix(): call(functools.partial(early_kernel, sources), pltpu.VMEM((groups, half_w...]
  transfers between devices with their start and end apart: 18 -> 18, of which waited for: 12 -> 14; matrix products, arithmetic and copies ran while one was open for 1% -> 1% of each run, Pallas kernels for 8% -> 10%
where the time goes in v4:
time: 46.2 us; the launch traced here: 46.1 us
  waiting for transfers between devices  19.2 us (42%)
  starting transfers between devices  18.1 us (39%)
  Pallas kernels  6.61 us (14%)
  between operations  1.41 us (3%)
  local copies, waits for them, and re-layouts  0.69 us (1%)
    ppermute x10, starting transfers between devices, swap(): return lax.ppermute(x, axis, [(i, i ^ bit) for i in range(size)])  12.5 us
    ppermute x10, waiting for transfers between devices, swap(): return lax.ppermute(x, axis, [(i, i ^ bit) for i in range(size)])  12.4 us
    ppermute x3, waiting for transfers between devices, shift_two(): return lax.ppermute(x, ('col', 'rep'), perm)  3.78 us
    ppermute x3, starting transfers between devices, swap_two(): return lax.ppermute(x, axes, perm)  3.49 us
    pallas_call x1, Pallas kernels, split_slabs(): call(split_kernel, (out, out), [pl.ANY], 'split_slabs', scratch, cost)  2.66 us
    ppermute x3, waiting for transfers between devices, swap_two(): return lax.ppermute(x, axes, perm)  1.99 us
    ppermute x3, starting transfers between devices, shift_two(): return lax.ppermute(x, ('col', 'rep'), perm)  1.93 us
    pallas_call x1, Pallas kernels, mix(): call(functools.partial(early_kernel, sources), pltpu.VMEM((groups, half_w...  1.87 us
  transfers between devices with their start and end apart: 18, of which 14 were waited for; matrix products, arithmetic and copies ran while one was open for 1% of the time, Pallas kernels for 10%

profile of v4, /device:TPU:0, one launch (start us, length us, event | category | flops | bytes accessed | tf_op | source)
XLA Modules:
  0.0 46.1 jit_solution(14660408812802923692)
XLA Ops:
  0.6 3.0 %collective-permute-start.1 = (f32[64,512]{1,0:T(8,128)}, f32[64,512]{1,0:T(8,128)S(1)}, u32[]{:S(2)}, u32[]{:S(2)}) collective-permute-start(f32[64,512]{1,0:T(8,128)} %refs_0_.1), channel_id=1, source_target_pairs={{0,4},{4,0},{8,12},{12,8},{16,20},{20,16},{24,28},{28,24},{1,5},{5... | collective-permute-start | bytes 393224 | tf_op jit(solution)/shard_map/ppermute | solution.py:203
  3.6 3.6 %collective-permute-start = (f32[64,512]{1,0:T(8,128)}, f32[64,512]{1,0:T(8,128)S(1)}, u32[]{:S(2)}, u32[]{:S(2)}) collective-permute-start(f32[64,512]{1,0:T(8,128)} %refs_0_.1), channel_id=1, source_target_pairs={{0,24},{4,28},{8,16},{12,20},{16,8},{20,12},{24,0},{28,4},{1,25},{... | collective-permute-start | bytes 393224 | tf_op jit(solution)/shard_map/ppermute | solution.py:203
  7.3 2.7 %split_slabs.1 = (bf16[4,512,512]{2,1,0:T(8,128)(2,1)S(1)}, bf16[4,512,512]{2,1,0:T(8,128)(2,1)S(1)}) custom-call(f32[4,512,512]{2,1,0:T(8,128)} %bitcast.3), custom_call_target="tpu_custom_call" | custom-call | flops 4194304 | bytes 8388608 | tf_op jit(solution)/shard_map/split_slabs/pallas_call | solution.py:58
  10.0 2.1 %collective-permute-done.refs_2_ = f32[64,512]{1,0:T(8,128)S(1)} collective-permute-done((f32[64,512]{1,0:T(8,128)}, f32[64,512]{1,0:T(8,128)S(1)}, u32[]{:S(2)}, u32[]{:S(2)}) %collective-permute-start) | collective-permute-done | bytes 131104 | tf_op jit(solution)/shard_map/ppermute | solution.py:203
  12.1 1.1 %collective-permute-start.4 = (f32[64,512]{1,0:T(8,128)S(1)}, f32[64,512]{1,0:T(8,128)S(1)}, u32[]{:S(2)}, u32[]{:S(2)}) collective-permute-start(f32[64,512]{1,0:T(8,128)S(1)} %collective-permute-done.refs_2_), channel_id=1, source_target_pairs={{0,8},{4,12},{8,0},{12,4},{16,24},{20,28},{24,16},{28,20},{1,9},{5... | collective-permute-start | bytes 393224 | tf_op jit(solution)/shard_map/ppermute | solution.py:203
  13.2 0.9 %collective-permute-start.3 = (f32[64,512]{1,0:T(8,128)S(1)}, f32[64,512]{1,0:T(8,128)S(1)}, u32[]{:S(2)}, u32[]{:S(2)}) collective-permute-start(f32[64,512]{1,0:T(8,128)S(1)} %copy-done), channel_id=1, source_target_pairs={{0,8},{4,12},{8,0},{12,4},{16,24},{20,28},{24,16},{28,20},{1,9},{5... | collective-permute-start | bytes 393224 | tf_op jit(solution)/shard_map/ppermute | solution.py:203
  14.4 3.9 %collective-permute-done.4.refs_3_ = f32[64,512]{1,0:T(8,128)S(1)} collective-permute-done((f32[64,512]{1,0:T(8,128)S(1)}, f32[64,512]{1,0:T(8,128)S(1)}, u32[]{:S(2)}, u32[]{:S(2)}) %collective-permute-start.4) | collective-permute-done | bytes 131104 | tf_op jit(solution)/shard_map/ppermute | solution.py:203
  19.0 0.7 %collective-permute-done.3.refs_1_ = f32[64,512]{1,0:T(8,128)S(1)} collective-permute-done((f32[64,512]{1,0:T(8,128)S(1)}, f32[64,512]{1,0:T(8,128)S(1)}, u32[]{:S(2)}, u32[]{:S(2)}) %collective-permute-start.3) | collective-permute-done | bytes 131104 | tf_op jit(solution)/shard_map/ppermute | solution.py:203
  20.2 1.9 %mix_early.1.early = f32[2,64,512]{2,1,0:T(8,128)S(1)} custom-call(s32[1,1,4]{2,1,0:T(1,128)S(1)} %copy-done.3, s32[1,1,4]{2,1,0:T(1,128)S(1)} %copy-done.4, s32[1,1]{1,0:T(1,128)S(6)} %copy.12.counts, bf16[4,512,512]{2,1,0:T(8,128)(2,1)S(1)} %get-tuple-element.23.high, bf16[4,512,512]{2,1,0:T(8,128)(2,1)S(1)} %get-tuple-element.24.low, ...), custom_call_target="tpu_custom_call" | custom-call | flops 402653184 | bytes 4194304 | tf_op jit(solution)/shard_map/mix_early/pallas_call | solution.py:130
  22.1 1.2 %collective-permute-done.7.refs_0_ = f32[64,512]{1,0:T(8,128)S(1)} collective-permute-done((f32[64,512]{1,0:T(8,128)S(1)}, f32[64,512]{1,0:T(8,128)S(1)}, u32[]{:S(2)}, u32[]{:S(2)}) %collective-permute-start.7) | collective-permute-done | bytes 131104 | tf_op jit(solution)/shard_map/ppermute | solution.py:203
  23.3 0.9 %mix_late.1 = (f32[64,256]{1,0:T(8,128)S(1)}, f32[64,256]{1,0:T(8,128)S(1)}, f32[64,256]{1,0:T(8,128)S(1)}, f32[64,256]{1,0:T(8,128)S(1)}) custom-call(s32[1,1,4]{2,1,0:T(1,128)S(1)} %copy-done.3, s32[1,1,4]{2,1,0:T(1,128)S(1)} %copy-done.4, s32[1,1]{1,0:T(1,128)S(6)} %copy.12.counts, bf16[4,512,512]{2,1,0:T(8,128)(2,1)S(1)} %get-tuple-element.23.high, ...), custom_call_target="tpu_custom_call" | custom-call | tf_op jit(solution)/shard_map/mix_late/pallas_call | solution.py:139
  24.3 1.3 %collective-permute-start.9 = (f32[64,256]{1,0:T(8,128)S(1)}, f32[64,256]{1,0:T(8,128)S(1)}, u32[]{:S(2)}, u32[]{:S(2)}) collective-permute-start(f32[64,256]{1,0:T(8,128)S(1)} %get-tuple-element.30), channel_id=1, source_target_pairs={{0,2},{1,3},{2,0},{3,1},{4,6},{5,7},{6,4},{7,5},{8,10},{9,11},{10,... | collective-permute-start | bytes 196616 | tf_op jit(solution)/shard_map/ppermute | solution.py:199
  26.1 2.9 %collective-permute-done.9.refs_2_ = f32[64,256]{1,0:T(8,128)S(1)} collective-permute-done((f32[64,256]{1,0:T(8,128)S(1)}, f32[64,256]{1,0:T(8,128)S(1)}, u32[]{:S(2)}, u32[]{:S(2)}) %collective-permute-start.9) | collective-permute-done | bytes 65568 | tf_op jit(solution)/shard_map/ppermute | solution.py:199
  29.1 0.9 %collective-permute-done.10.refs_3_ = f32[64,256]{1,0:T(8,128)S(1)} collective-permute-done((f32[64,256]{1,0:T(8,128)S(1)}, f32[64,256]{1,0:T(8,128)S(1)}, u32[]{:S(2)}, u32[]{:S(2)}) %collective-permute-start.10) | collective-permute-done | bytes 65568 | tf_op jit(solution)/shard_map/ppermute | solution.py:199
  30.7 1.1 %collective-permute-done.11 = f32[72,128]{1,0:T(8,128)S(1)} collective-permute-done((f32[72,128]{1,0:T(8,128)S(1)}, f32[72,128]{1,0:T(8,128)S(1)}, u32[]{:S(2)}, u32[]{:S(2)}) %collective-permute-start.11) | collective-permute-done | bytes 36896 | tf_op jit(solution)/shard_map/ppermute | solution.py:191
  31.8 0.8 %collective-permute-start.14 = (f32[72,128]{1,0:T(8,128)S(1)}, f32[72,128]{1,0:T(8,128)S(1)}, u32[]{:S(2)}, u32[]{:S(2)}) collective-permute-start(f32[72,128]{1,0:T(8,128)S(1)} %add.18), channel_id=1, source_target_pairs={{0,6},{2,4},{4,2},{6,0},{8,14},{10,12},{12,10},{14,8},{16,22},{18,... | collective-permute-start | bytes 110600 | tf_op jit(solution)/shard_map/ppermute | solution.py:211
  32.6 0.7 %collective-permute-start.13 = (f32[72,128]{1,0:T(8,128)S(1)}, f32[72,128]{1,0:T(8,128)S(1)}, u32[]{:S(2)}, u32[]{:S(2)}) collective-permute-start(f32[72,128]{1,0:T(8,128)S(1)} %add.18), channel_id=1, source_target_pairs={{0,2},{2,0},{4,6},{6,4},{8,10},{10,8},{12,14},{14,12},{16,18},{18,... | collective-permute-start | bytes 110600 | tf_op jit(solution)/shard_map/ppermute | solution.py:211
  33.3 2.0 %collective-permute-start.12 = (f32[72,128]{1,0:T(8,128)S(1)}, f32[72,128]{1,0:T(8,128)S(1)}, u32[]{:S(2)}, u32[]{:S(2)}) collective-permute-start(f32[72,128]{1,0:T(8,128)S(1)} %add.18), channel_id=1, source_target_pairs={{0,4},{2,6},{4,0},{6,2},{8,12},{10,14},{12,8},{14,10},{16,20},{18,... | collective-permute-start | bytes 110600 | tf_op jit(solution)/shard_map/ppermute | solution.py:211
  35.3 1.6 %collective-permute-done.14 = f32[72,128]{1,0:T(8,128)S(1)} collective-permute-done((f32[72,128]{1,0:T(8,128)S(1)}, f32[72,128]{1,0:T(8,128)S(1)}, u32[]{:S(2)}, u32[]{:S(2)}) %collective-permute-start.14) | collective-permute-done | bytes 36896 | tf_op jit(solution)/shard_map/ppermute | solution.py:211
  37.3 1.8 %collective-permute-start.15 = (f32[72,128]{1,0:T(8,128)S(1)}, f32[72,128]{1,0:T(8,128)S(1)}, u32[]{:S(2)}, u32[]{:S(2)}) collective-permute-start(f32[72,128]{1,0:T(8,128)S(1)} %add_add_fusion), channel_id=1, source_target_pairs={{0,8},{4,12},{8,0},{12,4},{16,24},{20,28},{24,16},{28,20},{1,9},{5... | collective-permute-start | bytes 110600 | tf_op jit(solution)/shard_map/ppermute | solution.py:203
  39.0 1.6 %collective-permute-start.17 = (f32[72,128]{1,0:T(8,128)S(1)}, f32[72,128]{1,0:T(8,128)S(1)}, u32[]{:S(2)}, u32[]{:S(2)}) collective-permute-start(f32[72,128]{1,0:T(8,128)S(1)} %add_add_fusion), channel_id=1, source_target_pairs={{0,24},{4,28},{8,16},{12,20},{16,8},{20,12},{24,0},{28,4},{1,25},{... | collective-permute-start | bytes 110600 | tf_op jit(solution)/shard_map/ppermute | solution.py:203
  41.1 0.7 %copy.11 = f32[256,128]{1,0:T(8,128)} copy(f32[256,128]{1,0:T(8,128)S(1)} %get-tuple-element.39) | data formatting | bytes 262144
  41.8 3.0 %collective-permute-done.17 = f32[72,128]{1,0:T(8,128)S(1)} collective-permute-done((f32[72,128]{1,0:T(8,128)S(1)}, f32[72,128]{1,0:T(8,128)S(1)}, u32[]{:S(2)}, u32[]{:S(2)}) %collective-permute-start.17) | collective-permute-done | bytes 36896 | tf_op jit(solution)/shard_map/ppermute | solution.py:203
  44.8 0.7 %collective-permute-done.16 = f32[72,128]{1,0:T(8,128)S(1)} collective-permute-done((f32[72,128]{1,0:T(8,128)S(1)}, f32[72,128]{1,0:T(8,128)S(1)}, u32[]{:S(2)}, u32[]{:S(2)}) %collective-permute-start.16) | collective-permute-done | bytes 36896 | tf_op jit(solution)/shard_map/ppermute | solution.py:203
  (34 shorter events, 3.8 us)
Async XLA Ops:
  0.6 9.3 %collective-permute-start.1 = (f32[64,512]{1,0:T(8,128)}, f32[64,512]{1,0:T(8,128)S(1)}, u32[]{:S(2)}, u32[]{:S(2)}) collective-permute-start(f32[64,512]{1,0:T(8,128)} %refs_0_.1), channel_id=1, source_target_pairs={{0,4},{4,0},{8,12},{12,8},{16,20},{20,16},{24,28},{28,24},{1,5},{5... | collective-permute-start | bytes 393224 | tf_op jit(solution)/shard_map/ppermute | solution.py:203
  3.6 8.4 %collective-permute-start = (f32[64,512]{1,0:T(8,128)}, f32[64,512]{1,0:T(8,128)S(1)}, u32[]{:S(2)}, u32[]{:S(2)}) collective-permute-start(f32[64,512]{1,0:T(8,128)} %refs_0_.1), channel_id=1, source_target_pairs={{0,24},{4,28},{8,16},{12,20},{16,8},{20,12},{24,0},{28,4},{1,25},{... | collective-permute-start | bytes 393224 | tf_op jit(solution)/shard_map/ppermute | solution.py:203
  7.2 2.7 %collective-permute-start.2 = (f32[64,128]{1,0:T(8,128)}, f32[64,128]{1,0:T(8,128)S(1)}, u32[]{:S(2)}, u32[]{:S(2)}) collective-permute-start(f32[64,128]{1,0:T(8,128)} %refs_4_), channel_id=1, source_target_pairs={{0,1},{1,0},{2,3},{3,2},{4,5},{5,4},{6,7},{7,6},{8,9},{9,8},{10,11... | collective-permute-start | bytes 98312 | tf_op jit(solution)/shard_map/ppermute | solution.py:191
  7.2 7.2 %collective-permute-start.5 = (f32[64,512]{1,0:T(8,128)}, f32[64,512]{1,0:T(8,128)S(1)}, u32[]{:S(2)}, u32[]{:S(2)}) collective-permute-start(f32[64,512]{1,0:T(8,128)} %refs_0_.1), channel_id=1, source_target_pairs={{0,12},{4,8},{8,4},{12,0},{16,28},{20,24},{24,20},{28,16},{1,13},{... | collective-permute-start | bytes 393224 | tf_op jit(solution)/shard_map/ppermute | solution.py:203
  7.2 5.9 %copy-start = (f32[64,512]{1,0:T(8,128)S(1)}, f32[64,512]{1,0:T(8,128)}, u32[]{:S(2)}) copy-start(f32[64,512]{1,0:T(8,128)} %refs_0_.1) | copy-start | bytes 393220
  7.2 12.9 %copy-start.3 = (s32[1,1,4]{2,1,0:T(1,128)S(1)}, s32[1,1,4]{2,1,0:T(1,128)}, u32[]{:S(2)}) copy-start(s32[1,1,4]{2,1,0:T(1,128)} %rows.3) | copy-start | bytes 52
  7.3 12.9 %copy-start.4 = (s32[1,1,4]{2,1,0:T(1,128)S(1)}, s32[1,1,4]{2,1,0:T(1,128)}, u32[]{:S(2)}) copy-start(s32[1,1,4]{2,1,0:T(1,128)} %cols.3) | copy-start | bytes 52
  12.1 6.3 %collective-permute-start.4 = (f32[64,512]{1,0:T(8,128)S(1)}, f32[64,512]{1,0:T(8,128)S(1)}, u32[]{:S(2)}, u32[]{:S(2)}) collective-permute-start(f32[64,512]{1,0:T(8,128)S(1)} %collective-permute-done.refs_2_), channel_id=1, source_target_pairs={{0,8},{4,12},{8,0},{12,4},{16,24},{20,28},{24,16},{28,20},{1,9},{5... | collective-permute-start | bytes 393224 | tf_op jit(solution)/shard_map/ppermute | solution.py:203
  13.2 6.5 %collective-permute-start.3 = (f32[64,512]{1,0:T(8,128)S(1)}, f32[64,512]{1,0:T(8,128)S(1)}, u32[]{:S(2)}, u32[]{:S(2)}) collective-permute-start(f32[64,512]{1,0:T(8,128)S(1)} %copy-done), channel_id=1, source_target_pairs={{0,8},{4,12},{8,0},{12,4},{16,24},{20,28},{24,16},{28,20},{1,9},{5... | collective-permute-start | bytes 393224 | tf_op jit(solution)/shard_map/ppermute | solution.py:203
  14.1 6.1 %collective-permute-start.6 = (f32[64,512]{1,0:T(8,128)S(1)}, f32[64,512]{1,0:T(8,128)S(1)}, u32[]{:S(2)}, u32[]{:S(2)}) collective-permute-start(f32[64,512]{1,0:T(8,128)S(1)} %collective-permute-done.refs_2_), channel_id=1, source_target_pairs={{0,4},{4,0},{8,12},{12,8},{16,20},{20,16},{24,28},{28,24},{1,5},{5... | collective-permute-start | bytes 393224 | tf_op jit(solution)/shard_map/ppermute | solution.py:203
  18.3 5.0 %collective-permute-start.7 = (f32[64,512]{1,0:T(8,128)S(1)}, f32[64,512]{1,0:T(8,128)S(1)}, u32[]{:S(2)}, u32[]{:S(2)}) collective-permute-start(f32[64,512]{1,0:T(8,128)S(1)} %collective-permute-done.4.refs_3_), channel_id=1, source_target_pairs={{0,4},{4,0},{8,12},{12,8},{16,20},{20,16},{24,28},{28,24},{1,5},{5... | collective-permute-start | bytes 393224 | tf_op jit(solution)/shard_map/ppermute | solution.py:203
  22.1 7.8 %copy-start.1 = (f32[256,128]{1,0:T(8,128)S(1)}, f32[256,128]{1,0:T(8,128)}, u32[]{:S(2)}) copy-start(f32[256,128]{1,0:T(8,128)} %refs_7_.1) | copy-start | bytes 393220
  22.1 7.8 %copy-start.2 = (f32[64,128]{1,0:T(8,128)S(1)}, f32[64,128]{1,0:T(8,128)}, u32[]{:S(2)}) copy-start(f32[64,128]{1,0:T(8,128)} %refs_4_) | copy-start | bytes 98308
  22.1 7.8 %copy-start.5 = (f32[128]{0:T(128)S(1)}, f32[128]{0:T(128)}, u32[]{:S(2)}) copy-start(f32[128]{0:T(128)} %param.14) | copy-start | bytes 1540
  24.2 1.9 %collective-permute-start.8 = (f32[64,256]{1,0:T(8,128)S(1)}, f32[64,256]{1,0:T(8,128)S(1)}, u32[]{:S(2)}, u32[]{:S(2)}) collective-permute-start(f32[64,256]{1,0:T(8,128)S(1)} %get-tuple-element.29), channel_id=1, source_target_pairs={{0,1},{1,0},{2,3},{3,2},{4,5},{5,4},{6,7},{7,6},{8,9},{9,8},{10,11... | collective-permute-start | bytes 196616 | tf_op jit(solution)/shard_map/ppermute | solution.py:199
  24.3 4.8 %collective-permute-start.9 = (f32[64,256]{1,0:T(8,128)S(1)}, f32[64,256]{1,0:T(8,128)S(1)}, u32[]{:S(2)}, u32[]{:S(2)}) collective-permute-start(f32[64,256]{1,0:T(8,128)S(1)} %get-tuple-element.30), channel_id=1, source_target_pairs={{0,2},{1,3},{2,0},{3,1},{4,6},{5,7},{6,4},{7,5},{8,10},{9,11},{10,... | collective-permute-start | bytes 196616 | tf_op jit(solution)/shard_map/ppermute | solution.py:199
  25.6 4.3 %collective-permute-start.10 = (f32[64,256]{1,0:T(8,128)S(1)}, f32[64,256]{1,0:T(8,128)S(1)}, u32[]{:S(2)}, u32[]{:S(2)}) collective-permute-start(f32[64,256]{1,0:T(8,128)S(1)} %get-tuple-element.31), channel_id=1, source_target_pairs={{0,3},{1,2},{2,1},{3,0},{4,7},{5,6},{6,5},{7,4},{8,11},{9,10},{10,... | collective-permute-start | bytes 196616 | tf_op jit(solution)/shard_map/ppermute | solution.py:199
  30.5 1.3 %collective-permute-start.11 = (f32[72,128]{1,0:T(8,128)S(1)}, f32[72,128]{1,0:T(8,128)S(1)}, u32[]{:S(2)}, u32[]{:S(2)}) collective-permute-start(f32[72,128]{1,0:T(8,128)S(1)} %get-tuple-element.36), channel_id=1, source_target_pairs={{0,1},{1,0},{2,3},{3,2},{4,5},{5,4},{6,7},{7,6},{8,9},{9,8},{10,11... | collective-permute-start | bytes 110600 | tf_op jit(solution)/shard_map/ppermute | solution.py:191
  31.8 5.1 %collective-permute-start.14 = (f32[72,128]{1,0:T(8,128)S(1)}, f32[72,128]{1,0:T(8,128)S(1)}, u32[]{:S(2)}, u32[]{:S(2)}) collective-permute-start(f32[72,128]{1,0:T(8,128)S(1)} %add.18), channel_id=1, source_target_pairs={{0,6},{2,4},{4,2},{6,0},{8,14},{10,12},{12,10},{14,8},{16,22},{18,... | collective-permute-start | bytes 110600 | tf_op jit(solution)/shard_map/ppermute | solution.py:211
  32.6 4.4 %collective-permute-start.13 = (f32[72,128]{1,0:T(8,128)S(1)}, f32[72,128]{1,0:T(8,128)S(1)}, u32[]{:S(2)}, u32[]{:S(2)}) collective-permute-start(f32[72,128]{1,0:T(8,128)S(1)} %add.18), channel_id=1, source_target_pairs={{0,2},{2,0},{4,6},{6,4},{8,10},{10,8},{12,14},{14,12},{16,18},{18,... | collective-permute-start | bytes 110600 | tf_op jit(solution)/shard_map/ppermute | solution.py:211
  33.3 4.0 %collective-permute-start.12 = (f32[72,128]{1,0:T(8,128)S(1)}, f32[72,128]{1,0:T(8,128)S(1)}, u32[]{:S(2)}, u32[]{:S(2)}) collective-permute-start(f32[72,128]{1,0:T(8,128)S(1)} %add.18), channel_id=1, source_target_pairs={{0,4},{2,6},{4,0},{6,2},{8,12},{10,14},{12,8},{14,10},{16,20},{18,... | collective-permute-start | bytes 110600 | tf_op jit(solution)/shard_map/ppermute | solution.py:211
  37.3 4.5 %collective-permute-start.15 = (f32[72,128]{1,0:T(8,128)S(1)}, f32[72,128]{1,0:T(8,128)S(1)}, u32[]{:S(2)}, u32[]{:S(2)}) collective-permute-start(f32[72,128]{1,0:T(8,128)S(1)} %add_add_fusion), channel_id=1, source_target_pairs={{0,8},{4,12},{8,0},{12,4},{16,24},{20,28},{24,16},{28,20},{1,9},{5... | collective-permute-start | bytes 110600 | tf_op jit(solution)/shard_map/ppermute | solution.py:203
  39.0 5.8 %collective-permute-start.17 = (f32[72,128]{1,0:T(8,128)S(1)}, f32[72,128]{1,0:T(8,128)S(1)}, u32[]{:S(2)}, u32[]{:S(2)}) collective-permute-start(f32[72,128]{1,0:T(8,128)S(1)} %add_add_fusion), channel_id=1, source_target_pairs={{0,24},{4,28},{8,16},{12,20},{16,8},{20,12},{24,0},{28,4},{1,25},{... | collective-permute-start | bytes 110600 | tf_op jit(solution)/shard_map/ppermute | solution.py:203
  40.6 4.9 %collective-permute-start.16 = (f32[72,128]{1,0:T(8,128)S(1)}, f32[72,128]{1,0:T(8,128)S(1)}, u32[]{:S(2)}, u32[]{:S(2)}) collective-permute-start(f32[72,128]{1,0:T(8,128)S(1)} %add_add_fusion), channel_id=1, source_target_pairs={{0,16},{4,20},{8,24},{12,28},{16,0},{20,4},{24,8},{28,12},{1,17},{... | collective-permute-start | bytes 110600 | tf_op jit(solution)/shard_map/ppermute | solution.py:203

commit v5 on v4

--- a/solution.py
+++ b/solution.py
@@ -10,6 +10,7 @@
 F32 = jnp.float32
 BF16 = jnp.bfloat16
 SUBLANES = 8
+LANES = 128
 VMEM_BYTES = 40 * 2**20
 
 
@@ -40,24 +41,43 @@
     )
 
 
-def split_kernel(slabs, high, low, held, sems):
-    count = slabs.shape[0]
-    copies = [pltpu.make_async_copy(slabs.at[t], held.at[t], sems.at[t]) for t in range(count)]
+def split_kernel(sources, groups, slabs, rows, cols, high, low, plan, held, rows_s, cols_s, sems):
+    slots = slabs.shape[0]
+    copies = [pltpu.make_async_copy(slabs.at[t], held.at[t], sems.at[t]) for t in range(slots)]
+    for k, pair in enumerate(((rows, rows_s), (cols, cols_s))):
+        copies.append(pltpu.make_async_copy(*pair, sems.at[slots + k]))
     for copy in copies:
         copy.start()
-    for t, copy in enumerate(copies):
+    for copy in copies[slots:]:
+        copy.wait()
+    row = lax.axis_index("row")
+    which = place = 0
+    for t in range(slots):
+        digit = 0
+        for p, source in enumerate(sources):
+            digit = jnp.where(cols_s[0, 0, t] == source(row), p + 1, digit)
+        which = which * (len(sources) + 1) + digit
+        place = place * groups + jnp.clip(rows_s[0, 0, t], 0, groups - 1)
+    plan[0] = jnp.full(plan.shape[1:], which, jnp.int32)
+    plan[1] = jnp.full(plan.shape[1:], place, jnp.int32)
+    for t, copy in enumerate(copies[:slots]):
         copy.wait()
         high[t], low[t] = split(held[t].T)
 
 
-def split_slabs(slabs):
-    count = slabs.shape[0]
-    out = pltpu.VMEM(slabs.shape, BF16)
-    scratch = [pltpu.VMEM(slabs.shape, F32), pltpu.SemaphoreType.DMA((count,))]
+def split_slabs(slabs, tile_rows, tile_cols, sources, groups):
+    slots = slabs.shape[0]
+    outs = [pltpu.VMEM(slabs.shape, BF16)] * 2 + [pltpu.VMEM((2, SUBLANES, LANES), jnp.int32)]
+    scratch = [pltpu.VMEM(slabs.shape, F32)] + [pltpu.SMEM(tile_rows.shape, jnp.int32)] * 2
+    scratch.append(pltpu.SemaphoreType.DMA((slots + 2,)))
     cost = pl.CostEstimate(flops=4 * slabs.size, bytes_accessed=8 * slabs.size, transcendentals=0)
-    return call(split_kernel, (out, out), [pl.ANY], "split_slabs", scratch, cost)(
-        pltpu.with_memory_space_constraint(slabs, pltpu.HBM)
-    )
+    operands = [pltpu.with_memory_space_constraint(x, pltpu.HBM) for x in (slabs, tile_rows, tile_cols)]
+    kernel = functools.partial(split_kernel, sources, groups)
+    return call(kernel, outs, [pl.ANY] * len(operands), "split_slabs", scratch, cost)(*operands)
+
+
+def digits(number, base, count):
+    return [lax.rem(lax.div(number, base ** (count - 1 - t)), base) for t in range(count)]
 
 
 def product(piece, high, low):
@@ -71,47 +91,46 @@
     picked[t, :half_width], picked[t, half_width:] = split(piece[...])
 
 
-def early_kernel(sources, rows, cols, counts, high, low, *refs):
-    pieces, (total, picked, found) = refs[: len(sources)], refs[-3:]
+def early_kernel(bases, counts, plan, high, low, *refs):
+    pieces, (total, rest, picked, which) = refs[:-4], refs[-4:]
     slots = high.shape[0]
-    live = counts[0, 0]
-    row = lax.axis_index("row")
+    place = digits(plan[1][0, 0], bases[1], slots)
+    found = [jnp.where(t < counts[0, 0], d, 0) for t, d in enumerate(digits(plan[0][0, 0], bases[0], slots))]
+    left = 0
     for t in range(slots):
-        found[t] = 0
-    for piece, source in zip(pieces, sources):
-        block = source(row)
+        which[t] = found[t]
+        left = left * (bases[1] + 1) + jnp.where(found[t] > len(pieces), place[t] + 1, 0)
+    rest[...] = jnp.full(rest.shape, left, jnp.int32)
+    for p, piece in enumerate(pieces):
 
         @pl.loop(0, slots)
         def _(t):
-            @pl.when((t < live) & (cols[0, 0, t] == block))
+            @pl.when(which[t] == p + 1)
             def _():
-                found[t] = 1
                 pick(picked, t, piece)
 
     total[...] = jnp.zeros_like(total)
     for t in range(slots):
 
-        @pl.when(found[t] == 1)
+        @pl.when((found[t] > 0) & (found[t] <= len(pieces)))
         def _():
-            total[rows[0, 0, t]] += product(picked[t], high[t], low[t])
-
-
-def late_kernel(sizes, sources, rows, cols, counts, high, low, early, *refs):
+            total[place[t]] += product(picked[t], high[t], low[t])
+
+
+def late_kernel(sizes, plan, high, low, early, piece, *refs):
     groups, halves = sizes
-    pieces, outs, (total, picked) = refs[: len(sources)], refs[len(sources) : -2], refs[-2:]
+    outs, (total, picked) = refs[:-2], refs[-2:]
     slots = high.shape[0]
     block_len = early.shape[2]
-    live = counts[0, 0]
-    row, col, rep = lax.axis_index("row"), lax.axis_index("col"), lax.axis_index("rep")
+    col, rep = lax.axis_index("col"), lax.axis_index("rep")
+    place = digits(plan[...][0, 0], groups + 1, slots)
     total[...] = early[...]
-    for piece, source in zip(pieces, sources):
-        block = source(row)
-        pick(picked, 0, piece)
-        for t in range(slots):
-
-            @pl.when((t < live) & (cols[0, 0, t] == block))
-            def _():
-                total[rows[0, 0, t]] += product(picked[0], high[t], low[t])
+    pick(picked, 0, piece)
+    for t in range(slots):
+
+        @pl.when(place[t] > 0)
+        def _():
+            total[place[t] - 1] += product(picked[0], high[t], low[t])
 
     part = block_len // halves
     for i, out in enumerate(outs):
@@ -120,29 +139,27 @@
         out[...] = total[lax.rem(col + k, groups), :, pl.ds(begin, part)]
 
 
-def mix(sizes, slot_info, slabs, early, late):
+def mix(sizes, slabs, counts, plan, pieces):
     groups, halves = sizes
     slots = slabs[0].shape[0]
-    half_width, block_len = early[0][0].shape
-    spaces = [pltpu.SMEM] * 3 + [pltpu.VMEM] * 2
+    half_width, block_len = pieces[0].shape
+    bases = (len(pieces) + 1, groups)
     picked = pltpu.VMEM((slots, 2 * half_width, block_len), BF16)
-    pieces, sources = zip(*early)
-    total = call(
-        functools.partial(early_kernel, sources),
-        pltpu.VMEM((groups, half_width, block_len), F32),
-        spaces + [pltpu.VMEM] * len(pieces),
+    total, rest = call(
+        functools.partial(early_kernel, bases),
+        [pltpu.VMEM((groups, half_width, block_len), F32), pltpu.VMEM((SUBLANES, LANES), jnp.int32)],
+        [pltpu.SMEM] + [pltpu.VMEM] * (2 + len(pieces)),
         "mix_early",
         [picked, pltpu.SMEM((slots,), jnp.int32)],
         pl.CostEstimate(flops=6 * slabs[0].size * half_width, bytes_accessed=4 * slabs[0].size, transcendentals=0),
-    )(*slot_info, *slabs, *pieces)
-    pieces, sources = zip(*late)
+    )(counts, plan, *slabs, *pieces[:-1])
     return call(
-        functools.partial(late_kernel, sizes, sources),
+        functools.partial(late_kernel, sizes),
         [pltpu.VMEM((half_width, block_len // halves), F32)] * (groups * halves),
-        spaces + [pltpu.VMEM] * (1 + len(pieces)),
+        [pltpu.VMEM] * 5,
         "mix_late",
         [pltpu.VMEM(total.shape, F32), picked],
-    )(*slot_info, *slabs, total, *pieces)
+    )(rest, *slabs, total, pieces[-1])
 
 
 def node_kernel(groups, halves, *refs):
@@ -215,38 +232,53 @@
     return n & (n - 1) == 0
 
 
+def line_basis(size):
+    bits = [1 << i for i in range(1, size.bit_length() - 1)]
+    return [size - 2] + bits[-2::-1] if bits else []
+
+
+def piece_sources(size):
+    if not is_power(size) or size < 2:
+        return [lambda row, k=k: lax.rem(row + size - k, size) for k in range(size)]
+    return [lambda row, mask=mask: lax.bitwise_xor(row, mask) for mask in piece_masks(size)]
+
+
+def piece_masks(size):
+    lines = [0]
+    for mask in line_basis(size):
+        lines += [other ^ mask for other in lines]
+    last = max(lines, key=lambda mask: (lines.index(mask) > 0 and mask not in line_basis(size), lines.index(mask)))
+    crossed = [mask ^ 1 for mask in lines if mask != last] + [last ^ 1]
+    return lines + crossed
+
+
 def gather_row(x, size, held):
     if not is_power(size) or size < 2:
-        pieces = [x] + [shift(x, "row", size, k) for k in range(1, size)]
-        return [(p, lambda row, k=k: lax.rem(row + size - k, size)) for k, p in enumerate(pieces)], held
-    bits = [1 << i for i in range(1, size.bit_length() - 1)]
-    basis = [size - 2] + bits[-2::-1] if bits else []
+        return [x] + [shift(x, "row", size, k) for k in range(1, size)], held
+    basis = line_basis(size)
     own_cross = swap(x, "row", size, 1)
-    found = {0: x}
+    pieces = {0: x, 1: own_cross}
+    if len(basis) > 1:
+        pieces[basis[-1] ^ 1] = swap(x, "row", size, basis[-1] ^ 1)
+    lines = [0]
     for step, mask in enumerate(basis):
-        new = {}
-        for other, block in found.items():
-            new[other ^ mask] = swap(block, "row", size, mask)
+        for other in lines:
+            if step and step == len(basis) - 1 and not other:
+                free, _ = lax.optimization_barrier((x, pieces[mask ^ 1]))
+                pieces[mask] = swap(free, "row", size, mask)
+            else:
+                pieces[other ^ mask] = swap(pieces[other], "row", size, mask)
         if step == 0:
-            near = swap(x, "row", size, basis[-1]) if len(basis) > 1 else x
-            new[mask], own_cross, held = lax.optimization_barrier((new[mask], own_cross, held))
-        elif step == len(basis) - 1:
-            new[mask] = near
-        found.update(new)
-    crossed = {0: own_cross}
-    if len(basis) > 1:
-        crossed[basis[-1]] = swap(x, "row", size, basis[-1] ^ 1)
-    last = None
-    for mask, block in found.items():
-        if mask not in crossed:
-            if mask not in basis and last is None:
-                last = mask
-                block, _ = lax.optimization_barrier((block, crossed[basis[-1]]))
-            crossed[mask] = swap(block, "row", size, 1)
-    order = sorted(found, key=lambda mask: (mask == last, mask not in basis and mask != 0, mask))
-    far = [(mask ^ 1, crossed[mask]) for mask in order]
-    near = [(mask, found[mask]) for mask in order]
-    return [(p, lambda row, mask=mask: lax.bitwise_xor(row, mask)) for mask, p in near + far], held
+            pieces[mask], pieces[1], held = lax.optimization_barrier((pieces[mask], pieces[1], held))
+        lines += [other ^ mask for other in lines]
+    order = piece_masks(size)
+    for mask in lines:
+        if mask ^ 1 not in pieces:
+            block = pieces[mask]
+            if mask ^ 1 == order[-1] and len(basis) > 1:
+                block, _ = lax.optimization_barrier((block, pieces[basis[-1] ^ 1]))
+            pieces[mask ^ 1] = swap(block, "row", size, 1)
+    return [pieces[mask] for mask in order], held
 
 
 def sum_all(grad, groups, row_size):
@@ -286,9 +318,9 @@
 
 def local(row_size, groups, halves, adj_tiles, tile_rows, tile_cols, tile_counts, features_t, weight, bias_vec, cotangent):
     weights = [weight] + [shift(weight, "rep", halves, k) for k in range(1, halves)]
-    pieces, (slabs, weights) = gather_row(features_t, row_size, (split_slabs(adj_tiles[0, 0]), weights))
-    slot_info = (tile_rows, tile_cols, tile_counts)
-    parts = mix((groups, halves), slot_info, slabs, pieces[:-1], pieces[-1:])
+    *slabs, plan = split_slabs(adj_tiles[0, 0], tile_rows, tile_cols, piece_sources(row_size), groups)
+    pieces, (slabs, plan, weights) = gather_row(features_t, row_size, (slabs, plan, weights))
+    parts = mix((groups, halves), slabs, tile_counts, plan, pieces)
 
     terms = [None] * len(parts)
     for i in sorted(range(len(parts)), key=lambda i: -i):

time: 46.2 us -> 45.6 us (0.987)
  starting transfers between devices: 18.1 us -> 19.9 us
  Pallas kernels: 6.61 us -> 5 us
  waiting for transfers between devices: 19.2 us -> 18.2 us
    ppermute x10, starting transfers between devices: 12.5 us -> 14.3 us  [swap(): return lax.ppermute(x, axis, [(i, i ^ bit) for i in range(size)])]
    pallas_call x3, Pallas kernels: 5.45 us -> 3.85 us  [the longest x1 2.68 us: split_slabs(): call(kernel, outs, [pl.ANY] * len(operands), 'split_slabs', scratch, cost)]
    ppermute x10, waiting for transfers between devices: 12.4 us -> 11.2 us  [swap(): return lax.ppermute(x, axis, [(i, i ^ bit) for i in range(size)])]
  transfers between devices with their start and end apart: 18 -> 18, of which waited for: 14 -> 14; matrix products, arithmetic and copies ran while one was open for 1% -> 1% of each run, Pallas kernels for 10% -> 8%
where the time goes in v5:
time: 45.6 us; the launch traced here: 45.1 us
  starting transfers between devices  19.9 us (44%)
  waiting for transfers between devices  18.2 us (40%)
  Pallas kernels  5 us (11%)
  between operations  1.37 us (3%)
  local copies, waits for them, and re-layouts  0.67 us (1%)
    ppermute x10, starting transfers between devices, swap(): return lax.ppermute(x, axis, [(i, i ^ bit) for i in range(size)])  14.3 us
    ppermute x10, waiting for transfers between devices, swap(): return lax.ppermute(x, axis, [(i, i ^ bit) for i in range(size)])  11.2 us
    ppermute x3, waiting for transfers between devices, shift_two(): return lax.ppermute(x, ('col', 'rep'), perm)  3.71 us
    ppermute x3, starting transfers between devices, swap_two(): return lax.ppermute(x, axes, perm)  3.49 us
    pallas_call x1, Pallas kernels, split_slabs(): call(kernel, outs, [pl.ANY] * len(operands), 'split_slabs', scratch, cost)  2.68 us
    ppermute x3, waiting for transfers between devices, swap_two(): return lax.ppermute(x, axes, perm)  2.23 us
    ppermute x3, starting transfers between devices, shift_two(): return lax.ppermute(x, ('col', 'rep'), perm)  1.93 us
    pallas_call x1, Pallas kernels, mix(): call(functools.partial(early_kernel, bases), [pltpu.VMEM((groups, half_wi...  1.07 us
  transfers between devices with their start and end apart: 18, of which 14 were waited for; matrix products, arithmetic and copies ran while one was open for 1% of the time, Pallas kernels for 8%

profile of v5, /device:TPU:0, one launch (start us, length us, event | category | flops | bytes accessed | tf_op | source)
XLA Modules:
  0.0 45.1 jit_solution(1828173959745490253)
XLA Ops:
  0.6 3.0 %collective-permute-start.1 = (f32[64,512]{1,0:T(8,128)}, f32[64,512]{1,0:T(8,128)S(1)}, u32[]{:S(2)}, u32[]{:S(2)}) collective-permute-start(f32[64,512]{1,0:T(8,128)} %refs_0_.1), channel_id=1, source_target_pairs={{0,4},{4,0},{8,12},{12,8},{16,20},{20,16},{24,28},{28,24},{1,5},{5... | collective-permute-start | bytes 393224 | tf_op jit(solution)/shard_map/ppermute | solution.py:220
  3.6 3.6 %collective-permute-start = (f32[64,512]{1,0:T(8,128)}, f32[64,512]{1,0:T(8,128)S(1)}, u32[]{:S(2)}, u32[]{:S(2)}) collective-permute-start(f32[64,512]{1,0:T(8,128)} %refs_0_.1), channel_id=1, source_target_pairs={{0,24},{4,28},{8,16},{12,20},{16,8},{20,12},{24,0},{28,4},{1,25},{... | collective-permute-start | bytes 393224 | tf_op jit(solution)/shard_map/ppermute | solution.py:220
  7.2 2.7 %split_slabs.1 = (bf16[4,512,512]{2,1,0:T(8,128)(2,1)S(1)}, bf16[4,512,512]{2,1,0:T(8,128)(2,1)S(1)}, s32[2,8,128]{2,1,0:T(8,128)S(1)}) custom-call(f32[4,512,512]{2,1,0:T(8,128)} %bitcast.3, s32[1,1,4]{2,1,0:T(1,128)} %rows.1, s32[1,1,4]{2,1,0:T(1,128)} %cols.1), custom_call_target="tpu_custom_call" | custom-call | flops 4194304 | bytes 8388608 | tf_op jit(solution)/shard_map/split_slabs/pallas_call | solution.py:76
  10.0 2.1 %collective-permute-done.refs_1_ = f32[64,512]{1,0:T(8,128)S(1)} collective-permute-done((f32[64,512]{1,0:T(8,128)}, f32[64,512]{1,0:T(8,128)S(1)}, u32[]{:S(2)}, u32[]{:S(2)}) %collective-permute-start) | collective-permute-done | bytes 131104 | tf_op jit(solution)/shard_map/ppermute | solution.py:220
  12.1 1.1 %collective-permute-start.5 = (f32[64,512]{1,0:T(8,128)S(1)}, f32[64,512]{1,0:T(8,128)S(1)}, u32[]{:S(2)}, u32[]{:S(2)}) collective-permute-start(f32[64,512]{1,0:T(8,128)S(1)} %collective-permute-done.refs_1_), channel_id=1, source_target_pairs={{0,8},{4,12},{8,0},{12,4},{16,24},{20,28},{24,16},{28,20},{1,9},{5... | collective-permute-start | bytes 393224 | tf_op jit(solution)/shard_map/ppermute | solution.py:220
  13.2 0.6 %collective-permute-done.3.refs_6_ = f32[64,512]{1,0:T(8,128)S(1)} collective-permute-done((f32[64,512]{1,0:T(8,128)}, f32[64,512]{1,0:T(8,128)S(1)}, u32[]{:S(2)}, u32[]{:S(2)}) %collective-permute-start.3) | collective-permute-done | bytes 131104 | tf_op jit(solution)/shard_map/ppermute | solution.py:220
  13.8 1.4 %collective-permute-start.4 = (f32[64,512]{1,0:T(8,128)S(1)}, f32[64,512]{1,0:T(8,128)S(1)}, u32[]{:S(2)}, u32[]{:S(2)}) collective-permute-start(f32[64,512]{1,0:T(8,128)S(1)} %copy-done.1), channel_id=1, source_target_pairs={{0,8},{4,12},{8,0},{12,4},{16,24},{20,28},{24,16},{28,20},{1,9},{5... | collective-permute-start | bytes 393224 | tf_op jit(solution)/shard_map/ppermute | solution.py:220
  15.2 1.6 %collective-permute-start.6 = (f32[64,512]{1,0:T(8,128)S(1)}, f32[64,512]{1,0:T(8,128)S(1)}, u32[]{:S(2)}, u32[]{:S(2)}) collective-permute-start(f32[64,512]{1,0:T(8,128)S(1)} %collective-permute-done.refs_1_), channel_id=1, source_target_pairs={{0,4},{4,0},{8,12},{12,8},{16,20},{20,16},{24,28},{28,24},{1,5},{5... | collective-permute-start | bytes 393224 | tf_op jit(solution)/shard_map/ppermute | solution.py:220
  16.8 1.6 %collective-permute-done.5.refs_3_ = f32[64,512]{1,0:T(8,128)S(1)} collective-permute-done((f32[64,512]{1,0:T(8,128)S(1)}, f32[64,512]{1,0:T(8,128)S(1)}, u32[]{:S(2)}, u32[]{:S(2)}) %collective-permute-start.5) | collective-permute-done | bytes 131104 | tf_op jit(solution)/shard_map/ppermute | solution.py:220
  19.0 0.7 %collective-permute-done.4.refs_2_ = f32[64,512]{1,0:T(8,128)S(1)} collective-permute-done((f32[64,512]{1,0:T(8,128)S(1)}, f32[64,512]{1,0:T(8,128)S(1)}, u32[]{:S(2)}, u32[]{:S(2)}) %collective-permute-start.4) | collective-permute-done | bytes 131104 | tf_op jit(solution)/shard_map/ppermute | solution.py:220
  20.4 1.1 %mix_early.1 = (f32[2,64,512]{2,1,0:T(8,128)S(1)}, s32[8,128]{1,0:T(8,128)S(1)}) custom-call(s32[1,1]{1,0:T(1,128)S(6)} %copy.12.counts, s32[2,8,128]{2,1,0:T(8,128)S(1)} %get-tuple-element.29.plan, bf16[4,512,512]{2,1,0:T(8,128)(2,1)S(1)} %get-tuple-element.30.high, bf16[4,512,512]{2,1,0:T(8,128)(2,1)S(1)} %get-tuple-element.31.low, ...), custom_call_target="tpu_custom_call" | custom-call | flops 402653184 | bytes 4194304 | tf_op jit(solution)/shard_map/mix_early/pallas_call | solution.py:148
  21.5 1.9 %collective-permute-done.7.piece = f32[64,512]{1,0:T(8,128)S(1)} collective-permute-done((f32[64,512]{1,0:T(8,128)S(1)}, f32[64,512]{1,0:T(8,128)S(1)}, u32[]{:S(2)}, u32[]{:S(2)}) %collective-permute-start.7) | collective-permute-done | bytes 131104 | tf_op jit(solution)/shard_map/ppermute | solution.py:220
  23.5 1.5 %collective-permute-start.9 = (f32[64,256]{1,0:T(8,128)S(1)}, f32[64,256]{1,0:T(8,128)S(1)}, u32[]{:S(2)}, u32[]{:S(2)}) collective-permute-start(f32[64,256]{1,0:T(8,128)S(1)} %get-tuple-element.40), channel_id=1, source_target_pairs={{0,2},{1,3},{2,0},{3,1},{4,6},{5,7},{6,4},{7,5},{8,10},{9,11},{10,... | collective-permute-start | bytes 196616 | tf_op jit(solution)/shard_map/ppermute | solution.py:216
  25.4 2.6 %collective-permute-done.9.refs_2_ = f32[64,256]{1,0:T(8,128)S(1)} collective-permute-done((f32[64,256]{1,0:T(8,128)S(1)}, f32[64,256]{1,0:T(8,128)S(1)}, u32[]{:S(2)}, u32[]{:S(2)}) %collective-permute-start.9) | collective-permute-done | bytes 65568 | tf_op jit(solution)/shard_map/ppermute | solution.py:216
  28.0 1.1 %collective-permute-done.10.refs_3_ = f32[64,256]{1,0:T(8,128)S(1)} collective-permute-done((f32[64,256]{1,0:T(8,128)S(1)}, f32[64,256]{1,0:T(8,128)S(1)}, u32[]{:S(2)}, u32[]{:S(2)}) %collective-permute-start.10) | collective-permute-done | bytes 65568 | tf_op jit(solution)/shard_map/ppermute | solution.py:216
  29.9 1.0 %collective-permute-done.11 = f32[72,128]{1,0:T(8,128)S(1)} collective-permute-done((f32[72,128]{1,0:T(8,128)S(1)}, f32[72,128]{1,0:T(8,128)S(1)}, u32[]{:S(2)}, u32[]{:S(2)}) %collective-permute-start.11) | collective-permute-done | bytes 36896 | tf_op jit(solution)/shard_map/ppermute | solution.py:208
  31.0 0.9 %collective-permute-start.14 = (f32[72,128]{1,0:T(8,128)S(1)}, f32[72,128]{1,0:T(8,128)S(1)}, u32[]{:S(2)}, u32[]{:S(2)}) collective-permute-start(f32[72,128]{1,0:T(8,128)S(1)} %add.18), channel_id=1, source_target_pairs={{0,6},{2,4},{4,2},{6,0},{8,14},{10,12},{12,10},{14,8},{16,22},{18,... | collective-permute-start | bytes 110600 | tf_op jit(solution)/shard_map/ppermute | solution.py:228
  31.8 0.9 %collective-permute-start.13 = (f32[72,128]{1,0:T(8,128)S(1)}, f32[72,128]{1,0:T(8,128)S(1)}, u32[]{:S(2)}, u32[]{:S(2)}) collective-permute-start(f32[72,128]{1,0:T(8,128)S(1)} %add.18), channel_id=1, source_target_pairs={{0,2},{2,0},{4,6},{6,4},{8,10},{10,8},{12,14},{14,12},{16,18},{18,... | collective-permute-start | bytes 110600 | tf_op jit(solution)/shard_map/ppermute | solution.py:228
  32.7 1.7 %collective-permute-start.12 = (f32[72,128]{1,0:T(8,128)S(1)}, f32[72,128]{1,0:T(8,128)S(1)}, u32[]{:S(2)}, u32[]{:S(2)}) collective-permute-start(f32[72,128]{1,0:T(8,128)S(1)} %add.18), channel_id=1, source_target_pairs={{0,4},{2,6},{4,0},{6,2},{8,12},{10,14},{12,8},{14,10},{16,20},{18,... | collective-permute-start | bytes 110600 | tf_op jit(solution)/shard_map/ppermute | solution.py:228
  34.4 1.5 %collective-permute-done.14 = f32[72,128]{1,0:T(8,128)S(1)} collective-permute-done((f32[72,128]{1,0:T(8,128)S(1)}, f32[72,128]{1,0:T(8,128)S(1)}, u32[]{:S(2)}, u32[]{:S(2)}) %collective-permute-start.14) | collective-permute-done | bytes 36896 | tf_op jit(solution)/shard_map/ppermute | solution.py:228
  36.7 1.5 %collective-permute-start.15 = (f32[72,128]{1,0:T(8,128)S(1)}, f32[72,128]{1,0:T(8,128)S(1)}, u32[]{:S(2)}, u32[]{:S(2)}) collective-permute-start(f32[72,128]{1,0:T(8,128)S(1)} %add_add_fusion), channel_id=1, source_target_pairs={{0,8},{4,12},{8,0},{12,4},{16,24},{20,28},{24,16},{28,20},{1,9},{5... | collective-permute-start | bytes 110600 | tf_op jit(solution)/shard_map/ppermute | solution.py:220
  38.2 1.5 %collective-permute-start.17 = (f32[72,128]{1,0:T(8,128)S(1)}, f32[72,128]{1,0:T(8,128)S(1)}, u32[]{:S(2)}, u32[]{:S(2)}) collective-permute-start(f32[72,128]{1,0:T(8,128)S(1)} %add_add_fusion), channel_id=1, source_target_pairs={{0,24},{4,28},{8,16},{12,20},{16,8},{20,12},{24,0},{28,4},{1,25},{... | collective-permute-start | bytes 110600 | tf_op jit(solution)/shard_map/ppermute | solution.py:220
  40.2 0.7 %copy.11 = f32[256,128]{1,0:T(8,128)} copy(f32[256,128]{1,0:T(8,128)S(1)} %get-tuple-element.49) | data formatting | bytes 262144
  40.9 3.0 %collective-permute-done.17 = f32[72,128]{1,0:T(8,128)S(1)} collective-permute-done((f32[72,128]{1,0:T(8,128)S(1)}, f32[72,128]{1,0:T(8,128)S(1)}, u32[]{:S(2)}, u32[]{:S(2)}) %collective-permute-start.17) | collective-permute-done | bytes 36896 | tf_op jit(solution)/shard_map/ppermute | solution.py:220
  (30 shorter events, 4.5 us)
Async XLA Ops:
  0.6 9.3 %collective-permute-start.1 = (f32[64,512]{1,0:T(8,128)}, f32[64,512]{1,0:T(8,128)S(1)}, u32[]{:S(2)}, u32[]{:S(2)}) collective-permute-start(f32[64,512]{1,0:T(8,128)} %refs_0_.1), channel_id=1, source_target_pairs={{0,4},{4,0},{8,12},{12,8},{16,20},{20,16},{24,28},{28,24},{1,5},{5... | collective-permute-start | bytes 393224 | tf_op jit(solution)/shard_map/ppermute | solution.py:220
  3.6 8.4 %collective-permute-start = (f32[64,512]{1,0:T(8,128)}, f32[64,512]{1,0:T(8,128)S(1)}, u32[]{:S(2)}, u32[]{:S(2)}) collective-permute-start(f32[64,512]{1,0:T(8,128)} %refs_0_.1), channel_id=1, source_target_pairs={{0,24},{4,28},{8,16},{12,20},{16,8},{20,12},{24,0},{28,4},{1,25},{... | collective-permute-start | bytes 393224 | tf_op jit(solution)/shard_map/ppermute | solution.py:220
  7.2 6.6 %collective-permute-start.3 = (f32[64,512]{1,0:T(8,128)}, f32[64,512]{1,0:T(8,128)S(1)}, u32[]{:S(2)}, u32[]{:S(2)}) collective-permute-start(f32[64,512]{1,0:T(8,128)} %refs_0_.1), channel_id=1, source_target_pairs={{0,12},{4,8},{8,4},{12,0},{16,28},{20,24},{24,20},{28,16},{1,13},{... | collective-permute-start | bytes 393224 | tf_op jit(solution)/shard_map/ppermute | solution.py:220
  7.2 2.7 %collective-permute-start.2 = (f32[64,128]{1,0:T(8,128)}, f32[64,128]{1,0:T(8,128)S(1)}, u32[]{:S(2)}, u32[]{:S(2)}) collective-permute-start(f32[64,128]{1,0:T(8,128)} %refs_4_), channel_id=1, source_target_pairs={{0,1},{1,0},{2,3},{3,2},{4,5},{5,4},{6,7},{7,6},{8,9},{9,8},{10,11... | collective-permute-start | bytes 98312 | tf_op jit(solution)/shard_map/ppermute | solution.py:208
  7.2 6.6 %copy-start.1 = (f32[64,512]{1,0:T(8,128)S(1)}, f32[64,512]{1,0:T(8,128)}, u32[]{:S(2)}) copy-start(f32[64,512]{1,0:T(8,128)} %refs_0_.1) | copy-start | bytes 393220
  12.1 6.3 %collective-permute-start.5 = (f32[64,512]{1,0:T(8,128)S(1)}, f32[64,512]{1,0:T(8,128)S(1)}, u32[]{:S(2)}, u32[]{:S(2)}) collective-permute-start(f32[64,512]{1,0:T(8,128)S(1)} %collective-permute-done.refs_1_), channel_id=1, source_target_pairs={{0,8},{4,12},{8,0},{12,4},{16,24},{20,28},{24,16},{28,20},{1,9},{5... | collective-permute-start | bytes 393224 | tf_op jit(solution)/shard_map/ppermute | solution.py:220
  13.8 6.0 %collective-permute-start.4 = (f32[64,512]{1,0:T(8,128)S(1)}, f32[64,512]{1,0:T(8,128)S(1)}, u32[]{:S(2)}, u32[]{:S(2)}) collective-permute-start(f32[64,512]{1,0:T(8,128)S(1)} %copy-done.1), channel_id=1, source_target_pairs={{0,8},{4,12},{8,0},{12,4},{16,24},{20,28},{24,16},{28,20},{1,9},{5... | collective-permute-start | bytes 393224 | tf_op jit(solution)/shard_map/ppermute | solution.py:220
  15.2 5.2 %collective-permute-start.6 = (f32[64,512]{1,0:T(8,128)S(1)}, f32[64,512]{1,0:T(8,128)S(1)}, u32[]{:S(2)}, u32[]{:S(2)}) collective-permute-start(f32[64,512]{1,0:T(8,128)S(1)} %collective-permute-done.refs_1_), channel_id=1, source_target_pairs={{0,4},{4,0},{8,12},{12,8},{16,20},{20,16},{24,28},{28,24},{1,5},{5... | collective-permute-start | bytes 393224 | tf_op jit(solution)/shard_map/ppermute | solution.py:220
  18.4 5.0 %collective-permute-start.7 = (f32[64,512]{1,0:T(8,128)S(1)}, f32[64,512]{1,0:T(8,128)S(1)}, u32[]{:S(2)}, u32[]{:S(2)}) collective-permute-start(f32[64,512]{1,0:T(8,128)S(1)} %collective-permute-done.5.refs_3_), channel_id=1, source_target_pairs={{0,4},{4,0},{8,12},{12,8},{16,20},{20,16},{24,28},{28,24},{1,5},{5... | collective-permute-start | bytes 393224 | tf_op jit(solution)/shard_map/ppermute | solution.py:220
  23.3 5.8 %copy-start = (f32[256,128]{1,0:T(8,128)S(1)}, f32[256,128]{1,0:T(8,128)}, u32[]{:S(2)}) copy-start(f32[256,128]{1,0:T(8,128)} %refs_7_.1) | copy-start | bytes 393220
  23.4 5.8 %copy-start.2 = (f32[64,128]{1,0:T(8,128)S(1)}, f32[64,128]{1,0:T(8,128)}, u32[]{:S(2)}) copy-start(f32[64,128]{1,0:T(8,128)} %refs_4_) | copy-start | bytes 98308
  23.4 5.8 %copy-start.3 = (f32[128]{0:T(128)S(1)}, f32[128]{0:T(128)}, u32[]{:S(2)}) copy-start(f32[128]{0:T(128)} %param.14) | copy-start | bytes 1540
  23.5 1.9 %collective-permute-start.8 = (f32[64,256]{1,0:T(8,128)S(1)}, f32[64,256]{1,0:T(8,128)S(1)}, u32[]{:S(2)}, u32[]{:S(2)}) collective-permute-start(f32[64,256]{1,0:T(8,128)S(1)} %get-tuple-element.39), channel_id=1, source_target_pairs={{0,1},{1,0},{2,3},{3,2},{4,5},{5,4},{6,7},{7,6},{8,9},{9,8},{10,11... | collective-permute-start | bytes 196616 | tf_op jit(solution)/shard_map/ppermute | solution.py:216
  23.5 4.5 %collective-permute-start.9 = (f32[64,256]{1,0:T(8,128)S(1)}, f32[64,256]{1,0:T(8,128)S(1)}, u32[]{:S(2)}, u32[]{:S(2)}) collective-permute-start(f32[64,256]{1,0:T(8,128)S(1)} %get-tuple-element.40), channel_id=1, source_target_pairs={{0,2},{1,3},{2,0},{3,1},{4,6},{5,7},{6,4},{7,5},{8,10},{9,11},{10,... | collective-permute-start | bytes 196616 | tf_op jit(solution)/shard_map/ppermute | solution.py:216
  25.1 4.0 %collective-permute-start.10 = (f32[64,256]{1,0:T(8,128)S(1)}, f32[64,256]{1,0:T(8,128)S(1)}, u32[]{:S(2)}, u32[]{:S(2)}) collective-permute-start(f32[64,256]{1,0:T(8,128)S(1)} %get-tuple-element.41), channel_id=1, source_target_pairs={{0,3},{1,2},{2,1},{3,0},{4,7},{5,6},{6,5},{7,4},{8,11},{9,10},{10,... | collective-permute-start | bytes 196616 | tf_op jit(solution)/shard_map/ppermute | solution.py:216
  29.7 1.3 %collective-permute-start.11 = (f32[72,128]{1,0:T(8,128)S(1)}, f32[72,128]{1,0:T(8,128)S(1)}, u32[]{:S(2)}, u32[]{:S(2)}) collective-permute-start(f32[72,128]{1,0:T(8,128)S(1)} %get-tuple-element.46), channel_id=1, source_target_pairs={{0,1},{1,0},{2,3},{3,2},{4,5},{5,4},{6,7},{7,6},{8,9},{9,8},{10,11... | collective-permute-start | bytes 110600 | tf_op jit(solution)/shard_map/ppermute | solution.py:208
  31.0 5.0 %collective-permute-start.14 = (f32[72,128]{1,0:T(8,128)S(1)}, f32[72,128]{1,0:T(8,128)S(1)}, u32[]{:S(2)}, u32[]{:S(2)}) collective-permute-start(f32[72,128]{1,0:T(8,128)S(1)} %add.18), channel_id=1, source_target_pairs={{0,6},{2,4},{4,2},{6,0},{8,14},{10,12},{12,10},{14,8},{16,22},{18,... | collective-permute-start | bytes 110600 | tf_op jit(solution)/shard_map/ppermute | solution.py:228
  31.8 4.4 %collective-permute-start.13 = (f32[72,128]{1,0:T(8,128)S(1)}, f32[72,128]{1,0:T(8,128)S(1)}, u32[]{:S(2)}, u32[]{:S(2)}) collective-permute-start(f32[72,128]{1,0:T(8,128)S(1)} %add.18), channel_id=1, source_target_pairs={{0,2},{2,0},{4,6},{6,4},{8,10},{10,8},{12,14},{14,12},{16,18},{18,... | collective-permute-start | bytes 110600 | tf_op jit(solution)/shard_map/ppermute | solution.py:228
  32.7 4.0 %collective-permute-start.12 = (f32[72,128]{1,0:T(8,128)S(1)}, f32[72,128]{1,0:T(8,128)S(1)}, u32[]{:S(2)}, u32[]{:S(2)}) collective-permute-start(f32[72,128]{1,0:T(8,128)S(1)} %add.18), channel_id=1, source_target_pairs={{0,4},{2,6},{4,0},{6,2},{8,12},{10,14},{12,8},{14,10},{16,20},{18,... | collective-permute-start | bytes 110600 | tf_op jit(solution)/shard_map/ppermute | solution.py:228
  36.7 4.2 %collective-permute-start.15 = (f32[72,128]{1,0:T(8,128)S(1)}, f32[72,128]{1,0:T(8,128)S(1)}, u32[]{:S(2)}, u32[]{:S(2)}) collective-permute-start(f32[72,128]{1,0:T(8,128)S(1)} %add_add_fusion), channel_id=1, source_target_pairs={{0,8},{4,12},{8,0},{12,4},{16,24},{20,28},{24,16},{28,20},{1,9},{5... | collective-permute-start | bytes 110600 | tf_op jit(solution)/shard_map/ppermute | solution.py:220
  38.2 5.8 %collective-permute-start.17 = (f32[72,128]{1,0:T(8,128)S(1)}, f32[72,128]{1,0:T(8,128)S(1)}, u32[]{:S(2)}, u32[]{:S(2)}) collective-permute-start(f32[72,128]{1,0:T(8,128)S(1)} %add_add_fusion), channel_id=1, source_target_pairs={{0,24},{4,28},{8,16},{12,20},{16,8},{20,12},{24,0},{28,4},{1,25},{... | collective-permute-start | bytes 110600 | tf_op jit(solution)/shard_map/ppermute | solution.py:220
  39.7 4.9 %collective-permute-start.16 = (f32[72,128]{1,0:T(8,128)S(1)}, f32[72,128]{1,0:T(8,128)S(1)}, u32[]{:S(2)}, u32[]{:S(2)}) collective-permute-start(f32[72,128]{1,0:T(8,128)S(1)} %add_add_fusion), channel_id=1, source_target_pairs={{0,16},{4,20},{8,24},{12,28},{16,0},{20,4},{24,8},{28,12},{1,17},{... | collective-permute-start | bytes 110600 | tf_op jit(solution)/shard_map/ppermute | solution.py:220

commit v6 on v5

--- a/solution.py
+++ b/solution.py
@@ -304,8 +304,8 @@
         if two:
             steps.append(
                 lambda x, one=one, two=two: (
-                    x + swap(x, "row", row_size, one),
-                    swap(x, "row", row_size, two) + swap(x, "row", row_size, one ^ two),
+                    x + swap(x, "row", row_size, one ^ two),
+                    swap(x, "row", row_size, two) + swap(x, "row", row_size, one),
                 )
             )
         else:

time: 45.6 us -> 44.9 us (0.985)
  waiting for transfers between devices: 18.2 us -> 17.2 us
  starting transfers between devices: 19.9 us -> 20.8 us
    ppermute x10, waiting for transfers between devices: 11.2 us -> 10.2 us  [swap(): return lax.ppermute(x, axis, [(i, i ^ bit) for i in range(size)])]
    ppermute x10, starting transfers between devices: 14.3 us -> 15.2 us  [swap(): return lax.ppermute(x, axis, [(i, i ^ bit) for i in range(size)])]
  transfers between devices with their start and end apart: 18 -> 18, of which waited for: 14 -> 15; matrix products, arithmetic and copies ran while one was open for 1% -> 1% of each run, Pallas kernels for 8% -> 8%
where the time goes in v6:
time: 44.9 us; the launch traced here: 44.8 us
  starting transfers between devices  20.8 us (46%)
  waiting for transfers between devices  17.2 us (38%)
  Pallas kernels  4.7 us (10%)
  between operations  1.37 us (3%)
  local copies, waits for them, and re-layouts  0.67 us (1%)
    ppermute x10, starting transfers between devices, swap(): return lax.ppermute(x, axis, [(i, i ^ bit) for i in range(size)])  15.2 us
    ppermute x10, waiting for transfers between devices, swap(): return lax.ppermute(x, axis, [(i, i ^ bit) for i in range(size)])  10.2 us
    ppermute x3, waiting for transfers between devices, shift_two(): return lax.ppermute(x, ('col', 'rep'), perm)  3.71 us
    ppermute x3, starting transfers between devices, swap_two(): return lax.ppermute(x, axes, perm)  3.49 us
    pallas_call x1, Pallas kernels, split_slabs(): call(kernel, outs, [pl.ANY] * len(operands), 'split_slabs', scratch, cost)  2.68 us
    ppermute x3, waiting for transfers between devices, swap_two(): return lax.ppermute(x, axes, perm)  2.2 us
    ppermute x3, starting transfers between devices, shift_two(): return lax.ppermute(x, ('col', 'rep'), perm)  1.93 us
    ppermute x2, waiting for transfers between devices, shift(): return lax.ppermute(x, axis, [(i, (i + k) % size) for i in range(size)])  1.05 us
  transfers between devices with their start and end apart: 18, of which 15 were waited for; matrix products, arithmetic and copies ran while one was open for 1% of the time, Pallas kernels for 8%

profile of v6, /device:TPU:0, one launch (start us, length us, event | category | flops | bytes accessed | tf_op | source)
XLA Modules:
  0.0 44.8 jit_solution(703918585504160497)
XLA Ops:
  0.6 3.0 %collective-permute-start.1 = (f32[64,512]{1,0:T(8,128)}, f32[64,512]{1,0:T(8,128)S(1)}, u32[]{:S(2)}, u32[]{:S(2)}) collective-permute-start(f32[64,512]{1,0:T(8,128)} %refs_0_.1), channel_id=1, source_target_pairs={{0,4},{4,0},{8,12},{12,8},{16,20},{20,16},{24,28},{28,24},{1,5},{5... | collective-permute-start | bytes 393224 | tf_op jit(solution)/shard_map/ppermute | solution.py:220
  3.6 3.6 %collective-permute-start = (f32[64,512]{1,0:T(8,128)}, f32[64,512]{1,0:T(8,128)S(1)}, u32[]{:S(2)}, u32[]{:S(2)}) collective-permute-start(f32[64,512]{1,0:T(8,128)} %refs_0_.1), channel_id=1, source_target_pairs={{0,24},{4,28},{8,16},{12,20},{16,8},{20,12},{24,0},{28,4},{1,25},{... | collective-permute-start | bytes 393224 | tf_op jit(solution)/shard_map/ppermute | solution.py:220
  7.2 2.7 %split_slabs.1 = (bf16[4,512,512]{2,1,0:T(8,128)(2,1)S(1)}, bf16[4,512,512]{2,1,0:T(8,128)(2,1)S(1)}, s32[2,8,128]{2,1,0:T(8,128)S(1)}) custom-call(f32[4,512,512]{2,1,0:T(8,128)} %bitcast.3, s32[1,1,4]{2,1,0:T(1,128)} %rows.1, s32[1,1,4]{2,1,0:T(1,128)} %cols.1), custom_call_target="tpu_custom_call" | custom-call | flops 4194304 | bytes 8388608 | tf_op jit(solution)/shard_map/split_slabs/pallas_call | solution.py:76
  10.0 2.1 %collective-permute-done.refs_1_ = f32[64,512]{1,0:T(8,128)S(1)} collective-permute-done((f32[64,512]{1,0:T(8,128)}, f32[64,512]{1,0:T(8,128)S(1)}, u32[]{:S(2)}, u32[]{:S(2)}) %collective-permute-start) | collective-permute-done | bytes 131104 | tf_op jit(solution)/shard_map/ppermute | solution.py:220
  12.1 1.1 %collective-permute-start.5 = (f32[64,512]{1,0:T(8,128)S(1)}, f32[64,512]{1,0:T(8,128)S(1)}, u32[]{:S(2)}, u32[]{:S(2)}) collective-permute-start(f32[64,512]{1,0:T(8,128)S(1)} %collective-permute-done.refs_1_), channel_id=1, source_target_pairs={{0,8},{4,12},{8,0},{12,4},{16,24},{20,28},{24,16},{28,20},{1,9},{5... | collective-permute-start | bytes 393224 | tf_op jit(solution)/shard_map/ppermute | solution.py:220
  13.8 1.4 %collective-permute-start.4 = (f32[64,512]{1,0:T(8,128)S(1)}, f32[64,512]{1,0:T(8,128)S(1)}, u32[]{:S(2)}, u32[]{:S(2)}) collective-permute-start(f32[64,512]{1,0:T(8,128)S(1)} %copy-done.1), channel_id=1, source_target_pairs={{0,8},{4,12},{8,0},{12,4},{16,24},{20,28},{24,16},{28,20},{1,9},{5... | collective-permute-start | bytes 393224 | tf_op jit(solution)/shard_map/ppermute | solution.py:220
  15.2 1.6 %collective-permute-start.6 = (f32[64,512]{1,0:T(8,128)S(1)}, f32[64,512]{1,0:T(8,128)S(1)}, u32[]{:S(2)}, u32[]{:S(2)}) collective-permute-start(f32[64,512]{1,0:T(8,128)S(1)} %collective-permute-done.refs_1_), channel_id=1, source_target_pairs={{0,4},{4,0},{8,12},{12,8},{16,20},{20,16},{24,28},{28,24},{1,5},{5... | collective-permute-start | bytes 393224 | tf_op jit(solution)/shard_map/ppermute | solution.py:220
  16.8 1.6 %collective-permute-done.5.refs_3_ = f32[64,512]{1,0:T(8,128)S(1)} collective-permute-done((f32[64,512]{1,0:T(8,128)S(1)}, f32[64,512]{1,0:T(8,128)S(1)}, u32[]{:S(2)}, u32[]{:S(2)}) %collective-permute-start.5) | collective-permute-done | bytes 131104 | tf_op jit(solution)/shard_map/ppermute | solution.py:220
  19.0 0.7 %collective-permute-done.4.refs_2_ = f32[64,512]{1,0:T(8,128)S(1)} collective-permute-done((f32[64,512]{1,0:T(8,128)S(1)}, f32[64,512]{1,0:T(8,128)S(1)}, u32[]{:S(2)}, u32[]{:S(2)}) %collective-permute-start.4) | collective-permute-done | bytes 131104 | tf_op jit(solution)/shard_map/ppermute | solution.py:220
  20.4 0.8 %mix_early.1 = (f32[2,64,512]{2,1,0:T(8,128)S(1)}, s32[8,128]{1,0:T(8,128)S(1)}) custom-call(s32[1,1]{1,0:T(1,128)S(6)} %copy.12.counts, s32[2,8,128]{2,1,0:T(8,128)S(1)} %get-tuple-element.29.plan, bf16[4,512,512]{2,1,0:T(8,128)(2,1)S(1)} %get-tuple-element.30.high, bf16[4,512,512]{2,1,0:T(8,128)(2,1)S(1)} %get-tuple-element.31.low, ...), custom_call_target="tpu_custom_call" | custom-call | flops 402653184 | bytes 4194304 | tf_op jit(solution)/shard_map/mix_early/pallas_call | solution.py:148
  21.2 2.2 %collective-permute-done.7.piece = f32[64,512]{1,0:T(8,128)S(1)} collective-permute-done((f32[64,512]{1,0:T(8,128)S(1)}, f32[64,512]{1,0:T(8,128)S(1)}, u32[]{:S(2)}, u32[]{:S(2)}) %collective-permute-start.7) | collective-permute-done | bytes 131104 | tf_op jit(solution)/shard_map/ppermute | solution.py:220
  23.5 1.5 %collective-permute-start.9 = (f32[64,256]{1,0:T(8,128)S(1)}, f32[64,256]{1,0:T(8,128)S(1)}, u32[]{:S(2)}, u32[]{:S(2)}) collective-permute-start(f32[64,256]{1,0:T(8,128)S(1)} %get-tuple-element.40), channel_id=1, source_target_pairs={{0,2},{1,3},{2,0},{3,1},{4,6},{5,7},{6,4},{7,5},{8,10},{9,11},{10,... | collective-permute-start | bytes 196616 | tf_op jit(solution)/shard_map/ppermute | solution.py:216
  25.4 2.6 %collective-permute-done.9.refs_2_ = f32[64,256]{1,0:T(8,128)S(1)} collective-permute-done((f32[64,256]{1,0:T(8,128)S(1)}, f32[64,256]{1,0:T(8,128)S(1)}, u32[]{:S(2)}, u32[]{:S(2)}) %collective-permute-start.9) | collective-permute-done | bytes 65568 | tf_op jit(solution)/shard_map/ppermute | solution.py:216
  28.0 1.1 %collective-permute-done.10.refs_3_ = f32[64,256]{1,0:T(8,128)S(1)} collective-permute-done((f32[64,256]{1,0:T(8,128)S(1)}, f32[64,256]{1,0:T(8,128)S(1)}, u32[]{:S(2)}, u32[]{:S(2)}) %collective-permute-start.10) | collective-permute-done | bytes 65568 | tf_op jit(solution)/shard_map/ppermute | solution.py:216
  29.9 1.0 %collective-permute-done.11 = f32[72,128]{1,0:T(8,128)S(1)} collective-permute-done((f32[72,128]{1,0:T(8,128)S(1)}, f32[72,128]{1,0:T(8,128)S(1)}, u32[]{:S(2)}, u32[]{:S(2)}) %collective-permute-start.11) | collective-permute-done | bytes 36896 | tf_op jit(solution)/shard_map/ppermute | solution.py:208
  31.0 0.9 %collective-permute-start.14 = (f32[72,128]{1,0:T(8,128)S(1)}, f32[72,128]{1,0:T(8,128)S(1)}, u32[]{:S(2)}, u32[]{:S(2)}) collective-permute-start(f32[72,128]{1,0:T(8,128)S(1)} %add.18), channel_id=1, source_target_pairs={{0,6},{2,4},{4,2},{6,0},{8,14},{10,12},{12,10},{14,8},{16,22},{18,... | collective-permute-start | bytes 110600 | tf_op jit(solution)/shard_map/ppermute | solution.py:228
  31.8 0.9 %collective-permute-start.13 = (f32[72,128]{1,0:T(8,128)S(1)}, f32[72,128]{1,0:T(8,128)S(1)}, u32[]{:S(2)}, u32[]{:S(2)}) collective-permute-start(f32[72,128]{1,0:T(8,128)S(1)} %add.18), channel_id=1, source_target_pairs={{0,2},{2,0},{4,6},{6,4},{8,10},{10,8},{12,14},{14,12},{16,18},{18,... | collective-permute-start | bytes 110600 | tf_op jit(solution)/shard_map/ppermute | solution.py:228
  32.7 1.8 %collective-permute-start.12 = (f32[72,128]{1,0:T(8,128)S(1)}, f32[72,128]{1,0:T(8,128)S(1)}, u32[]{:S(2)}, u32[]{:S(2)}) collective-permute-start(f32[72,128]{1,0:T(8,128)S(1)} %add.18), channel_id=1, source_target_pairs={{0,4},{2,6},{4,0},{6,2},{8,12},{10,14},{12,8},{14,10},{16,20},{18,... | collective-permute-start | bytes 110600 | tf_op jit(solution)/shard_map/ppermute | solution.py:228
  34.4 1.5 %collective-permute-done.14 = f32[72,128]{1,0:T(8,128)S(1)} collective-permute-done((f32[72,128]{1,0:T(8,128)S(1)}, f32[72,128]{1,0:T(8,128)S(1)}, u32[]{:S(2)}, u32[]{:S(2)}) %collective-permute-start.14) | collective-permute-done | bytes 36896 | tf_op jit(solution)/shard_map/ppermute | solution.py:228
  36.7 2.6 %collective-permute-start.15 = (f32[72,128]{1,0:T(8,128)S(1)}, f32[72,128]{1,0:T(8,128)S(1)}, u32[]{:S(2)}, u32[]{:S(2)}) collective-permute-start(f32[72,128]{1,0:T(8,128)S(1)} %add_add_fusion), channel_id=1, source_target_pairs={{0,24},{4,28},{8,16},{12,20},{16,8},{20,12},{24,0},{28,4},{1,25},{... | collective-permute-start | bytes 110600 | tf_op jit(solution)/shard_map/ppermute | solution.py:220
  39.3 1.8 %collective-permute-start.16 = (f32[72,128]{1,0:T(8,128)S(1)}, f32[72,128]{1,0:T(8,128)S(1)}, u32[]{:S(2)}, u32[]{:S(2)}) collective-permute-start(f32[72,128]{1,0:T(8,128)S(1)} %add_add_fusion), channel_id=1, source_target_pairs={{0,16},{4,20},{8,24},{12,28},{16,0},{20,4},{24,8},{28,12},{1,17},{... | collective-permute-start | bytes 110600 | tf_op jit(solution)/shard_map/ppermute | solution.py:220
  41.1 0.7 %copy.11 = f32[256,128]{1,0:T(8,128)} copy(f32[256,128]{1,0:T(8,128)S(1)} %get-tuple-element.49) | data formatting | bytes 262144
  41.8 0.8 %collective-permute-done.15 = f32[72,128]{1,0:T(8,128)S(1)} collective-permute-done((f32[72,128]{1,0:T(8,128)S(1)}, f32[72,128]{1,0:T(8,128)S(1)}, u32[]{:S(2)}, u32[]{:S(2)}) %collective-permute-start.15) | collective-permute-done | bytes 36896 | tf_op jit(solution)/shard_map/ppermute | solution.py:220
  43.2 0.9 %collective-permute-done.16 = f32[72,128]{1,0:T(8,128)S(1)} collective-permute-done((f32[72,128]{1,0:T(8,128)S(1)}, f32[72,128]{1,0:T(8,128)S(1)}, u32[]{:S(2)}, u32[]{:S(2)}) %collective-permute-start.16) | collective-permute-done | bytes 36896 | tf_op jit(solution)/shard_map/ppermute | solution.py:220
  (30 shorter events, 4.6 us)
Async XLA Ops:
  0.6 9.3 %collective-permute-start.1 = (f32[64,512]{1,0:T(8,128)}, f32[64,512]{1,0:T(8,128)S(1)}, u32[]{:S(2)}, u32[]{:S(2)}) collective-permute-start(f32[64,512]{1,0:T(8,128)} %refs_0_.1), channel_id=1, source_target_pairs={{0,4},{4,0},{8,12},{12,8},{16,20},{20,16},{24,28},{28,24},{1,5},{5... | collective-permute-start | bytes 393224 | tf_op jit(solution)/shard_map/ppermute | solution.py:220
  3.6 8.4 %collective-permute-start = (f32[64,512]{1,0:T(8,128)}, f32[64,512]{1,0:T(8,128)S(1)}, u32[]{:S(2)}, u32[]{:S(2)}) collective-permute-start(f32[64,512]{1,0:T(8,128)} %refs_0_.1), channel_id=1, source_target_pairs={{0,24},{4,28},{8,16},{12,20},{16,8},{20,12},{24,0},{28,4},{1,25},{... | collective-permute-start | bytes 393224 | tf_op jit(solution)/shard_map/ppermute | solution.py:220
  7.2 6.6 %collective-permute-start.3 = (f32[64,512]{1,0:T(8,128)}, f32[64,512]{1,0:T(8,128)S(1)}, u32[]{:S(2)}, u32[]{:S(2)}) collective-permute-start(f32[64,512]{1,0:T(8,128)} %refs_0_.1), channel_id=1, source_target_pairs={{0,12},{4,8},{8,4},{12,0},{16,28},{20,24},{24,20},{28,16},{1,13},{... | collective-permute-start | bytes 393224 | tf_op jit(solution)/shard_map/ppermute | solution.py:220
  7.2 2.7 %collective-permute-start.2 = (f32[64,128]{1,0:T(8,128)}, f32[64,128]{1,0:T(8,128)S(1)}, u32[]{:S(2)}, u32[]{:S(2)}) collective-permute-start(f32[64,128]{1,0:T(8,128)} %refs_4_), channel_id=1, source_target_pairs={{0,1},{1,0},{2,3},{3,2},{4,5},{5,4},{6,7},{7,6},{8,9},{9,8},{10,11... | collective-permute-start | bytes 98312 | tf_op jit(solution)/shard_map/ppermute | solution.py:208
  7.2 6.6 %copy-start.1 = (f32[64,512]{1,0:T(8,128)S(1)}, f32[64,512]{1,0:T(8,128)}, u32[]{:S(2)}) copy-start(f32[64,512]{1,0:T(8,128)} %refs_0_.1) | copy-start | bytes 393220
  12.1 6.3 %collective-permute-start.5 = (f32[64,512]{1,0:T(8,128)S(1)}, f32[64,512]{1,0:T(8,128)S(1)}, u32[]{:S(2)}, u32[]{:S(2)}) collective-permute-start(f32[64,512]{1,0:T(8,128)S(1)} %collective-permute-done.refs_1_), channel_id=1, source_target_pairs={{0,8},{4,12},{8,0},{12,4},{16,24},{20,28},{24,16},{28,20},{1,9},{5... | collective-permute-start | bytes 393224 | tf_op jit(solution)/shard_map/ppermute | solution.py:220
  13.8 6.0 %collective-permute-start.4 = (f32[64,512]{1,0:T(8,128)S(1)}, f32[64,512]{1,0:T(8,128)S(1)}, u32[]{:S(2)}, u32[]{:S(2)}) collective-permute-start(f32[64,512]{1,0:T(8,128)S(1)} %copy-done.1), channel_id=1, source_target_pairs={{0,8},{4,12},{8,0},{12,4},{16,24},{20,28},{24,16},{28,20},{1,9},{5... | collective-permute-start | bytes 393224 | tf_op jit(solution)/shard_map/ppermute | solution.py:220
  15.2 5.2 %collective-permute-start.6 = (f32[64,512]{1,0:T(8,128)S(1)}, f32[64,512]{1,0:T(8,128)S(1)}, u32[]{:S(2)}, u32[]{:S(2)}) collective-permute-start(f32[64,512]{1,0:T(8,128)S(1)} %collective-permute-done.refs_1_), channel_id=1, source_target_pairs={{0,4},{4,0},{8,12},{12,8},{16,20},{20,16},{24,28},{28,24},{1,5},{5... | collective-permute-start | bytes 393224 | tf_op jit(solution)/shard_map/ppermute | solution.py:220
  18.4 5.0 %collective-permute-start.7 = (f32[64,512]{1,0:T(8,128)S(1)}, f32[64,512]{1,0:T(8,128)S(1)}, u32[]{:S(2)}, u32[]{:S(2)}) collective-permute-start(f32[64,512]{1,0:T(8,128)S(1)} %collective-permute-done.5.refs_3_), channel_id=1, source_target_pairs={{0,4},{4,0},{8,12},{12,8},{16,20},{20,16},{24,28},{28,24},{1,5},{5... | collective-permute-start | bytes 393224 | tf_op jit(solution)/shard_map/ppermute | solution.py:220
  23.3 5.8 %copy-start = (f32[256,128]{1,0:T(8,128)S(1)}, f32[256,128]{1,0:T(8,128)}, u32[]{:S(2)}) copy-start(f32[256,128]{1,0:T(8,128)} %refs_7_.1) | copy-start | bytes 393220
  23.4 5.8 %copy-start.2 = (f32[64,128]{1,0:T(8,128)S(1)}, f32[64,128]{1,0:T(8,128)}, u32[]{:S(2)}) copy-start(f32[64,128]{1,0:T(8,128)} %refs_4_) | copy-start | bytes 98308
  23.4 5.8 %copy-start.3 = (f32[128]{0:T(128)S(1)}, f32[128]{0:T(128)}, u32[]{:S(2)}) copy-start(f32[128]{0:T(128)} %param.14) | copy-start | bytes 1540
  23.5 1.9 %collective-permute-start.8 = (f32[64,256]{1,0:T(8,128)S(1)}, f32[64,256]{1,0:T(8,128)S(1)}, u32[]{:S(2)}, u32[]{:S(2)}) collective-permute-start(f32[64,256]{1,0:T(8,128)S(1)} %get-tuple-element.39), channel_id=1, source_target_pairs={{0,1},{1,0},{2,3},{3,2},{4,5},{5,4},{6,7},{7,6},{8,9},{9,8},{10,11... | collective-permute-start | bytes 196616 | tf_op jit(solution)/shard_map/ppermute | solution.py:216
  23.5 4.5 %collective-permute-start.9 = (f32[64,256]{1,0:T(8,128)S(1)}, f32[64,256]{1,0:T(8,128)S(1)}, u32[]{:S(2)}, u32[]{:S(2)}) collective-permute-start(f32[64,256]{1,0:T(8,128)S(1)} %get-tuple-element.40), channel_id=1, source_target_pairs={{0,2},{1,3},{2,0},{3,1},{4,6},{5,7},{6,4},{7,5},{8,10},{9,11},{10,... | collective-permute-start | bytes 196616 | tf_op jit(solution)/shard_map/ppermute | solution.py:216
  25.1 4.0 %collective-permute-start.10 = (f32[64,256]{1,0:T(8,128)S(1)}, f32[64,256]{1,0:T(8,128)S(1)}, u32[]{:S(2)}, u32[]{:S(2)}) collective-permute-start(f32[64,256]{1,0:T(8,128)S(1)} %get-tuple-element.41), channel_id=1, source_target_pairs={{0,3},{1,2},{2,1},{3,0},{4,7},{5,6},{6,5},{7,4},{8,11},{9,10},{10,... | collective-permute-start | bytes 196616 | tf_op jit(solution)/shard_map/ppermute | solution.py:216
  29.7 1.3 %collective-permute-start.11 = (f32[72,128]{1,0:T(8,128)S(1)}, f32[72,128]{1,0:T(8,128)S(1)}, u32[]{:S(2)}, u32[]{:S(2)}) collective-permute-start(f32[72,128]{1,0:T(8,128)S(1)} %get-tuple-element.46), channel_id=1, source_target_pairs={{0,1},{1,0},{2,3},{3,2},{4,5},{5,4},{6,7},{7,6},{8,9},{9,8},{10,11... | collective-permute-start | bytes 110600 | tf_op jit(solution)/shard_map/ppermute | solution.py:208
  31.0 5.0 %collective-permute-start.14 = (f32[72,128]{1,0:T(8,128)S(1)}, f32[72,128]{1,0:T(8,128)S(1)}, u32[]{:S(2)}, u32[]{:S(2)}) collective-permute-start(f32[72,128]{1,0:T(8,128)S(1)} %add.18), channel_id=1, source_target_pairs={{0,6},{2,4},{4,2},{6,0},{8,14},{10,12},{12,10},{14,8},{16,22},{18,... | collective-permute-start | bytes 110600 | tf_op jit(solution)/shard_map/ppermute | solution.py:228
  31.8 4.4 %collective-permute-start.13 = (f32[72,128]{1,0:T(8,128)S(1)}, f32[72,128]{1,0:T(8,128)S(1)}, u32[]{:S(2)}, u32[]{:S(2)}) collective-permute-start(f32[72,128]{1,0:T(8,128)S(1)} %add.18), channel_id=1, source_target_pairs={{0,2},{2,0},{4,6},{6,4},{8,10},{10,8},{12,14},{14,12},{16,18},{18,... | collective-permute-start | bytes 110600 | tf_op jit(solution)/shard_map/ppermute | solution.py:228
  32.7 4.0 %collective-permute-start.12 = (f32[72,128]{1,0:T(8,128)S(1)}, f32[72,128]{1,0:T(8,128)S(1)}, u32[]{:S(2)}, u32[]{:S(2)}) collective-permute-start(f32[72,128]{1,0:T(8,128)S(1)} %add.18), channel_id=1, source_target_pairs={{0,4},{2,6},{4,0},{6,2},{8,12},{10,14},{12,8},{14,10},{16,20},{18,... | collective-permute-start | bytes 110600 | tf_op jit(solution)/shard_map/ppermute | solution.py:228
  36.7 5.9 %collective-permute-start.15 = (f32[72,128]{1,0:T(8,128)S(1)}, f32[72,128]{1,0:T(8,128)S(1)}, u32[]{:S(2)}, u32[]{:S(2)}) collective-permute-start(f32[72,128]{1,0:T(8,128)S(1)} %add_add_fusion), channel_id=1, source_target_pairs={{0,24},{4,28},{8,16},{12,20},{16,8},{20,12},{24,0},{28,4},{1,25},{... | collective-permute-start | bytes 110600 | tf_op jit(solution)/shard_map/ppermute | solution.py:220
  39.3 4.0 %collective-permute-start.17 = (f32[72,128]{1,0:T(8,128)S(1)}, f32[72,128]{1,0:T(8,128)S(1)}, u32[]{:S(2)}, u32[]{:S(2)}) collective-permute-start(f32[72,128]{1,0:T(8,128)S(1)} %add_add_fusion), channel_id=1, source_target_pairs={{0,8},{4,12},{8,0},{12,4},{16,24},{20,28},{24,16},{28,20},{1,9},{5... | collective-permute-start | bytes 110600 | tf_op jit(solution)/shard_map/ppermute | solution.py:220
  39.3 4.9 %collective-permute-start.16 = (f32[72,128]{1,0:T(8,128)S(1)}, f32[72,128]{1,0:T(8,128)S(1)}, u32[]{:S(2)}, u32[]{:S(2)}) collective-permute-start(f32[72,128]{1,0:T(8,128)S(1)} %add_add_fusion), channel_id=1, source_target_pairs={{0,16},{4,20},{8,24},{12,28},{16,0},{20,4},{24,8},{28,12},{1,17},{... | collective-permute-start | bytes 110600 | tf_op jit(solution)/shard_map/ppermute | solution.py:220

commit v7 on v6

--- a/solution.py
+++ b/solution.py
@@ -163,7 +163,7 @@
 
 
 def node_kernel(groups, halves, *refs):
-    terms, refs = refs[: groups * halves], refs[groups * halves :]
+    terms, refs = refs[: groups * halves][::-1], refs[groups * halves :]
     weights, (bias, cotangent, output, *grads) = refs[:halves], refs[halves:]
     half_width = terms[0].shape[0]
     mixed = [sum(terms[k * halves + h][...] for k in range(groups)) for h in range(halves)]
@@ -189,7 +189,7 @@
         [pltpu.VMEM(cotangent.shape, F32)] + [grad] * halves,
         [pltpu.VMEM] * (len(terms) + halves + 2),
         "node_step",
-    )(*terms, *weights, bias.reshape(1, width), cotangent)
+    )(*terms[::-1], *weights, bias.reshape(1, width), cotangent)
 
 
 def last_kernel(a, b, grad_weight, grad_bias):
@@ -311,8 +311,8 @@
         else:
             steps.append(lambda x, one=one: (x, swap(x, "row", row_size, one)))
     for step in steps[:-1]:
-        a, b = step(grad)
-        grad = a + b
+        terms = step(grad)
+        grad = terms[0] + terms[1]
     return steps[-1](grad)
 
 

time: 44.9 us -> 45.2 us (level)
  transfers between devices with their start and end apart: 18 -> 18, of which waited for: 15 -> 14; matrix products, arithmetic and copies ran while one was open for 1% -> 1% of each run, Pallas kernels for 8% -> 8%
where the time goes in v7:
time: 45.2 us
  starting transfers between devices  20.7 us (46%)
  waiting for transfers between devices  17.4 us (38%)
  Pallas kernels  5 us (11%)
  between operations  1.38 us (3%)
  local copies, waits for them, and re-layouts  0.67 us (1%)
    ppermute x10, starting transfers between devices, swap(): return lax.ppermute(x, axis, [(i, i ^ bit) for i in range(size)])  15.2 us
    ppermute x10, waiting for transfers between devices, swap(): return lax.ppermute(x, axis, [(i, i ^ bit) for i in range(size)])  10.4 us
    ppermute x3, waiting for transfers between devices, shift_two(): return lax.ppermute(x, ('col', 'rep'), perm)  3.94 us
    ppermute x3, starting transfers between devices, swap_two(): return lax.ppermute(x, axes, perm)  3.49 us
    pallas_call x1, Pallas kernels, split_slabs(): call(kernel, outs, [pl.ANY] * len(operands), 'split_slabs', scratch, cost)  2.68 us
    ppermute x3, waiting for transfers between devices, swap_two(): return lax.ppermute(x, axes, perm)  1.93 us
    ppermute x3, starting transfers between devices, shift_two(): return lax.ppermute(x, ('col', 'rep'), perm)  1.92 us
    ppermute x2, waiting for transfers between devices, shift(): return lax.ppermute(x, axis, [(i, (i + k) % size) for i in range(size)])  1.12 us
  transfers between devices with their start and end apart: 18, of which 14 were waited for; matrix products, arithmetic and copies ran while one was open for 1% of the time, Pallas kernels for 8%

profile of v7, /device:TPU:0, one launch (start us, length us, event | category | flops | bytes accessed | tf_op | source)
XLA Modules:
  0.0 45.2 jit_solution(6237309030035713208)
XLA Ops:
  0.6 3.0 %collective-permute-start.1 = (f32[64,512]{1,0:T(8,128)}, f32[64,512]{1,0:T(8,128)S(1)}, u32[]{:S(2)}, u32[]{:S(2)}) collective-permute-start(f32[64,512]{1,0:T(8,128)} %refs_0_.1), channel_id=1, source_target_pairs={{0,4},{4,0},{8,12},{12,8},{16,20},{20,16},{24,28},{28,24},{1,5},{5... | collective-permute-start | bytes 393224 | tf_op jit(solution)/shard_map/ppermute | solution.py:220
  3.6 3.6 %collective-permute-start = (f32[64,512]{1,0:T(8,128)}, f32[64,512]{1,0:T(8,128)S(1)}, u32[]{:S(2)}, u32[]{:S(2)}) collective-permute-start(f32[64,512]{1,0:T(8,128)} %refs_0_.1), channel_id=1, source_target_pairs={{0,24},{4,28},{8,16},{12,20},{16,8},{20,12},{24,0},{28,4},{1,25},{... | collective-permute-start | bytes 393224 | tf_op jit(solution)/shard_map/ppermute | solution.py:220
  7.2 2.7 %split_slabs.1 = (bf16[4,512,512]{2,1,0:T(8,128)(2,1)S(1)}, bf16[4,512,512]{2,1,0:T(8,128)(2,1)S(1)}, s32[2,8,128]{2,1,0:T(8,128)S(1)}) custom-call(f32[4,512,512]{2,1,0:T(8,128)} %bitcast.3, s32[1,1,4]{2,1,0:T(1,128)} %rows.1, s32[1,1,4]{2,1,0:T(1,128)} %cols.1), custom_call_target="tpu_custom_call" | custom-call | flops 4194304 | bytes 8388608 | tf_op jit(solution)/shard_map/split_slabs/pallas_call | solution.py:76
  10.0 2.1 %collective-permute-done.refs_1_ = f32[64,512]{1,0:T(8,128)S(1)} collective-permute-done((f32[64,512]{1,0:T(8,128)}, f32[64,512]{1,0:T(8,128)S(1)}, u32[]{:S(2)}, u32[]{:S(2)}) %collective-permute-start) | collective-permute-done | bytes 131104 | tf_op jit(solution)/shard_map/ppermute | solution.py:220
  12.1 1.1 %collective-permute-start.5 = (f32[64,512]{1,0:T(8,128)S(1)}, f32[64,512]{1,0:T(8,128)S(1)}, u32[]{:S(2)}, u32[]{:S(2)}) collective-permute-start(f32[64,512]{1,0:T(8,128)S(1)} %collective-permute-done.refs_1_), channel_id=1, source_target_pairs={{0,8},{4,12},{8,0},{12,4},{16,24},{20,28},{24,16},{28,20},{1,9},{5... | collective-permute-start | bytes 393224 | tf_op jit(solution)/shard_map/ppermute | solution.py:220
  13.8 1.4 %collective-permute-start.4 = (f32[64,512]{1,0:T(8,128)S(1)}, f32[64,512]{1,0:T(8,128)S(1)}, u32[]{:S(2)}, u32[]{:S(2)}) collective-permute-start(f32[64,512]{1,0:T(8,128)S(1)} %copy-done.1), channel_id=1, source_target_pairs={{0,8},{4,12},{8,0},{12,4},{16,24},{20,28},{24,16},{28,20},{1,9},{5... | collective-permute-start | bytes 393224 | tf_op jit(solution)/shard_map/ppermute | solution.py:220
  15.2 1.6 %collective-permute-start.6 = (f32[64,512]{1,0:T(8,128)S(1)}, f32[64,512]{1,0:T(8,128)S(1)}, u32[]{:S(2)}, u32[]{:S(2)}) collective-permute-start(f32[64,512]{1,0:T(8,128)S(1)} %collective-permute-done.refs_1_), channel_id=1, source_target_pairs={{0,4},{4,0},{8,12},{12,8},{16,20},{20,16},{24,28},{28,24},{1,5},{5... | collective-permute-start | bytes 393224 | tf_op jit(solution)/shard_map/ppermute | solution.py:220
  16.8 1.6 %collective-permute-done.5.refs_3_ = f32[64,512]{1,0:T(8,128)S(1)} collective-permute-done((f32[64,512]{1,0:T(8,128)S(1)}, f32[64,512]{1,0:T(8,128)S(1)}, u32[]{:S(2)}, u32[]{:S(2)}) %collective-permute-start.5) | collective-permute-done | bytes 131104 | tf_op jit(solution)/shard_map/ppermute | solution.py:220
  19.0 0.7 %collective-permute-done.4.refs_2_ = f32[64,512]{1,0:T(8,128)S(1)} collective-permute-done((f32[64,512]{1,0:T(8,128)S(1)}, f32[64,512]{1,0:T(8,128)S(1)}, u32[]{:S(2)}, u32[]{:S(2)}) %collective-permute-start.4) | collective-permute-done | bytes 131104 | tf_op jit(solution)/shard_map/ppermute | solution.py:220
  20.4 1.1 %mix_early.1 = (f32[2,64,512]{2,1,0:T(8,128)S(1)}, s32[8,128]{1,0:T(8,128)S(1)}) custom-call(s32[1,1]{1,0:T(1,128)S(6)} %copy.12.counts, s32[2,8,128]{2,1,0:T(8,128)S(1)} %get-tuple-element.29.plan, bf16[4,512,512]{2,1,0:T(8,128)(2,1)S(1)} %get-tuple-element.30.high, bf16[4,512,512]{2,1,0:T(8,128)(2,1)S(1)} %get-tuple-element.31.low, ...), custom_call_target="tpu_custom_call" | custom-call | flops 402653184 | bytes 4194304 | tf_op jit(solution)/shard_map/mix_early/pallas_call | solution.py:148
  21.5 1.9 %collective-permute-done.7.piece = f32[64,512]{1,0:T(8,128)S(1)} collective-permute-done((f32[64,512]{1,0:T(8,128)S(1)}, f32[64,512]{1,0:T(8,128)S(1)}, u32[]{:S(2)}, u32[]{:S(2)}) %collective-permute-start.7) | collective-permute-done | bytes 131104 | tf_op jit(solution)/shard_map/ppermute | solution.py:220
  23.5 1.5 %collective-permute-start.9 = (f32[64,256]{1,0:T(8,128)S(1)}, f32[64,256]{1,0:T(8,128)S(1)}, u32[]{:S(2)}, u32[]{:S(2)}) collective-permute-start(f32[64,256]{1,0:T(8,128)S(1)} %get-tuple-element.39), channel_id=1, source_target_pairs={{0,2},{1,3},{2,0},{3,1},{4,6},{5,7},{6,4},{7,5},{8,10},{9,11},{10,... | collective-permute-start | bytes 196616 | tf_op jit(solution)/shard_map/ppermute | solution.py:216
  25.4 2.5 %collective-permute-done.8.refs_0_ = f32[64,256]{1,0:T(8,128)S(1)} collective-permute-done((f32[64,256]{1,0:T(8,128)S(1)}, f32[64,256]{1,0:T(8,128)S(1)}, u32[]{:S(2)}, u32[]{:S(2)}) %collective-permute-start.8) | collective-permute-done | bytes 65568 | tf_op jit(solution)/shard_map/ppermute | solution.py:216
  27.9 1.4 %collective-permute-done.9.refs_1_ = f32[64,256]{1,0:T(8,128)S(1)} collective-permute-done((f32[64,256]{1,0:T(8,128)S(1)}, f32[64,256]{1,0:T(8,128)S(1)}, u32[]{:S(2)}, u32[]{:S(2)}) %collective-permute-start.9) | collective-permute-done | bytes 65568 | tf_op jit(solution)/shard_map/ppermute | solution.py:216
  30.0 1.1 %collective-permute-done.11 = f32[72,128]{1,0:T(8,128)S(1)} collective-permute-done((f32[72,128]{1,0:T(8,128)S(1)}, f32[72,128]{1,0:T(8,128)S(1)}, u32[]{:S(2)}, u32[]{:S(2)}) %collective-permute-start.11) | collective-permute-done | bytes 36896 | tf_op jit(solution)/shard_map/ppermute | solution.py:208
  31.3 1.1 %collective-permute-start.13 = (f32[72,128]{1,0:T(8,128)S(1)}, f32[72,128]{1,0:T(8,128)S(1)}, u32[]{:S(2)}, u32[]{:S(2)}) collective-permute-start(f32[72,128]{1,0:T(8,128)S(1)} %add.18), channel_id=1, source_target_pairs={{0,2},{2,0},{4,6},{6,4},{8,10},{10,8},{12,14},{14,12},{16,18},{18,... | collective-permute-start | bytes 110600 | tf_op jit(solution)/shard_map/ppermute | solution.py:228
  32.5 2.2 %collective-permute-start.12 = (f32[72,128]{1,0:T(8,128)S(1)}, f32[72,128]{1,0:T(8,128)S(1)}, u32[]{:S(2)}, u32[]{:S(2)}) collective-permute-start(f32[72,128]{1,0:T(8,128)S(1)} %add.18), channel_id=1, source_target_pairs={{0,4},{2,6},{4,0},{6,2},{8,12},{10,14},{12,8},{14,10},{16,20},{18,... | collective-permute-start | bytes 110600 | tf_op jit(solution)/shard_map/ppermute | solution.py:228
  34.7 1.4 %collective-permute-done.14 = f32[72,128]{1,0:T(8,128)S(1)} collective-permute-done((f32[72,128]{1,0:T(8,128)S(1)}, f32[72,128]{1,0:T(8,128)S(1)}, u32[]{:S(2)}, u32[]{:S(2)}) %collective-permute-start.14) | collective-permute-done | bytes 36896 | tf_op jit(solution)/shard_map/ppermute | solution.py:228
  36.6 3.1 %collective-permute-start.15 = (f32[72,128]{1,0:T(8,128)S(1)}, f32[72,128]{1,0:T(8,128)S(1)}, u32[]{:S(2)}, u32[]{:S(2)}) collective-permute-start(f32[72,128]{1,0:T(8,128)S(1)} %add_add_fusion), channel_id=1, source_target_pairs={{0,24},{4,28},{8,16},{12,20},{16,8},{20,12},{24,0},{28,4},{1,25},{... | collective-permute-start | bytes 110600 | tf_op jit(solution)/shard_map/ppermute | solution.py:220
  39.7 1.3 %collective-permute-start.16 = (f32[72,128]{1,0:T(8,128)S(1)}, f32[72,128]{1,0:T(8,128)S(1)}, u32[]{:S(2)}, u32[]{:S(2)}) collective-permute-start(f32[72,128]{1,0:T(8,128)S(1)} %add_add_fusion), channel_id=1, source_target_pairs={{0,16},{4,20},{8,24},{12,28},{16,0},{20,4},{24,8},{28,12},{1,17},{... | collective-permute-start | bytes 110600 | tf_op jit(solution)/shard_map/ppermute | solution.py:220
  41.1 0.7 %copy.11 = f32[256,128]{1,0:T(8,128)} copy(f32[256,128]{1,0:T(8,128)S(1)} %get-tuple-element.49) | data formatting | bytes 262144
  41.7 0.8 %collective-permute-done.15 = f32[72,128]{1,0:T(8,128)S(1)} collective-permute-done((f32[72,128]{1,0:T(8,128)S(1)}, f32[72,128]{1,0:T(8,128)S(1)}, u32[]{:S(2)}, u32[]{:S(2)}) %collective-permute-start.15) | collective-permute-done | bytes 36896 | tf_op jit(solution)/shard_map/ppermute | solution.py:220
  42.5 1.2 %collective-permute-done.17 = f32[72,128]{1,0:T(8,128)S(1)} collective-permute-done((f32[72,128]{1,0:T(8,128)S(1)}, f32[72,128]{1,0:T(8,128)S(1)}, u32[]{:S(2)}, u32[]{:S(2)}) %collective-permute-start.17) | collective-permute-done | bytes 36896 | tf_op jit(solution)/shard_map/ppermute | solution.py:220
  43.7 0.9 %collective-permute-done.16 = f32[72,128]{1,0:T(8,128)S(1)} collective-permute-done((f32[72,128]{1,0:T(8,128)S(1)}, f32[72,128]{1,0:T(8,128)S(1)}, u32[]{:S(2)}, u32[]{:S(2)}) %collective-permute-start.16) | collective-permute-done | bytes 36896 | tf_op jit(solution)/shard_map/ppermute | solution.py:220
  (30 shorter events, 3.8 us)
Async XLA Ops:
  0.6 9.3 %collective-permute-start.1 = (f32[64,512]{1,0:T(8,128)}, f32[64,512]{1,0:T(8,128)S(1)}, u32[]{:S(2)}, u32[]{:S(2)}) collective-permute-start(f32[64,512]{1,0:T(8,128)} %refs_0_.1), channel_id=1, source_target_pairs={{0,4},{4,0},{8,12},{12,8},{16,20},{20,16},{24,28},{28,24},{1,5},{5... | collective-permute-start | bytes 393224 | tf_op jit(solution)/shard_map/ppermute | solution.py:220
  3.6 8.4 %collective-permute-start = (f32[64,512]{1,0:T(8,128)}, f32[64,512]{1,0:T(8,128)S(1)}, u32[]{:S(2)}, u32[]{:S(2)}) collective-permute-start(f32[64,512]{1,0:T(8,128)} %refs_0_.1), channel_id=1, source_target_pairs={{0,24},{4,28},{8,16},{12,20},{16,8},{20,12},{24,0},{28,4},{1,25},{... | collective-permute-start | bytes 393224 | tf_op jit(solution)/shard_map/ppermute | solution.py:220
  7.2 6.6 %collective-permute-start.3 = (f32[64,512]{1,0:T(8,128)}, f32[64,512]{1,0:T(8,128)S(1)}, u32[]{:S(2)}, u32[]{:S(2)}) collective-permute-start(f32[64,512]{1,0:T(8,128)} %refs_0_.1), channel_id=1, source_target_pairs={{0,12},{4,8},{8,4},{12,0},{16,28},{20,24},{24,20},{28,16},{1,13},{... | collective-permute-start | bytes 393224 | tf_op jit(solution)/shard_map/ppermute | solution.py:220
  7.2 2.7 %collective-permute-start.2 = (f32[64,128]{1,0:T(8,128)}, f32[64,128]{1,0:T(8,128)S(1)}, u32[]{:S(2)}, u32[]{:S(2)}) collective-permute-start(f32[64,128]{1,0:T(8,128)} %refs_4_), channel_id=1, source_target_pairs={{0,1},{1,0},{2,3},{3,2},{4,5},{5,4},{6,7},{7,6},{8,9},{9,8},{10,11... | collective-permute-start | bytes 98312 | tf_op jit(solution)/shard_map/ppermute | solution.py:208
  7.2 6.6 %copy-start.1 = (f32[64,512]{1,0:T(8,128)S(1)}, f32[64,512]{1,0:T(8,128)}, u32[]{:S(2)}) copy-start(f32[64,512]{1,0:T(8,128)} %refs_0_.1) | copy-start | bytes 393220
  12.1 6.3 %collective-permute-start.5 = (f32[64,512]{1,0:T(8,128)S(1)}, f32[64,512]{1,0:T(8,128)S(1)}, u32[]{:S(2)}, u32[]{:S(2)}) collective-permute-start(f32[64,512]{1,0:T(8,128)S(1)} %collective-permute-done.refs_1_), channel_id=1, source_target_pairs={{0,8},{4,12},{8,0},{12,4},{16,24},{20,28},{24,16},{28,20},{1,9},{5... | collective-permute-start | bytes 393224 | tf_op jit(solution)/shard_map/ppermute | solution.py:220
  13.8 6.0 %collective-permute-start.4 = (f32[64,512]{1,0:T(8,128)S(1)}, f32[64,512]{1,0:T(8,128)S(1)}, u32[]{:S(2)}, u32[]{:S(2)}) collective-permute-start(f32[64,512]{1,0:T(8,128)S(1)} %copy-done.1), channel_id=1, source_target_pairs={{0,8},{4,12},{8,0},{12,4},{16,24},{20,28},{24,16},{28,20},{1,9},{5... | collective-permute-start | bytes 393224 | tf_op jit(solution)/shard_map/ppermute | solution.py:220
  15.2 5.2 %collective-permute-start.6 = (f32[64,512]{1,0:T(8,128)S(1)}, f32[64,512]{1,0:T(8,128)S(1)}, u32[]{:S(2)}, u32[]{:S(2)}) collective-permute-start(f32[64,512]{1,0:T(8,128)S(1)} %collective-permute-done.refs_1_), channel_id=1, source_target_pairs={{0,4},{4,0},{8,12},{12,8},{16,20},{20,16},{24,28},{28,24},{1,5},{5... | collective-permute-start | bytes 393224 | tf_op jit(solution)/shard_map/ppermute | solution.py:220
  18.4 5.0 %collective-permute-start.7 = (f32[64,512]{1,0:T(8,128)S(1)}, f32[64,512]{1,0:T(8,128)S(1)}, u32[]{:S(2)}, u32[]{:S(2)}) collective-permute-start(f32[64,512]{1,0:T(8,128)S(1)} %collective-permute-done.5.refs_3_), channel_id=1, source_target_pairs={{0,4},{4,0},{8,12},{12,8},{16,20},{20,16},{24,28},{28,24},{1,5},{5... | collective-permute-start | bytes 393224 | tf_op jit(solution)/shard_map/ppermute | solution.py:220
  23.3 6.0 %copy-start = (f32[256,128]{1,0:T(8,128)S(1)}, f32[256,128]{1,0:T(8,128)}, u32[]{:S(2)}) copy-start(f32[256,128]{1,0:T(8,128)} %refs_7_.1) | copy-start | bytes 393220
  23.4 6.0 %copy-start.2 = (f32[64,128]{1,0:T(8,128)S(1)}, f32[64,128]{1,0:T(8,128)}, u32[]{:S(2)}) copy-start(f32[64,128]{1,0:T(8,128)} %refs_4_) | copy-start | bytes 98308
  23.4 6.0 %copy-start.3 = (f32[128]{0:T(128)S(1)}, f32[128]{0:T(128)}, u32[]{:S(2)}) copy-start(f32[128]{0:T(128)} %param.14) | copy-start | bytes 1540
  23.5 4.4 %collective-permute-start.8 = (f32[64,256]{1,0:T(8,128)S(1)}, f32[64,256]{1,0:T(8,128)S(1)}, u32[]{:S(2)}, u32[]{:S(2)}) collective-permute-start(f32[64,256]{1,0:T(8,128)S(1)} %get-tuple-element.38), channel_id=1, source_target_pairs={{0,3},{1,2},{2,1},{3,0},{4,7},{5,6},{6,5},{7,4},{8,11},{9,10},{10,... | collective-permute-start | bytes 196616 | tf_op jit(solution)/shard_map/ppermute | solution.py:216
  23.5 5.8 %collective-permute-start.9 = (f32[64,256]{1,0:T(8,128)S(1)}, f32[64,256]{1,0:T(8,128)S(1)}, u32[]{:S(2)}, u32[]{:S(2)}) collective-permute-start(f32[64,256]{1,0:T(8,128)S(1)} %get-tuple-element.39), channel_id=1, source_target_pairs={{0,2},{1,3},{2,0},{3,1},{4,6},{5,7},{6,4},{7,5},{8,10},{9,11},{10,... | collective-permute-start | bytes 196616 | tf_op jit(solution)/shard_map/ppermute | solution.py:216
  25.1 4.3 %collective-permute-start.10 = (f32[64,256]{1,0:T(8,128)S(1)}, f32[64,256]{1,0:T(8,128)S(1)}, u32[]{:S(2)}, u32[]{:S(2)}) collective-permute-start(f32[64,256]{1,0:T(8,128)S(1)} %get-tuple-element.40), channel_id=1, source_target_pairs={{0,1},{1,0},{2,3},{3,2},{4,5},{5,4},{6,7},{7,6},{8,9},{9,8},{10,11... | collective-permute-start | bytes 196616 | tf_op jit(solution)/shard_map/ppermute | solution.py:216
  29.9 1.3 %collective-permute-start.11 = (f32[72,128]{1,0:T(8,128)S(1)}, f32[72,128]{1,0:T(8,128)S(1)}, u32[]{:S(2)}, u32[]{:S(2)}) collective-permute-start(f32[72,128]{1,0:T(8,128)S(1)} %get-tuple-element.46), channel_id=1, source_target_pairs={{0,1},{1,0},{2,3},{3,2},{4,5},{5,4},{6,7},{7,6},{8,9},{9,8},{10,11... | collective-permute-start | bytes 110600 | tf_op jit(solution)/shard_map/ppermute | solution.py:208
  31.2 4.9 %collective-permute-start.14 = (f32[72,128]{1,0:T(8,128)S(1)}, f32[72,128]{1,0:T(8,128)S(1)}, u32[]{:S(2)}, u32[]{:S(2)}) collective-permute-start(f32[72,128]{1,0:T(8,128)S(1)} %add.18), channel_id=1, source_target_pairs={{0,6},{2,4},{4,2},{6,0},{8,14},{10,12},{12,10},{14,8},{16,22},{18,... | collective-permute-start | bytes 110600 | tf_op jit(solution)/shard_map/ppermute | solution.py:228
  31.3 4.7 %collective-permute-start.13 = (f32[72,128]{1,0:T(8,128)S(1)}, f32[72,128]{1,0:T(8,128)S(1)}, u32[]{:S(2)}, u32[]{:S(2)}) collective-permute-start(f32[72,128]{1,0:T(8,128)S(1)} %add.18), channel_id=1, source_target_pairs={{0,2},{2,0},{4,6},{6,4},{8,10},{10,8},{12,14},{14,12},{16,18},{18,... | collective-permute-start | bytes 110600 | tf_op jit(solution)/shard_map/ppermute | solution.py:228
  32.5 4.1 %collective-permute-start.12 = (f32[72,128]{1,0:T(8,128)S(1)}, f32[72,128]{1,0:T(8,128)S(1)}, u32[]{:S(2)}, u32[]{:S(2)}) collective-permute-start(f32[72,128]{1,0:T(8,128)S(1)} %add.18), channel_id=1, source_target_pairs={{0,4},{2,6},{4,0},{6,2},{8,12},{10,14},{12,8},{14,10},{16,20},{18,... | collective-permute-start | bytes 110600 | tf_op jit(solution)/shard_map/ppermute | solution.py:228
  36.6 5.9 %collective-permute-start.15 = (f32[72,128]{1,0:T(8,128)S(1)}, f32[72,128]{1,0:T(8,128)S(1)}, u32[]{:S(2)}, u32[]{:S(2)}) collective-permute-start(f32[72,128]{1,0:T(8,128)S(1)} %add_add_fusion), channel_id=1, source_target_pairs={{0,24},{4,28},{8,16},{12,20},{16,8},{20,12},{24,0},{28,4},{1,25},{... | collective-permute-start | bytes 110600 | tf_op jit(solution)/shard_map/ppermute | solution.py:220
  39.7 4.0 %collective-permute-start.17 = (f32[72,128]{1,0:T(8,128)S(1)}, f32[72,128]{1,0:T(8,128)S(1)}, u32[]{:S(2)}, u32[]{:S(2)}) collective-permute-start(f32[72,128]{1,0:T(8,128)S(1)} %add_add_fusion), channel_id=1, source_target_pairs={{0,8},{4,12},{8,0},{12,4},{16,24},{20,28},{24,16},{28,20},{1,9},{5... | collective-permute-start | bytes 110600 | tf_op jit(solution)/shard_map/ppermute | solution.py:220
  39.7 4.9 %collective-permute-start.16 = (f32[72,128]{1,0:T(8,128)S(1)}, f32[72,128]{1,0:T(8,128)S(1)}, u32[]{:S(2)}, u32[]{:S(2)}) collective-permute-start(f32[72,128]{1,0:T(8,128)S(1)} %add_add_fusion), channel_id=1, source_target_pairs={{0,16},{4,20},{8,24},{12,28},{16,0},{20,4},{24,8},{28,12},{1,17},{... | collective-permute-start | bytes 110600 | tf_op jit(solution)/shard_map/ppermute | solution.py:220

commit v8 on v7

--- a/solution.py
+++ b/solution.py
@@ -176,14 +176,15 @@
     bias_term = jnp.sum(slope, axis=0, keepdims=True)
     product = dot_split(mixed, split(slope), ((1,), (0,)))
     for h, grad in enumerate(grads):
-        grad[:half_width] = product[h * half_width : (h + 1) * half_width]
-        grad[half_width:] = jnp.broadcast_to(bias_term, (SUBLANES, bias_term.shape[1]))
+        rows = product[h * half_width : (h + 1) * half_width]
+        grad[:half_width] = rows.reshape(half_width, 1, rows.shape[1])
+        grad[half_width] = bias_term
 
 
 def node_step(sizes, terms, weights, bias, cotangent):
     groups, halves = sizes
     width = cotangent.shape[1]
-    grad = pltpu.VMEM((terms[0].shape[0] + SUBLANES, width), F32)
+    grad = pltpu.VMEM((terms[0].shape[0] + 1, 1, width), F32)
     return call(
         functools.partial(node_kernel, groups, halves),
         [pltpu.VMEM(cotangent.shape, F32)] + [grad] * halves,
@@ -194,12 +195,13 @@
 
 def last_kernel(a, b, grad_weight, grad_bias):
     half_width = grad_weight.shape[0]
-    grad_weight[...] = a[:half_width] + b[:half_width]
-    grad_bias[...] = a[half_width] + b[half_width]
+    total = a[...] + b[...]
+    grad_weight[...] = total[:half_width].reshape(grad_weight.shape)
+    grad_bias[...] = total[half_width, 0]
 
 
 def last_step(a, b):
-    half_width, width = a.shape[0] - SUBLANES, a.shape[1]
+    half_width, width = a.shape[0] - 1, a.shape[2]
     out = [jax.ShapeDtypeStruct((half_width, width), F32), jax.ShapeDtypeStruct((width,), F32)]
     return call(last_kernel, out, [pltpu.VMEM] * 2, "last_step")(a, b)
 

time: 45.2 us -> 45.4 us (level)
  transfers between devices with their start and end apart: 18 -> 18, of which waited for: 14 -> 14; matrix products, arithmetic and copies ran while one was open for 1% -> 2% of each run, Pallas kernels for 8% -> 9%
where the time goes in v8:
time: 45.4 us
  starting transfers between devices  20.8 us (46%)
  waiting for transfers between devices  17 us (37%)
  Pallas kernels  5.35 us (12%)
  between operations  1.39 us (3%)
  local copies, waits for them, and re-layouts  0.67 us (1%)
    ppermute x10, starting transfers between devices, swap(): return lax.ppermute(x, axis, [(i, i ^ bit) for i in range(size)])  15.2 us
    ppermute x10, waiting for transfers between devices, swap(): return lax.ppermute(x, axis, [(i, i ^ bit) for i in range(size)])  10 us
    ppermute x3, waiting for transfers between devices, shift_two(): return lax.ppermute(x, ('col', 'rep'), perm)  3.94 us
    ppermute x3, starting transfers between devices, swap_two(): return lax.ppermute(x, axes, perm)  3.55 us
    pallas_call x1, Pallas kernels, split_slabs(): call(kernel, outs, [pl.ANY] * len(operands), 'split_slabs', scratch, cost)  2.68 us
    ppermute x3, starting transfers between devices, shift_two(): return lax.ppermute(x, ('col', 'rep'), perm)  1.92 us
    ppermute x3, waiting for transfers between devices, swap_two(): return lax.ppermute(x, axes, perm)  1.9 us
    pallas_call x1, Pallas kernels, mix(): call(functools.partial(early_kernel, bases), [pltpu.VMEM((groups, half_wi...  1.38 us
  transfers between devices with their start and end apart: 18, of which 14 were waited for; matrix products, arithmetic and copies ran while one was open for 2% of the time, Pallas kernels for 9%

profile of v8, /device:TPU:0, one launch (start us, length us, event | category | flops | bytes accessed | tf_op | source)
XLA Modules:
  0.0 45.4 jit_solution(2805339652596796326)
XLA Ops:
  0.6 3.0 %collective-permute-start.1 = (f32[64,512]{1,0:T(8,128)}, f32[64,512]{1,0:T(8,128)S(1)}, u32[]{:S(2)}, u32[]{:S(2)}) collective-permute-start(f32[64,512]{1,0:T(8,128)} %refs_0_.1), channel_id=1, source_target_pairs={{0,4},{4,0},{8,12},{12,8},{16,20},{20,16},{24,28},{28,24},{1,5},{5... | collective-permute-start | bytes 393224 | tf_op jit(solution)/shard_map/ppermute | solution.py:222
  3.6 3.6 %collective-permute-start = (f32[64,512]{1,0:T(8,128)}, f32[64,512]{1,0:T(8,128)S(1)}, u32[]{:S(2)}, u32[]{:S(2)}) collective-permute-start(f32[64,512]{1,0:T(8,128)} %refs_0_.1), channel_id=1, source_target_pairs={{0,24},{4,28},{8,16},{12,20},{16,8},{20,12},{24,0},{28,4},{1,25},{... | collective-permute-start | bytes 393224 | tf_op jit(solution)/shard_map/ppermute | solution.py:222
  7.2 2.7 %split_slabs.1 = (bf16[4,512,512]{2,1,0:T(8,128)(2,1)S(1)}, bf16[4,512,512]{2,1,0:T(8,128)(2,1)S(1)}, s32[2,8,128]{2,1,0:T(8,128)S(1)}) custom-call(f32[4,512,512]{2,1,0:T(8,128)} %bitcast.3, s32[1,1,4]{2,1,0:T(1,128)} %rows.1, s32[1,1,4]{2,1,0:T(1,128)} %cols.1), custom_call_target="tpu_custom_call" | custom-call | flops 4194304 | bytes 8388608 | tf_op jit(solution)/shard_map/split_slabs/pallas_call | solution.py:76
  10.0 2.1 %collective-permute-done.refs_1_ = f32[64,512]{1,0:T(8,128)S(1)} collective-permute-done((f32[64,512]{1,0:T(8,128)}, f32[64,512]{1,0:T(8,128)S(1)}, u32[]{:S(2)}, u32[]{:S(2)}) %collective-permute-start) | collective-permute-done | bytes 131104 | tf_op jit(solution)/shard_map/ppermute | solution.py:222
  12.1 1.1 %collective-permute-start.5 = (f32[64,512]{1,0:T(8,128)S(1)}, f32[64,512]{1,0:T(8,128)S(1)}, u32[]{:S(2)}, u32[]{:S(2)}) collective-permute-start(f32[64,512]{1,0:T(8,128)S(1)} %collective-permute-done.refs_1_), channel_id=1, source_target_pairs={{0,8},{4,12},{8,0},{12,4},{16,24},{20,28},{24,16},{28,20},{1,9},{5... | collective-permute-start | bytes 393224 | tf_op jit(solution)/shard_map/ppermute | solution.py:222
  13.8 1.4 %collective-permute-start.4 = (f32[64,512]{1,0:T(8,128)S(1)}, f32[64,512]{1,0:T(8,128)S(1)}, u32[]{:S(2)}, u32[]{:S(2)}) collective-permute-start(f32[64,512]{1,0:T(8,128)S(1)} %copy-done.1), channel_id=1, source_target_pairs={{0,8},{4,12},{8,0},{12,4},{16,24},{20,28},{24,16},{28,20},{1,9},{5... | collective-permute-start | bytes 393224 | tf_op jit(solution)/shard_map/ppermute | solution.py:222
  15.2 1.6 %collective-permute-start.6 = (f32[64,512]{1,0:T(8,128)S(1)}, f32[64,512]{1,0:T(8,128)S(1)}, u32[]{:S(2)}, u32[]{:S(2)}) collective-permute-start(f32[64,512]{1,0:T(8,128)S(1)} %collective-permute-done.refs_1_), channel_id=1, source_target_pairs={{0,4},{4,0},{8,12},{12,8},{16,20},{20,16},{24,28},{28,24},{1,5},{5... | collective-permute-start | bytes 393224 | tf_op jit(solution)/shard_map/ppermute | solution.py:222
  16.8 1.6 %collective-permute-done.5.refs_3_ = f32[64,512]{1,0:T(8,128)S(1)} collective-permute-done((f32[64,512]{1,0:T(8,128)S(1)}, f32[64,512]{1,0:T(8,128)S(1)}, u32[]{:S(2)}, u32[]{:S(2)}) %collective-permute-start.5) | collective-permute-done | bytes 131104 | tf_op jit(solution)/shard_map/ppermute | solution.py:222
  19.0 0.7 %collective-permute-done.4.refs_2_ = f32[64,512]{1,0:T(8,128)S(1)} collective-permute-done((f32[64,512]{1,0:T(8,128)S(1)}, f32[64,512]{1,0:T(8,128)S(1)}, u32[]{:S(2)}, u32[]{:S(2)}) %collective-permute-start.4) | collective-permute-done | bytes 131104 | tf_op jit(solution)/shard_map/ppermute | solution.py:222
  20.4 1.4 %mix_early.1 = (f32[2,64,512]{2,1,0:T(8,128)S(1)}, s32[8,128]{1,0:T(8,128)S(1)}) custom-call(s32[1,1]{1,0:T(1,128)S(6)} %copy.12.counts, s32[2,8,128]{2,1,0:T(8,128)S(1)} %get-tuple-element.29.plan, bf16[4,512,512]{2,1,0:T(8,128)(2,1)S(1)} %get-tuple-element.30.high, bf16[4,512,512]{2,1,0:T(8,128)(2,1)S(1)} %get-tuple-element.31.low, ...), custom_call_target="tpu_custom_call" | custom-call | flops 402653184 | bytes 4194304 | tf_op jit(solution)/shard_map/mix_early/pallas_call | solution.py:148
  21.8 1.6 %collective-permute-done.7.piece = f32[64,512]{1,0:T(8,128)S(1)} collective-permute-done((f32[64,512]{1,0:T(8,128)S(1)}, f32[64,512]{1,0:T(8,128)S(1)}, u32[]{:S(2)}, u32[]{:S(2)}) %collective-permute-start.7) | collective-permute-done | bytes 131104 | tf_op jit(solution)/shard_map/ppermute | solution.py:222
  23.5 1.5 %collective-permute-start.9 = (f32[64,256]{1,0:T(8,128)S(1)}, f32[64,256]{1,0:T(8,128)S(1)}, u32[]{:S(2)}, u32[]{:S(2)}) collective-permute-start(f32[64,256]{1,0:T(8,128)S(1)} %get-tuple-element.39), channel_id=1, source_target_pairs={{0,2},{1,3},{2,0},{3,1},{4,6},{5,7},{6,4},{7,5},{8,10},{9,11},{10,... | collective-permute-start | bytes 196616 | tf_op jit(solution)/shard_map/ppermute | solution.py:218
  25.4 2.5 %collective-permute-done.8.refs_0_ = f32[64,256]{1,0:T(8,128)S(1)} collective-permute-done((f32[64,256]{1,0:T(8,128)S(1)}, f32[64,256]{1,0:T(8,128)S(1)}, u32[]{:S(2)}, u32[]{:S(2)}) %collective-permute-start.8) | collective-permute-done | bytes 65568 | tf_op jit(solution)/shard_map/ppermute | solution.py:218
  27.9 1.4 %collective-permute-done.9.refs_1_ = f32[64,256]{1,0:T(8,128)S(1)} collective-permute-done((f32[64,256]{1,0:T(8,128)S(1)}, f32[64,256]{1,0:T(8,128)S(1)}, u32[]{:S(2)}, u32[]{:S(2)}) %collective-permute-start.9) | collective-permute-done | bytes 65568 | tf_op jit(solution)/shard_map/ppermute | solution.py:218
  30.1 1.1 %collective-permute-done.11 = f32[65,1,128]{2,1,0:T(1,128)S(1)} collective-permute-done((f32[65,1,128]{2,1,0:T(1,128)S(1)}, f32[65,1,128]{2,1,0:T(1,128)S(1)}, u32[]{:S(2)}, u32[]{:S(2)}) %collective-permute-start.11) | collective-permute-done | bytes 33312 | tf_op jit(solution)/shard_map/ppermute | solution.py:210
  31.5 1.3 %collective-permute-start.13 = (f32[65,1,128]{2,1,0:T(1,128)S(1)}, f32[65,1,128]{2,1,0:T(1,128)S(1)}, u32[]{:S(2)}, u32[]{:S(2)}) collective-permute-start(f32[65,1,128]{2,1,0:T(1,128)S(1)} %add.18), channel_id=1, source_target_pairs={{0,2},{2,0},{4,6},{6,4},{8,10},{10,8},{12,14},{14,12},{16,18},{18,... | collective-permute-start | bytes 99848 | tf_op jit(solution)/shard_map/ppermute | solution.py:230
  32.8 2.0 %collective-permute-start.12 = (f32[65,1,128]{2,1,0:T(1,128)S(1)}, f32[65,1,128]{2,1,0:T(1,128)S(1)}, u32[]{:S(2)}, u32[]{:S(2)}) collective-permute-start(f32[65,1,128]{2,1,0:T(1,128)S(1)} %add.18), channel_id=1, source_target_pairs={{0,4},{2,6},{4,0},{6,2},{8,12},{10,14},{12,8},{14,10},{16,20},{18,... | collective-permute-start | bytes 99848 | tf_op jit(solution)/shard_map/ppermute | solution.py:230
  34.8 1.3 %collective-permute-done.14 = f32[65,1,128]{2,1,0:T(1,128)S(1)} collective-permute-done((f32[65,1,128]{2,1,0:T(1,128)S(1)}, f32[65,1,128]{2,1,0:T(1,128)S(1)}, u32[]{:S(2)}, u32[]{:S(2)}) %collective-permute-start.14) | collective-permute-done | bytes 33312 | tf_op jit(solution)/shard_map/ppermute | solution.py:230
  36.7 3.1 %collective-permute-start.15 = (f32[65,1,128]{2,1,0:T(1,128)S(1)}, f32[65,1,128]{2,1,0:T(1,128)S(1)}, u32[]{:S(2)}, u32[]{:S(2)}) collective-permute-start(f32[65,1,128]{2,1,0:T(1,128)S(1)} %add_add_fusion), channel_id=1, source_target_pairs={{0,24},{4,28},{8,16},{12,20},{16,8},{20,12},{24,0},{28,4},{1,25},{... | collective-permute-start | bytes 99848 | tf_op jit(solution)/shard_map/ppermute | solution.py:222
  39.9 1.3 %collective-permute-start.16 = (f32[65,1,128]{2,1,0:T(1,128)S(1)}, f32[65,1,128]{2,1,0:T(1,128)S(1)}, u32[]{:S(2)}, u32[]{:S(2)}) collective-permute-start(f32[65,1,128]{2,1,0:T(1,128)S(1)} %add_add_fusion), channel_id=1, source_target_pairs={{0,16},{4,20},{8,24},{12,28},{16,0},{20,4},{24,8},{28,12},{1,17},{... | collective-permute-start | bytes 99848 | tf_op jit(solution)/shard_map/ppermute | solution.py:222
  41.2 0.7 %copy.11 = f32[256,128]{1,0:T(8,128)} copy(f32[256,128]{1,0:T(8,128)S(1)} %get-tuple-element.49) | data formatting | bytes 262144
  41.8 0.7 %collective-permute-done.15 = f32[65,1,128]{2,1,0:T(1,128)S(1)} collective-permute-done((f32[65,1,128]{2,1,0:T(1,128)S(1)}, f32[65,1,128]{2,1,0:T(1,128)S(1)}, u32[]{:S(2)}, u32[]{:S(2)}) %collective-permute-start.15) | collective-permute-done | bytes 33312 | tf_op jit(solution)/shard_map/ppermute | solution.py:222
  42.6 1.2 %collective-permute-done.17 = f32[65,1,128]{2,1,0:T(1,128)S(1)} collective-permute-done((f32[65,1,128]{2,1,0:T(1,128)S(1)}, f32[65,1,128]{2,1,0:T(1,128)S(1)}, u32[]{:S(2)}, u32[]{:S(2)}) %collective-permute-start.17) | collective-permute-done | bytes 33312 | tf_op jit(solution)/shard_map/ppermute | solution.py:222
  43.8 0.9 %collective-permute-done.16 = f32[65,1,128]{2,1,0:T(1,128)S(1)} collective-permute-done((f32[65,1,128]{2,1,0:T(1,128)S(1)}, f32[65,1,128]{2,1,0:T(1,128)S(1)}, u32[]{:S(2)}, u32[]{:S(2)}) %collective-permute-start.16) | collective-permute-done | bytes 33312 | tf_op jit(solution)/shard_map/ppermute | solution.py:222
  (30 shorter events, 4.1 us)
Async XLA Ops:
  0.6 9.3 %collective-permute-start.1 = (f32[64,512]{1,0:T(8,128)}, f32[64,512]{1,0:T(8,128)S(1)}, u32[]{:S(2)}, u32[]{:S(2)}) collective-permute-start(f32[64,512]{1,0:T(8,128)} %refs_0_.1), channel_id=1, source_target_pairs={{0,4},{4,0},{8,12},{12,8},{16,20},{20,16},{24,28},{28,24},{1,5},{5... | collective-permute-start | bytes 393224 | tf_op jit(solution)/shard_map/ppermute | solution.py:222
  3.6 8.4 %collective-permute-start = (f32[64,512]{1,0:T(8,128)}, f32[64,512]{1,0:T(8,128)S(1)}, u32[]{:S(2)}, u32[]{:S(2)}) collective-permute-start(f32[64,512]{1,0:T(8,128)} %refs_0_.1), channel_id=1, source_target_pairs={{0,24},{4,28},{8,16},{12,20},{16,8},{20,12},{24,0},{28,4},{1,25},{... | collective-permute-start | bytes 393224 | tf_op jit(solution)/shard_map/ppermute | solution.py:222
  7.2 6.6 %collective-permute-start.3 = (f32[64,512]{1,0:T(8,128)}, f32[64,512]{1,0:T(8,128)S(1)}, u32[]{:S(2)}, u32[]{:S(2)}) collective-permute-start(f32[64,512]{1,0:T(8,128)} %refs_0_.1), channel_id=1, source_target_pairs={{0,12},{4,8},{8,4},{12,0},{16,28},{20,24},{24,20},{28,16},{1,13},{... | collective-permute-start | bytes 393224 | tf_op jit(solution)/shard_map/ppermute | solution.py:222
  7.2 2.7 %collective-permute-start.2 = (f32[64,128]{1,0:T(8,128)}, f32[64,128]{1,0:T(8,128)S(1)}, u32[]{:S(2)}, u32[]{:S(2)}) collective-permute-start(f32[64,128]{1,0:T(8,128)} %refs_4_), channel_id=1, source_target_pairs={{0,1},{1,0},{2,3},{3,2},{4,5},{5,4},{6,7},{7,6},{8,9},{9,8},{10,11... | collective-permute-start | bytes 98312 | tf_op jit(solution)/shard_map/ppermute | solution.py:210
  7.2 6.6 %copy-start.1 = (f32[64,512]{1,0:T(8,128)S(1)}, f32[64,512]{1,0:T(8,128)}, u32[]{:S(2)}) copy-start(f32[64,512]{1,0:T(8,128)} %refs_0_.1) | copy-start | bytes 393220
  12.1 6.3 %collective-permute-start.5 = (f32[64,512]{1,0:T(8,128)S(1)}, f32[64,512]{1,0:T(8,128)S(1)}, u32[]{:S(2)}, u32[]{:S(2)}) collective-permute-start(f32[64,512]{1,0:T(8,128)S(1)} %collective-permute-done.refs_1_), channel_id=1, source_target_pairs={{0,8},{4,12},{8,0},{12,4},{16,24},{20,28},{24,16},{28,20},{1,9},{5... | collective-permute-start | bytes 393224 | tf_op jit(solution)/shard_map/ppermute | solution.py:222
  13.8 6.0 %collective-permute-start.4 = (f32[64,512]{1,0:T(8,128)S(1)}, f32[64,512]{1,0:T(8,128)S(1)}, u32[]{:S(2)}, u32[]{:S(2)}) collective-permute-start(f32[64,512]{1,0:T(8,128)S(1)} %copy-done.1), channel_id=1, source_target_pairs={{0,8},{4,12},{8,0},{12,4},{16,24},{20,28},{24,16},{28,20},{1,9},{5... | collective-permute-start | bytes 393224 | tf_op jit(solution)/shard_map/ppermute | solution.py:222
  15.2 5.2 %collective-permute-start.6 = (f32[64,512]{1,0:T(8,128)S(1)}, f32[64,512]{1,0:T(8,128)S(1)}, u32[]{:S(2)}, u32[]{:S(2)}) collective-permute-start(f32[64,512]{1,0:T(8,128)S(1)} %collective-permute-done.refs_1_), channel_id=1, source_target_pairs={{0,4},{4,0},{8,12},{12,8},{16,20},{20,16},{24,28},{28,24},{1,5},{5... | collective-permute-start | bytes 393224 | tf_op jit(solution)/shard_map/ppermute | solution.py:222
  18.4 5.0 %collective-permute-start.7 = (f32[64,512]{1,0:T(8,128)S(1)}, f32[64,512]{1,0:T(8,128)S(1)}, u32[]{:S(2)}, u32[]{:S(2)}) collective-permute-start(f32[64,512]{1,0:T(8,128)S(1)} %collective-permute-done.5.refs_3_), channel_id=1, source_target_pairs={{0,4},{4,0},{8,12},{12,8},{16,20},{20,16},{24,28},{28,24},{1,5},{5... | collective-permute-start | bytes 393224 | tf_op jit(solution)/shard_map/ppermute | solution.py:222
  23.3 6.0 %copy-start = (f32[256,128]{1,0:T(8,128)S(1)}, f32[256,128]{1,0:T(8,128)}, u32[]{:S(2)}) copy-start(f32[256,128]{1,0:T(8,128)} %refs_7_.1) | copy-start | bytes 393220
  23.4 6.0 %copy-start.2 = (f32[64,128]{1,0:T(8,128)S(1)}, f32[64,128]{1,0:T(8,128)}, u32[]{:S(2)}) copy-start(f32[64,128]{1,0:T(8,128)} %refs_4_) | copy-start | bytes 98308
  23.4 6.0 %copy-start.3 = (f32[128]{0:T(128)S(1)}, f32[128]{0:T(128)}, u32[]{:S(2)}) copy-start(f32[128]{0:T(128)} %param.14) | copy-start | bytes 1540
  23.5 4.4 %collective-permute-start.8 = (f32[64,256]{1,0:T(8,128)S(1)}, f32[64,256]{1,0:T(8,128)S(1)}, u32[]{:S(2)}, u32[]{:S(2)}) collective-permute-start(f32[64,256]{1,0:T(8,128)S(1)} %get-tuple-element.38), channel_id=1, source_target_pairs={{0,3},{1,2},{2,1},{3,0},{4,7},{5,6},{6,5},{7,4},{8,11},{9,10},{10,... | collective-permute-start | bytes 196616 | tf_op jit(solution)/shard_map/ppermute | solution.py:218
  23.5 5.8 %collective-permute-start.9 = (f32[64,256]{1,0:T(8,128)S(1)}, f32[64,256]{1,0:T(8,128)S(1)}, u32[]{:S(2)}, u32[]{:S(2)}) collective-permute-start(f32[64,256]{1,0:T(8,128)S(1)} %get-tuple-element.39), channel_id=1, source_target_pairs={{0,2},{1,3},{2,0},{3,1},{4,6},{5,7},{6,4},{7,5},{8,10},{9,11},{10,... | collective-permute-start | bytes 196616 | tf_op jit(solution)/shard_map/ppermute | solution.py:218
  25.1 4.3 %collective-permute-start.10 = (f32[64,256]{1,0:T(8,128)S(1)}, f32[64,256]{1,0:T(8,128)S(1)}, u32[]{:S(2)}, u32[]{:S(2)}) collective-permute-start(f32[64,256]{1,0:T(8,128)S(1)} %get-tuple-element.40), channel_id=1, source_target_pairs={{0,1},{1,0},{2,3},{3,2},{4,5},{5,4},{6,7},{7,6},{8,9},{9,8},{10,11... | collective-permute-start | bytes 196616 | tf_op jit(solution)/shard_map/ppermute | solution.py:218
  29.9 1.3 %collective-permute-start.11 = (f32[65,1,128]{2,1,0:T(1,128)S(1)}, f32[65,1,128]{2,1,0:T(1,128)S(1)}, u32[]{:S(2)}, u32[]{:S(2)}) collective-permute-start(f32[65,1,128]{2,1,0:T(1,128)S(1)} %get-tuple-element.46), channel_id=1, source_target_pairs={{0,1},{1,0},{2,3},{3,2},{4,5},{5,4},{6,7},{7,6},{8,9},{9,8},{10,11... | collective-permute-start | bytes 99848 | tf_op jit(solution)/shard_map/ppermute | solution.py:210
  31.2 4.9 %collective-permute-start.14 = (f32[65,1,128]{2,1,0:T(1,128)S(1)}, f32[65,1,128]{2,1,0:T(1,128)S(1)}, u32[]{:S(2)}, u32[]{:S(2)}) collective-permute-start(f32[65,1,128]{2,1,0:T(1,128)S(1)} %add.18), channel_id=1, source_target_pairs={{0,6},{2,4},{4,2},{6,0},{8,14},{10,12},{12,10},{14,8},{16,22},{18,... | collective-permute-start | bytes 99848 | tf_op jit(solution)/shard_map/ppermute | solution.py:230
  31.5 4.6 %collective-permute-start.13 = (f32[65,1,128]{2,1,0:T(1,128)S(1)}, f32[65,1,128]{2,1,0:T(1,128)S(1)}, u32[]{:S(2)}, u32[]{:S(2)}) collective-permute-start(f32[65,1,128]{2,1,0:T(1,128)S(1)} %add.18), channel_id=1, source_target_pairs={{0,2},{2,0},{4,6},{6,4},{8,10},{10,8},{12,14},{14,12},{16,18},{18,... | collective-permute-start | bytes 99848 | tf_op jit(solution)/shard_map/ppermute | solution.py:230
  32.8 3.9 %collective-permute-start.12 = (f32[65,1,128]{2,1,0:T(1,128)S(1)}, f32[65,1,128]{2,1,0:T(1,128)S(1)}, u32[]{:S(2)}, u32[]{:S(2)}) collective-permute-start(f32[65,1,128]{2,1,0:T(1,128)S(1)} %add.18), channel_id=1, source_target_pairs={{0,4},{2,6},{4,0},{6,2},{8,12},{10,14},{12,8},{14,10},{16,20},{18,... | collective-permute-start | bytes 99848 | tf_op jit(solution)/shard_map/ppermute | solution.py:230
  36.7 5.8 %collective-permute-start.15 = (f32[65,1,128]{2,1,0:T(1,128)S(1)}, f32[65,1,128]{2,1,0:T(1,128)S(1)}, u32[]{:S(2)}, u32[]{:S(2)}) collective-permute-start(f32[65,1,128]{2,1,0:T(1,128)S(1)} %add_add_fusion), channel_id=1, source_target_pairs={{0,24},{4,28},{8,16},{12,20},{16,8},{20,12},{24,0},{28,4},{1,25},{... | collective-permute-start | bytes 99848 | tf_op jit(solution)/shard_map/ppermute | solution.py:222
  39.8 3.9 %collective-permute-start.17 = (f32[65,1,128]{2,1,0:T(1,128)S(1)}, f32[65,1,128]{2,1,0:T(1,128)S(1)}, u32[]{:S(2)}, u32[]{:S(2)}) collective-permute-start(f32[65,1,128]{2,1,0:T(1,128)S(1)} %add_add_fusion), channel_id=1, source_target_pairs={{0,8},{4,12},{8,0},{12,4},{16,24},{20,28},{24,16},{28,20},{1,9},{5... | collective-permute-start | bytes 99848 | tf_op jit(solution)/shard_map/ppermute | solution.py:222
  39.9 4.8 %collective-permute-start.16 = (f32[65,1,128]{2,1,0:T(1,128)S(1)}, f32[65,1,128]{2,1,0:T(1,128)S(1)}, u32[]{:S(2)}, u32[]{:S(2)}) collective-permute-start(f32[65,1,128]{2,1,0:T(1,128)S(1)} %add_add_fusion), channel_id=1, source_target_pairs={{0,16},{4,20},{8,24},{12,28},{16,0},{20,4},{24,8},{28,12},{1,17},{... | collective-permute-start | bytes 99848 | tf_op jit(solution)/shard_map/ppermute | solution.py:222

commit v9 on v7

--- a/solution.py
+++ b/solution.py
@@ -91,11 +91,25 @@
     picked[t, :half_width], picked[t, half_width:] = split(piece[...])
 
 
-def early_kernel(bases, counts, plan, high, low, *refs):
+def live_kernel(slots, bases, counts, plan, out):
+    which = digits(plan[0][0, 0], bases[0], slots)
+    code = 0
+    for t in range(slots):
+        code = code * bases[0] + jnp.where(t < counts[0, 0], which[t], 0)
+    out[0] = jnp.full(out.shape[1:], code, jnp.int32)
+    out[1] = plan[1]
+
+
+def live_plan(plan, counts, slots, bases):
+    out = pltpu.VMEM(plan.shape, jnp.int32)
+    return call(functools.partial(live_kernel, slots, bases), out, [pltpu.SMEM, pltpu.VMEM], "live_plan")(counts, plan)
+
+
+def early_kernel(bases, plan, high, low, *refs):
     pieces, (total, rest, picked, which) = refs[:-4], refs[-4:]
     slots = high.shape[0]
     place = digits(plan[1][0, 0], bases[1], slots)
-    found = [jnp.where(t < counts[0, 0], d, 0) for t, d in enumerate(digits(plan[0][0, 0], bases[0], slots))]
+    found = digits(plan[0][0, 0], bases[0], slots)
     left = 0
     for t in range(slots):
         which[t] = found[t]
@@ -139,7 +153,7 @@
         out[...] = total[lax.rem(col + k, groups), :, pl.ds(begin, part)]
 
 
-def mix(sizes, slabs, counts, plan, pieces):
+def mix(sizes, slabs, plan, pieces):
     groups, halves = sizes
     slots = slabs[0].shape[0]
     half_width, block_len = pieces[0].shape
@@ -148,11 +162,11 @@
     total, rest = call(
         functools.partial(early_kernel, bases),
         [pltpu.VMEM((groups, half_width, block_len), F32), pltpu.VMEM((SUBLANES, LANES), jnp.int32)],
-        [pltpu.SMEM] + [pltpu.VMEM] * (2 + len(pieces)),
+        [pltpu.VMEM] * (2 + len(pieces)),
         "mix_early",
         [picked, pltpu.SMEM((slots,), jnp.int32)],
         pl.CostEstimate(flops=6 * slabs[0].size * half_width, bytes_accessed=4 * slabs[0].size, transcendentals=0),
-    )(counts, plan, *slabs, *pieces[:-1])
+    )(plan, *slabs, *pieces[:-1])
     return call(
         functools.partial(late_kernel, sizes),
         [pltpu.VMEM((half_width, block_len // halves), F32)] * (groups * halves),
@@ -319,8 +333,10 @@
 def local(row_size, groups, halves, adj_tiles, tile_rows, tile_cols, tile_counts, features_t, weight, bias_vec, cotangent):
     weights = [weight] + [shift(weight, "rep", halves, k) for k in range(1, halves)]
     *slabs, plan = split_slabs(adj_tiles[0, 0], tile_rows, tile_cols, piece_sources(row_size), groups)
+    slots = tile_cols.shape[2]
+    plan = live_plan(plan, tile_counts, slots, (row_size + 1, groups))
     pieces, (slabs, plan, weights) = gather_row(features_t, row_size, (slabs, plan, weights))
-    parts = mix((groups, halves), slabs, tile_counts, plan, pieces)
+    parts = mix((groups, halves), slabs, plan, pieces)
 
     terms = [None] * len(parts)
     for i in sorted(range(len(parts)), key=lambda i: -i):

time: 45.2 us -> 45.1 us (level)
  waiting for transfers between devices: 17.4 us -> 16.8 us
    ppermute x10, waiting for transfers between devices: 10.4 us -> 8.64 us  [swap(): return lax.ppermute(x, axis, [(i, i ^ bit) for i in range(size)])]
    ppermute x3, waiting for transfers between devices: 1.93 us -> 3.08 us  [swap_two(): return lax.ppermute(x, axes, perm)]
  transfers between devices with their start and end apart: 18 -> 18, of which waited for: 14 -> 15; matrix products, arithmetic and copies ran while one was open for 1% -> 1% of each run, Pallas kernels for 8% -> 8%
where the time goes in v9:
time: 45.1 us; the launch traced here: 44.9 us
  starting transfers between devices  21 us (47%)
  waiting for transfers between devices  16.8 us (37%)
  Pallas kernels  5.05 us (11%)
  between operations  1.39 us (3%)
  local copies, waits for them, and re-layouts  0.67 us (1%)
    ppermute x10, starting transfers between devices, swap(): return lax.ppermute(x, axis, [(i, i ^ bit) for i in range(size)])  15.5 us
    ppermute x10, waiting for transfers between devices, swap(): return lax.ppermute(x, axis, [(i, i ^ bit) for i in range(size)])  8.64 us
    ppermute x3, waiting for transfers between devices, shift_two(): return lax.ppermute(x, ('col', 'rep'), perm)  3.94 us
    ppermute x3, starting transfers between devices, swap_two(): return lax.ppermute(x, axes, perm)  3.49 us
    ppermute x3, waiting for transfers between devices, swap_two(): return lax.ppermute(x, axes, perm)  3.08 us
    pallas_call x1, Pallas kernels, split_slabs(): call(kernel, outs, [pl.ANY] * len(operands), 'split_slabs', scratch, cost)  2.68 us
    ppermute x3, starting transfers between devices, shift_two(): return lax.ppermute(x, ('col', 'rep'), perm)  1.92 us
    ppermute x2, waiting for transfers between devices, shift(): return lax.ppermute(x, axis, [(i, (i + k) % size) for i in range(size)])  1.11 us
  transfers between devices with their start and end apart: 18, of which 15 were waited for; matrix products, arithmetic and copies ran while one was open for 1% of the time, Pallas kernels for 8%

profile of v9, /device:TPU:0, one launch (start us, length us, event | category | flops | bytes accessed | tf_op | source)
XLA Modules:
  0.0 44.9 jit_solution(10837483751040708002)
XLA Ops:
  0.6 3.0 %collective-permute-start.1 = (f32[64,512]{1,0:T(8,128)}, f32[64,512]{1,0:T(8,128)S(1)}, u32[]{:S(2)}, u32[]{:S(2)}) collective-permute-start(f32[64,512]{1,0:T(8,128)} %refs_0_.1), channel_id=1, source_target_pairs={{0,4},{4,0},{8,12},{12,8},{16,20},{20,16},{24,28},{28,24},{1,5},{5... | collective-permute-start | bytes 393224 | tf_op jit(solution)/shard_map/ppermute | solution.py:234
  3.6 3.6 %collective-permute-start = (f32[64,512]{1,0:T(8,128)}, f32[64,512]{1,0:T(8,128)S(1)}, u32[]{:S(2)}, u32[]{:S(2)}) collective-permute-start(f32[64,512]{1,0:T(8,128)} %refs_0_.1), channel_id=1, source_target_pairs={{0,24},{4,28},{8,16},{12,20},{16,8},{20,12},{24,0},{28,4},{1,25},{... | collective-permute-start | bytes 393224 | tf_op jit(solution)/shard_map/ppermute | solution.py:234
  7.9 2.7 %split_slabs.1 = (bf16[4,512,512]{2,1,0:T(8,128)(2,1)S(1)}, bf16[4,512,512]{2,1,0:T(8,128)(2,1)S(1)}, s32[2,8,128]{2,1,0:T(8,128)S(1)}) custom-call(f32[4,512,512]{2,1,0:T(8,128)} %bitcast.3, s32[1,1,4]{2,1,0:T(1,128)} %rows.1, s32[1,1,4]{2,1,0:T(1,128)} %cols.1), custom_call_target="tpu_custom_call" | custom-call | flops 4194304 | bytes 8388608 | tf_op jit(solution)/shard_map/split_slabs/pallas_call | solution.py:76
  10.7 1.4 %collective-permute-done.refs_1_ = f32[64,512]{1,0:T(8,128)S(1)} collective-permute-done((f32[64,512]{1,0:T(8,128)}, f32[64,512]{1,0:T(8,128)S(1)}, u32[]{:S(2)}, u32[]{:S(2)}) %collective-permute-start) | collective-permute-done | bytes 131104 | tf_op jit(solution)/shard_map/ppermute | solution.py:234
  12.1 1.1 %collective-permute-start.5 = (f32[64,512]{1,0:T(8,128)S(1)}, f32[64,512]{1,0:T(8,128)S(1)}, u32[]{:S(2)}, u32[]{:S(2)}) collective-permute-start(f32[64,512]{1,0:T(8,128)S(1)} %collective-permute-done.refs_1_), channel_id=1, source_target_pairs={{0,8},{4,12},{8,0},{12,4},{16,24},{20,28},{24,16},{28,20},{1,9},{5... | collective-permute-start | bytes 393224 | tf_op jit(solution)/shard_map/ppermute | solution.py:234
  13.8 1.4 %collective-permute-start.4 = (f32[64,512]{1,0:T(8,128)S(1)}, f32[64,512]{1,0:T(8,128)S(1)}, u32[]{:S(2)}, u32[]{:S(2)}) collective-permute-start(f32[64,512]{1,0:T(8,128)S(1)} %copy-done), channel_id=1, source_target_pairs={{0,8},{4,12},{8,0},{12,4},{16,24},{20,28},{24,16},{28,20},{1,9},{5... | collective-permute-start | bytes 393224 | tf_op jit(solution)/shard_map/ppermute | solution.py:234
  15.2 1.5 %collective-permute-start.6 = (f32[64,512]{1,0:T(8,128)S(1)}, f32[64,512]{1,0:T(8,128)S(1)}, u32[]{:S(2)}, u32[]{:S(2)}) collective-permute-start(f32[64,512]{1,0:T(8,128)S(1)} %collective-permute-done.refs_1_), channel_id=1, source_target_pairs={{0,4},{4,0},{8,12},{12,8},{16,20},{20,16},{24,28},{28,24},{1,5},{5... | collective-permute-start | bytes 393224 | tf_op jit(solution)/shard_map/ppermute | solution.py:234
  16.7 1.7 %collective-permute-done.5.refs_3_ = f32[64,512]{1,0:T(8,128)S(1)} collective-permute-done((f32[64,512]{1,0:T(8,128)S(1)}, f32[64,512]{1,0:T(8,128)S(1)}, u32[]{:S(2)}, u32[]{:S(2)}) %collective-permute-start.5) | collective-permute-done | bytes 131104 | tf_op jit(solution)/shard_map/ppermute | solution.py:234
  18.8 1.0 %collective-permute-done.4.refs_2_ = f32[64,512]{1,0:T(8,128)S(1)} collective-permute-done((f32[64,512]{1,0:T(8,128)S(1)}, f32[64,512]{1,0:T(8,128)S(1)}, u32[]{:S(2)}, u32[]{:S(2)}) %collective-permute-start.4) | collective-permute-done | bytes 131104 | tf_op jit(solution)/shard_map/ppermute | solution.py:234
  19.8 1.6 %collective-permute-done.6.refs_5_ = f32[64,512]{1,0:T(8,128)S(1)} collective-permute-done((f32[64,512]{1,0:T(8,128)S(1)}, f32[64,512]{1,0:T(8,128)S(1)}, u32[]{:S(2)}, u32[]{:S(2)}) %collective-permute-start.6) | collective-permute-done | bytes 131104 | tf_op jit(solution)/shard_map/ppermute | solution.py:234
  21.4 1.1 %mix_early.1 = (f32[2,64,512]{2,1,0:T(8,128)S(1)}, s32[8,128]{1,0:T(8,128)S(1)}) custom-call(s32[2,8,128]{2,1,0:T(8,128)S(1)} %live_plan.1.plan, bf16[4,512,512]{2,1,0:T(8,128)(2,1)S(1)} %get-tuple-element.30.high, bf16[4,512,512]{2,1,0:T(8,128)(2,1)S(1)} %get-tuple-element.31.low, f32[64,512]{1,0:T(8,128)S(1)} %copy-done, ...), custom_call_target="tpu_custom_call" | custom-call | flops 402653184 | bytes 4194304 | tf_op jit(solution)/shard_map/mix_early/pallas_call | solution.py:162
  22.4 0.9 %collective-permute-done.7.piece = f32[64,512]{1,0:T(8,128)S(1)} collective-permute-done((f32[64,512]{1,0:T(8,128)S(1)}, f32[64,512]{1,0:T(8,128)S(1)}, u32[]{:S(2)}, u32[]{:S(2)}) %collective-permute-start.7) | collective-permute-done | bytes 131104 | tf_op jit(solution)/shard_map/ppermute | solution.py:234
  23.5 1.5 %collective-permute-start.9 = (f32[64,256]{1,0:T(8,128)S(1)}, f32[64,256]{1,0:T(8,128)S(1)}, u32[]{:S(2)}, u32[]{:S(2)}) collective-permute-start(f32[64,256]{1,0:T(8,128)S(1)} %get-tuple-element.39), channel_id=1, source_target_pairs={{0,2},{1,3},{2,0},{3,1},{4,6},{5,7},{6,4},{7,5},{8,10},{9,11},{10,... | collective-permute-start | bytes 196616 | tf_op jit(solution)/shard_map/ppermute | solution.py:230
  25.4 2.5 %collective-permute-done.8.refs_0_ = f32[64,256]{1,0:T(8,128)S(1)} collective-permute-done((f32[64,256]{1,0:T(8,128)S(1)}, f32[64,256]{1,0:T(8,128)S(1)}, u32[]{:S(2)}, u32[]{:S(2)}) %collective-permute-start.8) | collective-permute-done | bytes 65568 | tf_op jit(solution)/shard_map/ppermute | solution.py:230
  27.9 1.4 %collective-permute-done.9.refs_1_ = f32[64,256]{1,0:T(8,128)S(1)} collective-permute-done((f32[64,256]{1,0:T(8,128)S(1)}, f32[64,256]{1,0:T(8,128)S(1)}, u32[]{:S(2)}, u32[]{:S(2)}) %collective-permute-start.9) | collective-permute-done | bytes 65568 | tf_op jit(solution)/shard_map/ppermute | solution.py:230
  30.1 1.1 %collective-permute-done.11 = f32[72,128]{1,0:T(8,128)S(1)} collective-permute-done((f32[72,128]{1,0:T(8,128)S(1)}, f32[72,128]{1,0:T(8,128)S(1)}, u32[]{:S(2)}, u32[]{:S(2)}) %collective-permute-start.11) | collective-permute-done | bytes 36896 | tf_op jit(solution)/shard_map/ppermute | solution.py:222
  31.2 1.3 %collective-permute-start.14 = (f32[72,128]{1,0:T(8,128)S(1)}, f32[72,128]{1,0:T(8,128)S(1)}, u32[]{:S(2)}, u32[]{:S(2)}) collective-permute-start(f32[72,128]{1,0:T(8,128)S(1)} %add.18), channel_id=1, source_target_pairs={{0,6},{2,4},{4,2},{6,0},{8,14},{10,12},{12,10},{14,8},{16,22},{18,... | collective-permute-start | bytes 110600 | tf_op jit(solution)/shard_map/ppermute | solution.py:242
  32.5 1.3 %collective-permute-start.13 = (f32[72,128]{1,0:T(8,128)S(1)}, f32[72,128]{1,0:T(8,128)S(1)}, u32[]{:S(2)}, u32[]{:S(2)}) collective-permute-start(f32[72,128]{1,0:T(8,128)S(1)} %add.18), channel_id=1, source_target_pairs={{0,2},{2,0},{4,6},{6,4},{8,10},{10,8},{12,14},{14,12},{16,18},{18,... | collective-permute-start | bytes 110600 | tf_op jit(solution)/shard_map/ppermute | solution.py:242
  33.8 0.9 %collective-permute-start.12 = (f32[72,128]{1,0:T(8,128)S(1)}, f32[72,128]{1,0:T(8,128)S(1)}, u32[]{:S(2)}, u32[]{:S(2)}) collective-permute-start(f32[72,128]{1,0:T(8,128)S(1)} %add.18), channel_id=1, source_target_pairs={{0,4},{2,6},{4,0},{6,2},{8,12},{10,14},{12,8},{14,10},{16,20},{18,... | collective-permute-start | bytes 110600 | tf_op jit(solution)/shard_map/ppermute | solution.py:242
  34.7 1.4 %collective-permute-done.14 = f32[72,128]{1,0:T(8,128)S(1)} collective-permute-done((f32[72,128]{1,0:T(8,128)S(1)}, f32[72,128]{1,0:T(8,128)S(1)}, u32[]{:S(2)}, u32[]{:S(2)}) %collective-permute-start.14) | collective-permute-done | bytes 36896 | tf_op jit(solution)/shard_map/ppermute | solution.py:242
  36.4 1.3 %collective-permute-done.12 = f32[72,128]{1,0:T(8,128)S(1)} collective-permute-done((f32[72,128]{1,0:T(8,128)S(1)}, f32[72,128]{1,0:T(8,128)S(1)}, u32[]{:S(2)}, u32[]{:S(2)}) %collective-permute-start.12) | collective-permute-done | bytes 36896 | tf_op jit(solution)/shard_map/ppermute | solution.py:242
  37.8 1.7 %collective-permute-start.15 = (f32[72,128]{1,0:T(8,128)S(1)}, f32[72,128]{1,0:T(8,128)S(1)}, u32[]{:S(2)}, u32[]{:S(2)}) collective-permute-start(f32[72,128]{1,0:T(8,128)S(1)} %add_add_fusion), channel_id=1, source_target_pairs={{0,24},{4,28},{8,16},{12,20},{16,8},{20,12},{24,0},{28,4},{1,25},{... | collective-permute-start | bytes 110600 | tf_op jit(solution)/shard_map/ppermute | solution.py:234
  39.5 2.8 %collective-permute-start.16 = (f32[72,128]{1,0:T(8,128)S(1)}, f32[72,128]{1,0:T(8,128)S(1)}, u32[]{:S(2)}, u32[]{:S(2)}) collective-permute-start(f32[72,128]{1,0:T(8,128)S(1)} %add_add_fusion), channel_id=1, source_target_pairs={{0,16},{4,20},{8,24},{12,28},{16,0},{20,4},{24,8},{28,12},{1,17},{... | collective-permute-start | bytes 110600 | tf_op jit(solution)/shard_map/ppermute | solution.py:234
  42.9 0.8 %collective-permute-done.15 = f32[72,128]{1,0:T(8,128)S(1)} collective-permute-done((f32[72,128]{1,0:T(8,128)S(1)}, f32[72,128]{1,0:T(8,128)S(1)}, u32[]{:S(2)}, u32[]{:S(2)}) %collective-permute-start.15) | collective-permute-done | bytes 36896 | tf_op jit(solution)/shard_map/ppermute | solution.py:234
  (31 shorter events, 4.6 us)
Async XLA Ops:
  0.6 10.0 %collective-permute-start.1 = (f32[64,512]{1,0:T(8,128)}, f32[64,512]{1,0:T(8,128)S(1)}, u32[]{:S(2)}, u32[]{:S(2)}) collective-permute-start(f32[64,512]{1,0:T(8,128)} %refs_0_.1), channel_id=1, source_target_pairs={{0,4},{4,0},{8,12},{12,8},{16,20},{20,16},{24,28},{28,24},{1,5},{5... | collective-permute-start | bytes 393224 | tf_op jit(solution)/shard_map/ppermute | solution.py:234
  3.6 8.4 %collective-permute-start = (f32[64,512]{1,0:T(8,128)}, f32[64,512]{1,0:T(8,128)S(1)}, u32[]{:S(2)}, u32[]{:S(2)}) collective-permute-start(f32[64,512]{1,0:T(8,128)} %refs_0_.1), channel_id=1, source_target_pairs={{0,24},{4,28},{8,16},{12,20},{16,8},{20,12},{24,0},{28,4},{1,25},{... | collective-permute-start | bytes 393224 | tf_op jit(solution)/shard_map/ppermute | solution.py:234
  7.2 6.6 %collective-permute-start.3 = (f32[64,512]{1,0:T(8,128)}, f32[64,512]{1,0:T(8,128)S(1)}, u32[]{:S(2)}, u32[]{:S(2)}) collective-permute-start(f32[64,512]{1,0:T(8,128)} %refs_0_.1), channel_id=1, source_target_pairs={{0,12},{4,8},{8,4},{12,0},{16,28},{20,24},{24,20},{28,16},{1,13},{... | collective-permute-start | bytes 393224 | tf_op jit(solution)/shard_map/ppermute | solution.py:234
  7.2 3.4 %collective-permute-start.2 = (f32[64,128]{1,0:T(8,128)}, f32[64,128]{1,0:T(8,128)S(1)}, u32[]{:S(2)}, u32[]{:S(2)}) collective-permute-start(f32[64,128]{1,0:T(8,128)} %refs_4_), channel_id=1, source_target_pairs={{0,1},{1,0},{2,3},{3,2},{4,5},{5,4},{6,7},{7,6},{8,9},{9,8},{10,11... | collective-permute-start | bytes 98312 | tf_op jit(solution)/shard_map/ppermute | solution.py:222
  7.9 5.9 %copy-start = (f32[64,512]{1,0:T(8,128)S(1)}, f32[64,512]{1,0:T(8,128)}, u32[]{:S(2)}) copy-start(f32[64,512]{1,0:T(8,128)} %refs_0_.1) | copy-start | bytes 393220
  12.1 6.3 %collective-permute-start.5 = (f32[64,512]{1,0:T(8,128)S(1)}, f32[64,512]{1,0:T(8,128)S(1)}, u32[]{:S(2)}, u32[]{:S(2)}) collective-permute-start(f32[64,512]{1,0:T(8,128)S(1)} %collective-permute-done.refs_1_), channel_id=1, source_target_pairs={{0,8},{4,12},{8,0},{12,4},{16,24},{20,28},{24,16},{28,20},{1,9},{5... | collective-permute-start | bytes 393224 | tf_op jit(solution)/shard_map/ppermute | solution.py:234
  13.8 6.0 %collective-permute-start.4 = (f32[64,512]{1,0:T(8,128)S(1)}, f32[64,512]{1,0:T(8,128)S(1)}, u32[]{:S(2)}, u32[]{:S(2)}) collective-permute-start(f32[64,512]{1,0:T(8,128)S(1)} %copy-done), channel_id=1, source_target_pairs={{0,8},{4,12},{8,0},{12,4},{16,24},{20,28},{24,16},{28,20},{1,9},{5... | collective-permute-start | bytes 393224 | tf_op jit(solution)/shard_map/ppermute | solution.py:234
  15.2 6.1 %collective-permute-start.6 = (f32[64,512]{1,0:T(8,128)S(1)}, f32[64,512]{1,0:T(8,128)S(1)}, u32[]{:S(2)}, u32[]{:S(2)}) collective-permute-start(f32[64,512]{1,0:T(8,128)S(1)} %collective-permute-done.refs_1_), channel_id=1, source_target_pairs={{0,4},{4,0},{8,12},{12,8},{16,20},{20,16},{24,28},{28,24},{1,5},{5... | collective-permute-start | bytes 393224 | tf_op jit(solution)/shard_map/ppermute | solution.py:234
  18.4 5.0 %collective-permute-start.7 = (f32[64,512]{1,0:T(8,128)S(1)}, f32[64,512]{1,0:T(8,128)S(1)}, u32[]{:S(2)}, u32[]{:S(2)}) collective-permute-start(f32[64,512]{1,0:T(8,128)S(1)} %collective-permute-done.5.refs_3_), channel_id=1, source_target_pairs={{0,4},{4,0},{8,12},{12,8},{16,20},{20,16},{24,28},{28,24},{1,5},{5... | collective-permute-start | bytes 393224 | tf_op jit(solution)/shard_map/ppermute | solution.py:234
  23.4 6.0 %copy-start.1 = (f32[256,128]{1,0:T(8,128)S(1)}, f32[256,128]{1,0:T(8,128)}, u32[]{:S(2)}) copy-start(f32[256,128]{1,0:T(8,128)} %refs_7_.1) | copy-start | bytes 393220
  23.4 6.0 %copy-start.2 = (f32[64,128]{1,0:T(8,128)S(1)}, f32[64,128]{1,0:T(8,128)}, u32[]{:S(2)}) copy-start(f32[64,128]{1,0:T(8,128)} %refs_4_) | copy-start | bytes 98308
  23.4 6.0 %copy-start.3 = (f32[128]{0:T(128)S(1)}, f32[128]{0:T(128)}, u32[]{:S(2)}) copy-start(f32[128]{0:T(128)} %param.14) | copy-start | bytes 1540
  23.5 4.4 %collective-permute-start.8 = (f32[64,256]{1,0:T(8,128)S(1)}, f32[64,256]{1,0:T(8,128)S(1)}, u32[]{:S(2)}, u32[]{:S(2)}) collective-permute-start(f32[64,256]{1,0:T(8,128)S(1)} %get-tuple-element.38), channel_id=1, source_target_pairs={{0,3},{1,2},{2,1},{3,0},{4,7},{5,6},{6,5},{7,4},{8,11},{9,10},{10,... | collective-permute-start | bytes 196616 | tf_op jit(solution)/shard_map/ppermute | solution.py:230
  23.5 5.8 %collective-permute-start.9 = (f32[64,256]{1,0:T(8,128)S(1)}, f32[64,256]{1,0:T(8,128)S(1)}, u32[]{:S(2)}, u32[]{:S(2)}) collective-permute-start(f32[64,256]{1,0:T(8,128)S(1)} %get-tuple-element.39), channel_id=1, source_target_pairs={{0,2},{1,3},{2,0},{3,1},{4,6},{5,7},{6,4},{7,5},{8,10},{9,11},{10,... | collective-permute-start | bytes 196616 | tf_op jit(solution)/shard_map/ppermute | solution.py:230
  25.1 4.3 %collective-permute-start.10 = (f32[64,256]{1,0:T(8,128)S(1)}, f32[64,256]{1,0:T(8,128)S(1)}, u32[]{:S(2)}, u32[]{:S(2)}) collective-permute-start(f32[64,256]{1,0:T(8,128)S(1)} %get-tuple-element.40), channel_id=1, source_target_pairs={{0,1},{1,0},{2,3},{3,2},{4,5},{5,4},{6,7},{7,6},{8,9},{9,8},{10,11... | collective-permute-start | bytes 196616 | tf_op jit(solution)/shard_map/ppermute | solution.py:230
  29.9 1.3 %collective-permute-start.11 = (f32[72,128]{1,0:T(8,128)S(1)}, f32[72,128]{1,0:T(8,128)S(1)}, u32[]{:S(2)}, u32[]{:S(2)}) collective-permute-start(f32[72,128]{1,0:T(8,128)S(1)} %get-tuple-element.46), channel_id=1, source_target_pairs={{0,1},{1,0},{2,3},{3,2},{4,5},{5,4},{6,7},{7,6},{8,9},{9,8},{10,11... | collective-permute-start | bytes 110600 | tf_op jit(solution)/shard_map/ppermute | solution.py:222
  31.2 4.9 %collective-permute-start.14 = (f32[72,128]{1,0:T(8,128)S(1)}, f32[72,128]{1,0:T(8,128)S(1)}, u32[]{:S(2)}, u32[]{:S(2)}) collective-permute-start(f32[72,128]{1,0:T(8,128)S(1)} %add.18), channel_id=1, source_target_pairs={{0,6},{2,4},{4,2},{6,0},{8,14},{10,12},{12,10},{14,8},{16,22},{18,... | collective-permute-start | bytes 110600 | tf_op jit(solution)/shard_map/ppermute | solution.py:242
  32.5 4.0 %collective-permute-start.13 = (f32[72,128]{1,0:T(8,128)S(1)}, f32[72,128]{1,0:T(8,128)S(1)}, u32[]{:S(2)}, u32[]{:S(2)}) collective-permute-start(f32[72,128]{1,0:T(8,128)S(1)} %add.18), channel_id=1, source_target_pairs={{0,2},{2,0},{4,6},{6,4},{8,10},{10,8},{12,14},{14,12},{16,18},{18,... | collective-permute-start | bytes 110600 | tf_op jit(solution)/shard_map/ppermute | solution.py:242
  33.8 4.0 %collective-permute-start.12 = (f32[72,128]{1,0:T(8,128)S(1)}, f32[72,128]{1,0:T(8,128)S(1)}, u32[]{:S(2)}, u32[]{:S(2)}) collective-permute-start(f32[72,128]{1,0:T(8,128)S(1)} %add.18), channel_id=1, source_target_pairs={{0,4},{2,6},{4,0},{6,2},{8,12},{10,14},{12,8},{14,10},{16,20},{18,... | collective-permute-start | bytes 110600 | tf_op jit(solution)/shard_map/ppermute | solution.py:242
  37.8 5.9 %collective-permute-start.15 = (f32[72,128]{1,0:T(8,128)S(1)}, f32[72,128]{1,0:T(8,128)S(1)}, u32[]{:S(2)}, u32[]{:S(2)}) collective-permute-start(f32[72,128]{1,0:T(8,128)S(1)} %add_add_fusion), channel_id=1, source_target_pairs={{0,24},{4,28},{8,16},{12,20},{16,8},{20,12},{24,0},{28,4},{1,25},{... | collective-permute-start | bytes 110600 | tf_op jit(solution)/shard_map/ppermute | solution.py:234
  39.5 4.4 %collective-permute-start.17 = (f32[72,128]{1,0:T(8,128)S(1)}, f32[72,128]{1,0:T(8,128)S(1)}, u32[]{:S(2)}, u32[]{:S(2)}) collective-permute-start(f32[72,128]{1,0:T(8,128)S(1)} %add_add_fusion), channel_id=1, source_target_pairs={{0,8},{4,12},{8,0},{12,4},{16,24},{20,28},{24,16},{28,20},{1,9},{5... | collective-permute-start | bytes 110600 | tf_op jit(solution)/shard_map/ppermute | solution.py:234
  39.5 4.9 %collective-permute-start.16 = (f32[72,128]{1,0:T(8,128)S(1)}, f32[72,128]{1,0:T(8,128)S(1)}, u32[]{:S(2)}, u32[]{:S(2)}) collective-permute-start(f32[72,128]{1,0:T(8,128)S(1)} %add_add_fusion), channel_id=1, source_target_pairs={{0,16},{4,20},{8,24},{12,28},{16,0},{20,4},{24,8},{28,12},{1,17},{... | collective-permute-start | bytes 110600 | tf_op jit(solution)/shard_map/ppermute | solution.py:234
